TPU v7x, 256 devices: a whole 4x4x8 slice. The times are simulated.
256 devices in a mesh: seq: 16 (over x, y_hi, core), dp: 16 (over z, y_lo).
Axes of the slice: x: 4, y: 4 (y_hi: 2, y_lo: 2; y = y_hi * 2 + y_lo), z: 8, core: 2. Of those that a mesh axis runs over, the one named last changes fastest.
Arguments:
- frames: bfloat16 [16, 2048, 1024], P('dp', 'seq'), may hold values from -6 to 6
- lengths: int32 [16], P('dp'), may hold values from 1024 to 2048, as said below
- stretch_sizes: int32 [16], P('dp'), may hold values from 8 to 32, as said below
- look_ahead: int32 [16], P('dp'), may hold values from 1 to 8, as said below
- norm_one: float32 [1024], replicated, may hold values from 0.5 to 1.5
- norm_two: float32 [1024], replicated, may hold values from 0.5 to 1.5
- w_query: bfloat16 [1024, 1024], replicated, may hold values from -8 to 8
- w_key: bfloat16 [1024, 1024], replicated, may hold values from -1 to 1
- w_value: bfloat16 [1024, 1024], replicated, may hold values from -0.1875 to 0.1875
- w_out: bfloat16 [1024, 1024], replicated, may hold values from -0.1875 to 0.1875
- conv_kernel: bfloat16 [31, 1024], replicated, may hold values from -1 to 1
Outputs:
- full_output: bfloat16 [16, 2048, 1024], P('dp', 'seq')
- stretch_output: bfloat16 [16, 2048, 1024], P('dp', 'seq')
- kernel_grad: float32 [31, 1024], replicated
Inputs may be any that keep to these rules, and one draw needn't show every extreme that they name: `lengths`: utterance 0 has all 2048 frames. `stretch_sizes`: utterance 0 has stretch size 32. `look_ahead`: utterance 0 has preview 8.
All inputs are finite; a program needn't handle non-finite values.
Results may differ from a plain program's by a relative error of at most 0.0045.
The roundings to bfloat16 on the way count: a program that leaves them out, or rounds other values in their place, can miss the bound.
Values may be sent and summed in bfloat16 or wider, within the bound.
No kernel may reach another device: no remote copies, remote signals or barrier semaphores. Data moves between devices by JAX's collectives and lax.ppermute only.
A program may use at most 128 MiB of HBM per device.

v0:
```python
import math

import jax
import jax.numpy as jnp
from jax import lax
from jax.sharding import PartitionSpec as P

HEADS = 16
KERNEL = 31
LEFT = 64
HALO = 128


EPSILON = 1e-05
FLOOR_SCORE = -1e30


def with_halo(value, sides, width):
    for axis, dim in sides:
        size, length = (lax.axis_size(axis), value.shape[dim])
        up = [(i, (i + 1) % size) for i in range(size - 1)]
        down = [(j, i) for i, j in up]
        last = lax.slice_in_dim(value, length - width, length, axis=dim)
        leading = lax.slice_in_dim(value, 0, width, axis=dim)
        before = lax.ppermute(last, axis, up)
        after = lax.ppermute(leading, axis, down)
        value = jnp.concatenate([before, value, after], axis=dim)
    return value


def shifted(value, axis, by):
    length = lax.axis_size(axis)
    pairs = [(i, i + by) for i in range(length) if 0 <= i + by < length]
    return lax.ppermute(value, axis, pairs)


def layer_norm(values, gain_vector):
    values = values.astype(jnp.float32)
    center = values - jnp.mean(values, axis=-1, keepdims=True)
    spread = jnp.mean(center * center, axis=-1, keepdims=True)
    return center * lax.rsqrt(spread + EPSILON) * gain_vector


def fresh_state(row_count, head_count, depth_count):
    return (
        jnp.full((head_count, row_count), FLOOR_SCORE, jnp.float32),
        jnp.zeros((head_count, row_count), jnp.float32),
        jnp.zeros((row_count, head_count * depth_count), jnp.float32),
    )


def finish_state(state):
    highest, totals, summed = state
    row_count = summed.shape[0]
    head_count = totals.shape[0]
    mixed = summed.reshape(row_count, head_count, -1) / totals.T[:, :, None]
    return mixed.reshape(row_count, -1).astype(jnp.bfloat16)


def fold_keys(state, query3, query_pos, key3, value3, key_start, length, scale):
    highest, totals, summed = state
    key_count = key3.shape[0]
    scores = jnp.einsum("qhe,khe->hqk", query3, key3, preferred_element_type=jnp.float32) * scale
    key_pos = key_start + jnp.arange(key_count, dtype=jnp.int32)
    visible = (key_pos[None, :] < length) | (key_pos[None, :] == query_pos[:, None])
    scores = jnp.where(visible[None], scores, FLOOR_SCORE)
    new_high = jnp.maximum(highest, jnp.max(scores, axis=-1))
    factor = jnp.exp(highest - new_high)
    expo = jnp.where(visible[None], jnp.exp(scores - new_high[:, :, None]), 0.0)
    totals = totals * factor + jnp.sum(expo, axis=-1)
    adding = jnp.einsum(
        "hqk,khe->qhe", expo.astype(jnp.bfloat16), value3, preferred_element_type=jnp.float32
    )
    row_count, head_count, depth_count = adding.shape
    summed = summed.reshape(row_count, head_count, depth_count) * factor.T[:, :, None] + adding
    return (new_high, totals, summed.reshape(row_count, head_count * depth_count))


def fold_blocks(state, query3, query_pos, keys3, values3, length, scale):
    key_count = keys3.shape[0]
    block_width = math.gcd(key_count, 256)
    number = key_count // block_width
    key_blocks = keys3.reshape(number, block_width, keys3.shape[1], keys3.shape[2])
    value_blocks = values3.reshape(number, block_width, values3.shape[1], values3.shape[2])

    def advance(carry, inputs):
        index, key_block, value_block = inputs
        return (
            fold_keys(
                carry, query3, query_pos, key_block, value_block, index * block_width, length, scale
            ),
            None,
        )

    state, _ = lax.scan(
        advance, state, (jnp.arange(number, dtype=jnp.int32), key_blocks, value_blocks)
    )
    return state


def windowed(query3, key_ext3, value_ext3, first_pos, length, stretch, lookup, scale):
    query_count = query3.shape[0]
    block_rows = min(query_count, 512)
    number = query_count // block_rows
    span = block_rows + 2 * HALO

    def one_block(index):
        start = index * block_rows
        query_pos = first_pos + start + jnp.arange(block_rows, dtype=jnp.int32)
        key_pos = first_pos + start - HALO + jnp.arange(span, dtype=jnp.int32)
        begin = query_pos // stretch * stretch
        inside = (key_pos[None, :] >= begin[:, None] - LEFT) & (
            key_pos[None, :] < begin[:, None] + stretch + lookup
        )
        inside = inside & (key_pos[None, :] >= 0) & (key_pos[None, :] < length)
        visible = inside | (key_pos[None, :] == query_pos[:, None])
        scores = (
            jnp.einsum("qhe,khe->hqk", query3, key_ext3, preferred_element_type=jnp.float32) * scale
        )
        scores = jnp.where(visible[None], scores, FLOOR_SCORE)
        highest = jnp.max(scores, axis=-1, keepdims=True)
        expo = jnp.where(visible[None], jnp.exp(scores - highest), 0.0)
        totals = jnp.sum(expo, axis=-1)
        mixed = jnp.einsum(
            "hqk,khe->qhe",
            expo.astype(jnp.bfloat16),
            value_ext3,
            preferred_element_type=jnp.float32,
        )
        return (mixed / totals.T[:, :, None]).reshape(block_rows, -1).astype(jnp.bfloat16)

    return lax.map(one_block, jnp.arange(number, dtype=jnp.int32)).reshape(query_count, -1)


def per_device(
    frames,
    lengths,
    stretch_sizes,
    look_ahead,
    norm_one,
    norm_two,
    w_query,
    w_key,
    w_value,
    w_out,
    conv_kernel,
):
    source = frames[0]
    row_count, model_width = source.shape
    head_count = HEADS
    depth_count = model_width // head_count
    scale = float(depth_count) ** (-0.5)
    seq_place = lax.axis_index("seq")
    length = lengths[0]
    stretch = stretch_sizes[0]
    lookup = look_ahead[0]
    first_pos = seq_place * row_count
    query_pos = first_pos + jnp.arange(row_count, dtype=jnp.int32)
    normed = layer_norm(source, norm_one).astype(jnp.bfloat16)
    query = jnp.dot(normed, w_query, preferred_element_type=jnp.float32).astype(jnp.bfloat16)
    key_rows = jnp.dot(normed, w_key, preferred_element_type=jnp.float32).astype(jnp.bfloat16)
    value_rows = jnp.dot(normed, w_value, preferred_element_type=jnp.float32).astype(jnp.bfloat16)
    query3 = query.reshape(row_count, head_count, depth_count)
    key_piece = lax.all_gather(key_rows, "seq", axis=0, tiled=True)
    value_piece = lax.all_gather(value_rows, "seq", axis=0, tiled=True)
    piece_rows = key_piece.shape[0]
    state = fold_blocks(
        fresh_state(row_count, head_count, depth_count),
        query3,
        query_pos,
        key_piece.reshape(piece_rows, head_count, depth_count),
        value_piece.reshape(piece_rows, head_count, depth_count),
        length,
        scale,
    )
    context_full = finish_state(state)
    stacked = jnp.stack([key_rows, value_rows])
    extended = with_halo(stacked, (("seq", 1),), HALO)
    context_stretch = windowed(
        query3,
        extended[0].reshape(-1, head_count, depth_count),
        extended[1].reshape(-1, head_count, depth_count),
        first_pos,
        length,
        stretch,
        lookup,
        scale,
    )
    valid = (query_pos < length).astype(jnp.float32)
    kernel_taps = conv_kernel.astype(jnp.float32)
    projected = jnp.dot(
        jnp.concatenate([context_full, context_stretch], axis=0),
        w_out,
        preferred_element_type=jnp.float32,
    )
    residual_full = source.astype(jnp.float32) + projected[:row_count]
    residual_stretch = source.astype(jnp.float32) + projected[row_count:]
    input_full = (layer_norm(residual_full, norm_two) * valid[:, None]).astype(jnp.bfloat16)
    input_stretch = (layer_norm(residual_stretch, norm_two) * valid[:, None]).astype(jnp.bfloat16)
    padded_full = with_halo(input_full, (("seq", 0),), KERNEL // 2)
    carried = shifted(input_stretch[row_count - (KERNEL - 1) :], "seq", 1)
    padded_stretch = jnp.concatenate([carried, input_stretch], axis=0)
    conv_full = jnp.zeros((row_count, model_width), jnp.float32)
    conv_stretch = jnp.zeros((row_count, model_width), jnp.float32)
    for offset in range(KERNEL):
        conv_full = conv_full + kernel_taps[offset] * padded_full[
            offset : offset + row_count
        ].astype(jnp.float32)
        conv_stretch = conv_stretch + kernel_taps[offset] * padded_stretch[
            offset : offset + row_count
        ].astype(jnp.float32)
    output_full = residual_full + jax.nn.silu(conv_full)
    output_stretch = residual_stretch + jax.nn.silu(conv_stretch)
    push = (
        2.0 * (output_stretch - output_full) * valid[:, None] / jnp.sqrt(length.astype(jnp.float32))
    )
    sigma = jax.nn.sigmoid(conv_stretch)
    slope = push * sigma * (1.0 + conv_stretch * (1.0 - sigma))
    grad_local = jnp.stack(
        [
            jnp.sum(slope * padded_stretch[offset : offset + row_count].astype(jnp.float32), axis=0)
            for offset in range(KERNEL)
        ]
    )
    kernel_grad = lax.psum(grad_local, ("seq", "dp"))
    return (
        output_full.astype(jnp.bfloat16)[None],
        output_stretch.astype(jnp.bfloat16)[None],
        kernel_grad,
    )


def solution(mesh):
    in_specs = (P("dp", "seq", None), P("dp"), P("dp"), P("dp"), P(), P(), P(), P(), P(), P(), P())
    out_specs = (P("dp", "seq", None), P("dp", "seq", None), P())
    return jax.shard_map(
        per_device, mesh=mesh, in_specs=in_specs, out_specs=out_specs, check_vma=False
    )
```

profile of v0, /device:TPU:1, one launch (start us, length us, event | category | flops | bytes accessed | tf_op | source)
XLA Modules:
  0.0 529.1 jit_solution(953079403688141178)
XLA Ops:
  9.7 2.9 convolution_convert_fusion.2
  17.4 6.2 %collective-permute-start = (bf16[2,128,1024]{2,1,0:T(8,128)(2,1)}, bf16[2,128,1024]{2,1,0:T(8,128)(2,1)}, u32[]{:S(2)}, u32[]{:S(2)}) collective-permute-start(bf16[2,128,1024]{2,1,0:T(8,128)(2,1)} %pad_maximum_fusion.1), channel_id=1, source_target_pairs={{0,16},{16,32},{32,48},{48,64},{64,80},{80,96},{96,112},{112,128},... | collective-permute-start | bytes 1572872 | tf_op jit(solution)/shard_map/ppermute | solution.py:25
  32.2 5.7 %collective-permute-done = bf16[2,128,1024]{2,1,0:T(8,128)(2,1)} collective-permute-done((bf16[2,128,1024]{2,1,0:T(8,128)(2,1)}, bf16[2,128,1024]{2,1,0:T(8,128)(2,1)}, u32[]{:S(2)}, u32[]{:S(2)}) %collective-permute-start) | collective-permute-done | bytes 524320 | tf_op jit(solution)/shard_map/ppermute | solution.py:25
  44.6 3.8 fusion.188
  48.3 2.9 fusion.36
  51.3 31.7 %all-gather.3.cloned.1.call-done = bf16[2048,1024]{1,0:T(8,128)(2,1)} async-done(((bf16[128,1024]{1,0:T(8,128)(2,1)}), bf16[2048,1024]{1,0:T(8,128)(2,1)}) %all-gather.3.cloned.1.call-update) | async-done | bytes 4194320 | tf_op jit(solution)/shard_map/all_gather | solution.py:164
  83.0 11.6 %reshape.276 = bf16[8,256,16,64]{3,2,1,0:T(8,128)(2,1)} reshape(bf16[2048,1024]{1,0:T(8,128)(2,1)} %all-gather.3.cloned.1.call-done) | data formatting | bytes 8388608 | tf_op jit(solution)/shard_map/reshape;reshape | solution.py:83
  94.6 10.4 %copy.25 = bf16[8,256,16,64]{1,3,2,0:T(8,128)(2,1)} copy(bf16[8,256,16,64]{3,2,1,0:T(8,128)(2,1)} %reshape.276) | data formatting | bytes 8388608
  104.9 41.3 %all-gather.5.cloned.1.call-done = bf16[2048,1024]{1,0:T(8,128)(2,1)} async-done(((bf16[128,1024]{1,0:T(8,128)(2,1)}), bf16[2048,1024]{1,0:T(8,128)(2,1)}) %all-gather.5.cloned.1.call-update) | async-done | bytes 4194320 | tf_op jit(solution)/shard_map/all_gather | solution.py:165
  146.3 11.6 %reshape.277 = bf16[8,256,16,64]{3,2,1,0:T(8,128)(2,1)} reshape(bf16[2048,1024]{1,0:T(8,128)(2,1)} %all-gather.5.cloned.1.call-done) | data formatting | bytes 8388608 | tf_op jit(solution)/shard_map/reshape;reshape | solution.py:84
  157.8 10.3 %copy.26 = bf16[8,256,16,64]{1,3,2,0:T(8,128)(2,1)} copy(bf16[8,256,16,64]{3,2,1,0:T(8,128)(2,1)} %reshape.277) | data formatting | bytes 8388608
  168.2 65.6 %while.5 = (s32[]{:T(128)}, f32[16,128]{1,0:T(8,128)S(1)}, f32[16,128]{1,0:T(8,128)S(1)}, f32[128,1024]{0,1:T(8,128)S(1)}, s32[8]{0:T(128)S(1)}, /*index=5*/s32[...) while((s32[]{:T(128)}, f32[16,128]{1,0:T(8,128)S(1)}, ...), condition=%wide.region_5.6_spmd.clone, body=%wide.region_2.5_spmd.clone.sunk | while | flops 141374336 | bytes 17306316 | solution.py:95
  170.3 2.9 fusion.211
  178.5 2.9 fusion.211
  186.7 2.9 fusion.211
  194.9 2.9 fusion.211
  203.1 2.9 fusion.211
  211.3 2.9 fusion.211
  219.5 2.9 fusion.211
  227.7 2.9 fusion.211
  245.8 3.9 collective-permute-done.3
  249.7 21.2 %fusion.106 = (f32[1024]{0:T(1024)S(1)}, f32[1024]{0:T(1024)S(1)}, f32[1024]{0:T(1024)S(1)}, f32[1024]{0:T(1024)S(1)}, f32[1024]{0:T(1024)S(1)}, /*index=5*/f32[...) fusion(bf16[128,1024]{1,0:T(8,128)(2,1)} %copy-done.3, ...), kind=kLoop, calls=%fused_computation.235 | loop fusion | flops 57138176 | bytes 3432964 | tf_op jit(solution)/shard_map/reduce_sum | solution.py:221
  273.7 4.7 stack.139
  280.4 240.6 %all-reduce.2.cloned.1.call-done = f32[31,1024]{1,0:T(8,128)} async-done(((f32[31,1024]{1,0:T(8,128)}), f32[31,1024]{1,0:T(8,128)}) %all-reduce.2.cloned.1.call-update) | async-done | bytes 126992 | tf_op jit(solution)/shard_map/psum | solution.py:225
  (174 shorter events, 74.9 us)
Async XLA Ops:
  7.2 226.7 %copy-start = (bf16[1024,1024]{1,0:T(8,128)(2,1)S(1)}, bf16[1024,1024]{1,0:T(8,128)(2,1)}, u32[]{:S(2)}) copy-start(bf16[1024,1024]{1,0:T(8,128)(2,1)} %param.22) | copy-start | bytes 6291460
  7.2 5.5 %copy-start.2 = (bf16[1,128,1024]{2,1,0:T(8,128)(2,1)S(1)}, bf16[1,128,1024]{2,1,0:T(8,128)(2,1)}, u32[]{:S(2)}) copy-start(bf16[1,128,1024]{2,1,0:T(8,128)(2,1)} %param.13) | copy-start | bytes 786436
  7.2 5.5 %copy-start.10 = (f32[1024]{0:T(1024)S(1)}, f32[1024]{0:T(1024)}, u32[]{:S(2)}) copy-start(f32[1024]{0:T(1024)} %param.17) | copy-start | bytes 12292
  7.2 75.8 %all-gather.3.cloned.1.call-start = ((), (), s32[]{:S(2)}) async-start(), calls=%async_computation | async-start | bytes 4456448 | tf_op jit(solution)/shard_map/all_gather | solution.py:164
  12.6 3.0 copy-start.5
  12.6 133.7 %all-gather.5.cloned.1.call-start = ((), (), s32[]{:S(2)}) async-start(), calls=%async_computation.1 | async-start | bytes 4456448 | tf_op jit(solution)/shard_map/all_gather | solution.py:165
  15.5 505.5 %all-reduce.2.cloned.1.call-start = ((), (), s32[]{:S(2)}) async-start(), calls=%async_computation.2 | async-start | bytes 262144 | tf_op jit(solution)/shard_map/psum | solution.py:225
  15.5 15.3 %copy-start.9 = (bf16[31,1024]{1,0:T(8,128)(2,1)S(1)}, bf16[31,1024]{1,0:T(8,128)(2,1)}, u32[]{:S(2)}) copy-start(bf16[31,1024]{1,0:T(8,128)(2,1)} %param.23) | copy-start | bytes 190468
  15.5 23.2 %copy-start.6 = (bf16[128,1024]{1,0:T(8,128)(2,1)S(1)}, bf16[128,1024]{1,0:T(8,128)(2,1)}, u32[]{:S(2)}) copy-start(bf16[128,1024]{1,0:T(8,128)(2,1)} %convolution_convert_fusion) | copy-start | bytes 786436
  17.4 20.4 %collective-permute-start = (bf16[2,128,1024]{2,1,0:T(8,128)(2,1)}, bf16[2,128,1024]{2,1,0:T(8,128)(2,1)}, u32[]{:S(2)}, u32[]{:S(2)}) collective-permute-start(bf16[2,128,1024]{2,1,0:T(8,128)(2,1)} %pad_maximum_fusion.1), channel_id=1, source_target_pairs={{0,16},{16,32},{32,48},{48,64},{64,80},{80,96},{96,112},{112,128},... | collective-permute-start | bytes 1572872 | tf_op jit(solution)/shard_map/ppermute | solution.py:25
  23.6 15.1 %collective-permute-start.1 = (bf16[2,128,1024]{2,1,0:T(8,128)(2,1)}, bf16[2,128,1024]{2,1,0:T(8,128)(2,1)}, u32[]{:S(2)}, u32[]{:S(2)}) collective-permute-start(bf16[2,128,1024]{2,1,0:T(8,128)(2,1)} %pad_maximum_fusion.1), channel_id=1, source_target_pairs={{16,0},{32,16},{48,32},{64,48},{80,64},{96,80},{112,96},{128,112},... | collective-permute-start | bytes 1572872 | tf_op jit(solution)/shard_map/ppermute | solution.py:26
  44.6 3.8 copy-start.8
  173.2 2.6 copy-start.1
  181.4 2.6 copy-start.1
  189.6 2.6 copy-start.1
  197.8 2.6 copy-start.1
  214.2 2.6 copy-start.1
  222.4 2.6 copy-start.1
  230.6 2.6 copy-start.1
  236.6 3.1 copy-start.7
  237.3 12.4 %collective-permute-start.4 = (bf16[30,1024]{1,0:T(8,128)(2,1)S(1)}, bf16[30,1024]{1,0:T(8,128)(2,1)S(1)}, u32[]{:S(2)}, u32[]{:S(2)}) collective-permute-start(bf16[30,1024]{1,0:T(8,128)(2,1)S(1)} %slice.576), channel_id=1, source_target_pairs={{0,16},{16,32},{32,48},{48,64},{64,80},{80,96},{96,112},{112,128},... | collective-permute-start | bytes 184328 | tf_op jit(solution)/shard_map/ppermute | solution.py:34
  240.3 5.5 %collective-permute-start.2 = (bf16[15,1024]{1,0:T(8,128)(2,1)}, bf16[15,1024]{1,0:T(8,128)(2,1)}, u32[]{:S(2)}, u32[]{:S(2)}) collective-permute-start(bf16[15,1024]{1,0:T(8,128)(2,1)} %get-tuple-element.207), channel_id=1, source_target_pairs={{0,16},{16,32},{32,48},{48,64},{64,80},{80,96},{96,112},{112,128},... | collective-permute-start | bytes 92168 | tf_op jit(solution)/shard_map/ppermute | solution.py:25
  242.4 7.3 %collective-permute-start.3 = (bf16[15,1024]{1,0:T(8,128)(2,1)}, bf16[15,1024]{1,0:T(8,128)(2,1)}, u32[]{:S(2)}, u32[]{:S(2)}) collective-permute-start(bf16[15,1024]{1,0:T(8,128)(2,1)} %get-tuple-element.208), channel_id=1, source_target_pairs={{16,0},{32,16},{48,32},{64,48},{80,64},{96,80},{112,96},{128,112},... | collective-permute-start | bytes 92168 | tf_op jit(solution)/shard_map/ppermute | solution.py:26
  245.7 25.1 %copy-start.4 = (bf16[128,1024]{1,0:T(8,128)(2,1)S(1)}, bf16[128,1024]{1,0:T(8,128)(2,1)}, u32[]{:S(2)}) copy-start(bf16[128,1024]{1,0:T(8,128)(2,1)} %copy-done.3) | copy-start | bytes 786436
  (4 other events, 4.7 us)
Sparse Core Ops, SparseCore 0:
  12.7 70.2 all-gather.2
  86.3 59.9 all-gather.4
  278.6 242.3 all-reduce.1
where the time goes:
time: 532 us; the launch traced here: 529 us
  waiting for transfers between devices  324 us (61%)
  local copies, waits for them, and re-layouts  62.5 us (12%)
  matrix products  60.7 us (11%)
  other arithmetic  44.3 us (8%)
  between operations  16.1 us (3%)
  starting transfers between devices  15.5 us (3%)
  loops' own time  5.82 us (1%)
    psum x1, waiting for transfers between devices, per_device(): kernel_grad = lax.psum(grad_local, ('seq', 'dp'))  241 us
    all_gather x1, waiting for transfers between devices, per_device(): value_piece = lax.all_gather(value_rows, 'seq', axis=0, tiled=True)  41.3 us
    all_gather x1, waiting for transfers between devices, per_device(): key_piece = lax.all_gather(key_rows, 'seq', axis=0, tiled=True)  31.7 us
    reduce_sum x4, other arithmetic, per_device(): jnp.sum(slope * padded_stretch[offset:offset + row_count].astype(jnp.floa...  24 us
    dot_general x8, matrix products, fold_keys(): jnp.einsum('qhe,khe->hqk', query3, key3, preferred_element_type=jnp.float32)  23.4 us
    unnamed x27, local copies, waits for them, and re-layouts  23.2 us
    dot_general x8, matrix products, fold_keys(): jnp.einsum('hqk,khe->qhe', expo.astype(jnp.bfloat16), value3, preferred_e...  21 us
    another operation x1, local copies, waits for them, and re-layouts, fold_blocks(): values3.reshape(number, block_width, values3.shape[1], values3.shape[2])  11.6 us
  transfers between devices with their start and end apart: 8, of which 6 were waited for; matrix products, arithmetic and copies ran while one was open for 9% of the time, Pallas kernels for 0%

commit v1 on v0

v1 whole, which is shorter than its diff:
```python
import functools

import jax
import jax.numpy as jnp
from jax import lax
from jax.experimental import pallas as pl
from jax.experimental.pallas import tpu as pltpu
from jax.sharding import PartitionSpec as P

HEADS = 16
DEPTH = 64
KERNEL = 31
LEFT = 64
EPSILON = 1e-05
FLOOR_SCORE = -1e30
BEFORE = 32
AFTER = 16
LANES = 128
F32 = jnp.float32
BF16 = jnp.bfloat16


def norm_rows(values, gain):
    center = values - jnp.mean(values, axis=-1, keepdims=True)
    spread = jnp.mean(center * center, axis=-1, keepdims=True)
    return center * lax.rsqrt(spread + EPSILON) * gain


def low_lanes(rows):
    return lax.broadcasted_iota(jnp.int32, (rows, LANES), 1) < DEPTH


def half_turn(value):
    return pltpu.roll(value, DEPTH, 1)


def dot_rows(left, right):
    return lax.dot_general(left, right, (((1,), (1,)), ((), ())), preferred_element_type=F32)


def project_kernel(frames_ref, gain_ref, wq_ref, wk_ref, wv_ref, out_ref, normed_ref):
    rows = frames_ref.shape[0]
    half = rows // 2

    @pl.when(pl.program_id(0) == 0)
    def _():
        normed_ref[...] = norm_rows(frames_ref[...].astype(F32), gain_ref[...]).astype(BF16)

    normed = normed_ref[...]
    query = jnp.dot(normed, wq_ref[...], preferred_element_type=F32) * (DEPTH**-0.5)
    key = jnp.dot(normed, wk_ref[...], preferred_element_type=F32)
    value = jnp.dot(normed, wv_ref[...], preferred_element_type=F32)
    low = low_lanes(rows)
    low_half = low_lanes(half)
    for pair in range(out_ref.shape[0] // 2):
        cols = slice(pair * LANES, (pair + 1) * LANES)
        k, v, q = key[:, cols], value[:, cols], query[:, cols]
        kr, vr, qr = half_turn(k), half_turn(v), half_turn(q)
        out_ref[2 * pair, :rows] = jnp.where(low, k, vr).astype(BF16)
        out_ref[2 * pair + 1, :rows] = jnp.where(low, kr, v).astype(BF16)
        out_ref[2 * pair, rows:] = jnp.where(low_half, q[:half], qr[half:]).astype(BF16)
        out_ref[2 * pair + 1, rows:] = jnp.where(low_half, qr[:half], q[half:]).astype(BF16)


def project(frames, gain, wq, wk, wv):
    rows, width = frames.shape
    steps = 4
    cols = width // steps
    heads = HEADS // steps
    weight = pl.BlockSpec((width, cols), lambda i: (0, i))
    return pl.pallas_call(
        project_kernel,
        grid=(steps,),
        in_specs=[
            pl.BlockSpec((rows, width), lambda i: (0, 0)),
            pl.BlockSpec((1, width), lambda i: (0, 0)),
            weight,
            weight,
            weight,
        ],
        out_specs=pl.BlockSpec((heads, rows + rows // 2, LANES), lambda i: (i, 0, 0)),
        out_shape=jax.ShapeDtypeStruct((HEADS, rows + rows // 2, LANES), BF16),
        scratch_shapes=[pltpu.VMEM((rows, width), BF16)],
        compiler_params=pltpu.CompilerParams(vmem_limit_bytes=32 << 20),
        name="project",
    )(frames, gain, wq, wk, wv)


def attend_kernel(
    length_ref, stretch_ref, look_ref, packed_ref, out_ref, kv_ref, q_ref, bias_ref, s0_ref, s1_ref, ctx_ref
):
    blocks, packed_rows, _ = packed_ref.shape
    rows = packed_rows * 2 // 3
    half = rows // 2
    total = blocks * rows
    length = length_ref[0]
    stretch = stretch_ref[0].astype(F32)
    look = look_ref[0].astype(F32)
    length_f = length.astype(F32)
    low_half = low_lanes(half)
    kv_ref[:rows] = jnp.zeros((rows, LANES), BF16)
    kv_ref[rows + total :] = jnp.zeros((rows, LANES), BF16)
    for block in range(blocks):
        kv_ref[(block + 1) * rows : (block + 2) * rows] = packed_ref[block, :rows]
        q = packed_ref[block, rows:].astype(F32)
        q_ref[block * rows : block * rows + half] = jnp.where(low_half, q, 0.0).astype(BF16)
        q_ref[block * rows + half : (block + 1) * rows] = jnp.where(low_half, half_turn(q), 0.0).astype(BF16)
    key_pos = lax.broadcasted_iota(jnp.int32, (8, total), 1)
    bias_ref[...] = jnp.where(key_pos < length, 0.0, FLOOR_SCORE)
    ctx_ref[:BEFORE] = jnp.zeros((BEFORE, LANES), BF16)
    ctx_ref[BEFORE + total :] = jnp.zeros((AFTER, LANES), BF16)

    def at(index):
        return pl.ds(pl.multiple_of(index * rows, rows), rows)

    def score(index, s_ref):
        s_ref[...] = dot_rows(q_ref[at(index)], kv_ref[rows : rows + total]) + bias_ref[0:1]

    def finish(index, s_ref):
        start = pl.multiple_of(index * rows, rows)
        near = kv_ref[pl.ds(start, 3 * rows)]
        raw = dot_rows(q_ref[at(index)], near)
        row = lax.broadcasted_iota(jnp.int32, (rows, LANES), 0)
        lane = lax.broadcasted_iota(jnp.int32, (rows, LANES), 1)
        seen = (lane == row) | (lane + start < length)
        s_ref[:, at(index)] = jnp.where(seen, raw[:, rows : 2 * rows], FLOOR_SCORE)
        s = s_ref[...]
        highest = jnp.max(s, axis=-1, keepdims=True)
        expo = jnp.exp(s - highest)
        totals = jnp.sum(expo, axis=-1, keepdims=True)
        mixed = jnp.dot(expo.astype(BF16), kv_ref[rows : rows + total], preferred_element_type=F32)
        full = mixed / totals

        pos = (row + start).astype(F32)
        begin = jnp.floor((pos + 0.5) / stretch) * stretch
        first = jnp.maximum(begin - LEFT, 0.0)
        last = jnp.minimum(begin + stretch + look, length_f)
        parts = []
        for part in range(3):
            key_at = (lane + start + (part - 1) * rows).astype(F32)
            inside = (key_at >= first) & (key_at < last)
            if part == 1:
                inside = inside | (lane == row)
            parts.append(jnp.where(inside, raw[:, part * rows : (part + 1) * rows], FLOOR_SCORE))
        s = jnp.concatenate(parts, axis=1)
        highest = jnp.max(s, axis=-1, keepdims=True)
        expo = jnp.exp(s - highest)
        totals = jnp.sum(expo, axis=-1, keepdims=True)
        mixed = jnp.dot(expo.astype(BF16), near, preferred_element_type=F32)
        near_context = mixed / totals
        both = jnp.where(lane < DEPTH, half_turn(full), near_context)
        ctx_ref[pl.ds(pl.multiple_of(start + BEFORE, BEFORE), rows)] = both.astype(BF16)

    score(0, s0_ref)

    def body(step, carry):
        score(2 * step + 1, s1_ref)
        finish(2 * step, s0_ref)
        score(jnp.minimum(2 * step + 2, blocks - 1), s0_ref)
        finish(2 * step + 1, s1_ref)
        return carry

    lax.fori_loop(0, blocks // 2, body, 0)
    for block in range(blocks):
        out_ref[block] = ctx_ref[block * rows : block * rows + BEFORE + rows + AFTER]


def attend(length, stretch, look, packed):
    blocks, packed_rows, _ = packed.shape
    rows = packed_rows * 2 // 3
    total = blocks * rows
    smem = pl.BlockSpec(memory_space=pltpu.SMEM)
    vmem = pl.BlockSpec(memory_space=pltpu.VMEM)
    return pl.pallas_call(
        attend_kernel,
        in_specs=[smem, smem, smem, vmem],
        out_specs=vmem,
        out_shape=jax.ShapeDtypeStruct((blocks, BEFORE + rows + AFTER, LANES), BF16),
        scratch_shapes=[
            pltpu.VMEM((total + 2 * rows, LANES), BF16),
            pltpu.VMEM((total, LANES), BF16),
            pltpu.VMEM((8, total), F32),
            pltpu.VMEM((rows, total), F32),
            pltpu.VMEM((rows, total), F32),
            pltpu.VMEM((BEFORE + total + AFTER, LANES), BF16),
        ],
        compiler_params=pltpu.CompilerParams(vmem_limit_bytes=32 << 20),
        name="attend",
    )(length, stretch, look, packed)


def finish_kernel(
    place_ref,
    length_ref,
    ctx_ref,
    before_ref,
    frames_ref,
    after_ref,
    wo_ref,
    gain_ref,
    taps_ref,
    full_ref,
    near_ref,
    grad_ref,
    c_ref,
    res_ref,
    x_ref,
):
    rows, width = frames_ref.shape
    ext = BEFORE + rows + AFTER
    low = low_lanes(ext)
    for pair in range(HEADS // 2):
        cols = slice(pair * LANES, (pair + 1) * LANES)
        one, two = ctx_ref[2 * pair].astype(F32), ctx_ref[2 * pair + 1].astype(F32)
        c_ref[:ext, cols] = jnp.where(low, one, half_turn(two)).astype(BF16)
        c_ref[ext:, cols] = jnp.where(low, half_turn(one), two).astype(BF16)
    length = length_ref[0]
    source = jnp.concatenate([before_ref[...], frames_ref[...], after_ref[...]], axis=0).astype(F32)
    res_ref[...] = jnp.dot(c_ref[...], wo_ref[...], preferred_element_type=F32)
    pos = lax.broadcasted_iota(jnp.int32, (ext, 1), 0) + (place_ref[0] * rows - BEFORE)
    valid = (pos >= 0) & (pos < length)
    for part in range(2):
        span = slice(part * ext, (part + 1) * ext)
        residual = source + res_ref[span]
        res_ref[span] = residual
        normed = norm_rows(residual, gain_ref[...])
        x_ref[span] = jnp.where(valid, normed, 0.0).astype(BF16).astype(F32)
    inner = lax.broadcasted_iota(jnp.int32, (rows, 1), 0) + place_ref[0] * rows
    factor = jnp.where(inner < length, 2.0 / jnp.sqrt(jnp.full((rows, 1), length.astype(F32))), 0.0)

    def convolve(first, cols):
        total = jnp.zeros((rows, LANES), F32)
        for turn in range(8):
            offsets = [k for k in range(KERNEL) if (first + k) % 8 == turn]
            low_at = first + offsets[0]
            count = offsets[-1] - offsets[0] + rows
            piece = x_ref[low_at : low_at + count, cols]
            for k in offsets:
                skip = k - offsets[0]
                total = total + taps_ref[k : k + 1, cols] * piece[skip : skip + rows]
        return total

    def column(step, carry):
        cols = pl.ds(pl.multiple_of(step * LANES, LANES), LANES)
        conv_full = convolve(BEFORE - KERNEL // 2, cols)
        sig_full = 1.0 / (1.0 + jnp.exp(-conv_full))
        out_full = res_ref[BEFORE : BEFORE + rows, cols] + conv_full * sig_full
        full_ref[:, cols] = out_full.astype(BF16)
        near_first = ext + BEFORE - (KERNEL - 1)
        conv_near = convolve(near_first, cols)
        sig_near = 1.0 / (1.0 + jnp.exp(-conv_near))
        out_near = res_ref[ext + BEFORE : ext + BEFORE + rows, cols] + conv_near * sig_near
        near_ref[:, cols] = out_near.astype(BF16)
        slope = (out_near - out_full) * factor * (sig_near * (1.0 + conv_near * (1.0 - sig_near)))
        for turn in range(8):
            offsets = [k for k in range(KERNEL) if (near_first + k) % 8 == turn]
            low_at = near_first + offsets[0]
            count = offsets[-1] - offsets[0] + rows
            piece = x_ref[low_at : low_at + count, cols]
            for k in offsets:
                skip = k - offsets[0]
                term = jnp.sum(slope * piece[skip : skip + rows], axis=0, keepdims=True)
                grad_ref[2 * step + k // 16, k % 16 : k % 16 + 1] = term
        grad_ref[2 * step + 1, 15:16] = jnp.zeros((1, LANES), F32)
        return carry

    lax.fori_loop(0, width // LANES, column, 0)


def finish(place, length, ctx, before, frames, after, wo, gain, taps):
    rows, width = frames.shape
    ext = BEFORE + rows + AFTER
    smem = pl.BlockSpec(memory_space=pltpu.SMEM)
    vmem = pl.BlockSpec(memory_space=pltpu.VMEM)
    return pl.pallas_call(
        finish_kernel,
        in_specs=[smem, smem] + [vmem] * 7,
        out_specs=[vmem] * 3,
        out_shape=[
            jax.ShapeDtypeStruct((rows, width), BF16),
            jax.ShapeDtypeStruct((rows, width), BF16),
            jax.ShapeDtypeStruct((width // 64, 16, LANES), F32),
        ],
        scratch_shapes=[
            pltpu.VMEM((2 * ext, width), BF16),
            pltpu.VMEM((2 * ext, width), F32),
            pltpu.VMEM((2 * ext, width), F32),
        ],
        compiler_params=pltpu.CompilerParams(vmem_limit_bytes=40 << 20),
        name="finish",
    )(place, length, ctx, before, frames, after, wo, gain, taps)


def swap(value, axis):
    return lax.all_to_all(value, axis, 0, 0, tiled=True)


def spread_out(value, axis):
    size = lax.axis_size(axis)
    return swap(jnp.broadcast_to(value[None], (size,) + value.shape), axis)


def per_device(
    frames,
    lengths,
    stretch_sizes,
    look_ahead,
    norm_one,
    norm_two,
    w_query,
    w_key,
    w_value,
    w_out,
    conv_kernel,
):
    source = frames[0]
    rows, width = source.shape
    size = lax.axis_size("seq")
    place = lax.axis_index("seq").reshape(1).astype(jnp.int32)
    up = [(i, i + 1) for i in range(size - 1)]
    down = [(j, i) for i, j in up]
    before = lax.ppermute(source[rows - BEFORE :], "seq", up)
    after = lax.ppermute(source[:AFTER], "seq", down)
    taps = jnp.pad(conv_kernel.astype(F32), ((0, 1), (0, 0)))
    packed = project(source, norm_one[None], w_query, w_key, w_value)
    packed = swap(packed, "seq")
    ctx = attend(lengths, stretch_sizes, look_ahead, packed)
    ctx = swap(ctx, "seq")
    full, near, grad = finish(
        place, lengths, ctx, before, source, after, w_out, norm_two[None], taps
    )
    piece = jnp.sum(swap(grad, "seq"), axis=0)
    piece = jnp.sum(spread_out(piece, "dp"), axis=0)
    grads = spread_out(piece, "seq")
    grads = grads.reshape(width // LANES, 32, LANES).transpose(1, 0, 2).reshape(32, width)
    return full[None], near[None], grads[:KERNEL]


def solution(mesh):
    in_specs = (P("dp", "seq", None), P("dp"), P("dp"), P("dp"), P(), P(), P(), P(), P(), P(), P())
    out_specs = (P("dp", "seq", None), P("dp", "seq", None), P())
    return jax.shard_map(
        per_device, mesh=mesh, in_specs=in_specs, out_specs=out_specs, check_vma=False
    )
```

time: 532 us -> 117 us (0.22)
  waiting for transfers between devices: 324 us -> 18.7 us
  matrix products: 60.7 us -> 0 us
  local copies, waits for them, and re-layouts: 62.5 us -> 7.22 us
  other arithmetic: 44.3 us -> 0.05 us
  blocking collectives: 0 us -> 41.2 us
  Pallas kernels: 0 us -> 26.1 us
  between operations: 16.1 us -> 2.7 us
  loops' own time: 5.82 us -> 0 us
    psum x1 -> x0, waiting for transfers between devices: 241 us -> none  [per_device(): kernel_grad = lax.psum(grad_local, ('seq', 'dp'))]
    all_gather x2 -> x0, waiting for transfers between devices: 73.1 us -> none  [the longest x1 41.3 us: per_device(): value_piece = lax.all_gather(value_rows, 'seq', axis=0, tiled=True)]
    dot_general x21 -> x0, matrix products: 56.9 us -> none  [the longest x8 23.4 us: fold_keys(): jnp.einsum('qhe,khe->hqk', query3, key3, preferred_element_type=jnp.float32)]
    all_to_all x0 -> x3, blocking collectives: none -> 41.2 us  [swap(): return lax.all_to_all(value, axis, 0, 0, tiled=True)]
    reduce_sum x16 -> x2, other arithmetic: 30.8 us -> 0.04 us  [the longest x1 0.02 us: per_device(): piece = jnp.sum(swap(grad, 'seq'), axis=0)]
    another operation x3 -> x0, local copies, waits for them, and re-layouts: 27.9 us -> none  [the longest x1 11.6 us: fold_blocks(): values3.reshape(number, block_width, values3.shape[1], values3.shape[2])]
    pallas_call x0 -> x3, Pallas kernels: none -> 26.1 us  [the longest x1 13.5 us: attend(): pl.pallas_call(attend_kernel, in_specs=[smem, smem, smem, vmem], out_spec...]
    unnamed x27 -> x20, local copies, waits for them, and re-layouts: 23.2 us -> 7.11 us
  transfers between devices with their start and end apart: 8 -> 4, of which waited for: 6 -> 2; matrix products, arithmetic and copies ran while one was open for 9% -> 0% of each run, Pallas kernels for 0% -> 0%
where the time goes in v1:
time: 117 us; the launch traced here: 116 us
  blocking collectives  41.2 us (35%)
  Pallas kernels  26.1 us (22%)
  starting transfers between devices  20.1 us (17%)
  waiting for transfers between devices  18.7 us (16%)
  local copies, waits for them, and re-layouts  7.22 us (6%)
  between operations  2.7 us (2%)
    all_to_all x3, blocking collectives, swap(): return lax.all_to_all(value, axis, 0, 0, tiled=True)  41.2 us
    pallas_call x1, Pallas kernels, attend(): pl.pallas_call(attend_kernel, in_specs=[smem, smem, smem, vmem], out_spec...  13.5 us
    all_to_all x2, starting transfers between devices, swap(): return lax.all_to_all(value, axis, 0, 0, tiled=True)  13.1 us
    all_to_all x2, waiting for transfers between devices, swap(): return lax.all_to_all(value, axis, 0, 0, tiled=True)  12.2 us
    pallas_call x1, Pallas kernels, finish(): pl.pallas_call(finish_kernel, in_specs=[smem, smem] + [vmem] * 7, out_spe...  8.98 us
    unnamed x20, local copies, waits for them, and re-layouts  7.11 us
    ppermute x1, waiting for transfers between devices, per_device(): after = lax.ppermute(source[:AFTER], 'seq', down)  6.48 us
    ppermute x1, starting transfers between devices, per_device(): before = lax.ppermute(source[rows - BEFORE:], 'seq', up)  5.05 us
  transfers between devices with their start and end apart: 4, of which 2 were waited for; matrix products, arithmetic and copies ran while one was open for 0% of the time, Pallas kernels for 0%

profile of v1, /device:TPU:1, one launch (start us, length us, event | category | flops | bytes accessed | tf_op | source)
XLA Modules:
  0.0 116.1 jit_solution(14982303321552678252)
XLA Ops:
  0.6 0.0 copy-start
  0.6 1.6 %copy-done = bf16[1024,1024]{1,0:T(8,128)(2,1)S(1)} copy-done((bf16[1024,1024]{1,0:T(8,128)(2,1)S(1)}, bf16[1024,1024]{1,0:T(8,128)(2,1)}, u32[]{:S(2)}) %copy-start) | copy-done | bytes 2097176
  2.2 1.6 %copy-done.1 = bf16[1024,1024]{1,0:T(8,128)(2,1)S(1)} copy-done((bf16[1024,1024]{1,0:T(8,128)(2,1)S(1)}, bf16[1024,1024]{1,0:T(8,128)(2,1)}, u32[]{:S(2)}) %copy-start.1) | copy-done | bytes 2097176
  3.8 1.6 %copy-done.2 = bf16[1024,1024]{1,0:T(8,128)(2,1)S(1)} copy-done((bf16[1024,1024]{1,0:T(8,128)(2,1)S(1)}, bf16[1024,1024]{1,0:T(8,128)(2,1)}, u32[]{:S(2)}) %copy-start.2) | copy-done | bytes 2097176
  5.4 0.9 copy-done.4
  6.4 0.7 copy-done.6
  7.0 3.7 %project.1 = bf16[16,192,128]{2,1,0:T(8,128)(2,1)} custom-call(bf16[128,1024]{1,0:T(8,128)(2,1)S(1)} %bitcast.17, f32[1,1024]{1,0:T(1,128)S(1)} %bitcast.19, bf16[1024,1024]{1,0:T(8,128)(2,1)S(1)} %copy-done, bf16[1024,1024]{1,0:T(8,128)(2,1)S(1)} %copy-done.1, bf16[1024,1024]{1,0:T(8,128)(2,1)S(1)} %copy-done.2), custom_call_target="tpu_custom_call" | custom-call | tf_op jit(solution)/shard_map/project/pallas_call | solution.py:71
  10.7 8.6 %all-to-all-start = ((bf16[16,192,128]{2,1,0:T(8,128)(2,1)}), bf16[16,192,128]{2,1,0:T(8,128)(2,1)S(1)}, u32[]{:S(2)}, u32[]{:S(2)}) async-start(bf16[16,192,128]{2,1,0:T(8,128)(2,1)} %project.1), calls=%async_computation | async-start | bytes 1572864 | tf_op jit(solution)/shard_map/all_to_all | solution.py:295
  21.2 12.2 %all-to-all-done.packed_ref = bf16[16,192,128]{2,1,0:T(8,128)(2,1)S(1)} async-done(((bf16[16,192,128]{2,1,0:T(8,128)(2,1)}), bf16[16,192,128]{2,1,0:T(8,128)(2,1)S(1)}, u32[]{:S(2)}, u32[]{:S(2)}) %all-to-all-start) | async-done | bytes 786464 | tf_op jit(solution)/shard_map/all_to_all | solution.py:295
  33.5 13.5 %attend.1 = bf16[16,176,128]{2,1,0:T(8,128)(2,1)} custom-call(s32[1]{0:T(128)S(6)} %copy.17.length_ref, s32[1]{0:T(128)S(6)} %copy.18.stretch_ref, s32[1]{0:T(128)S(6)} %copy.19.look_ref, bf16[16,192,128]{2,1,0:T(8,128)(2,1)S(1)} %all-to-all-done.packed_ref), custom_call_target="tpu_custom_call" | custom-call | tf_op jit(solution)/shard_map/attend/pallas_call | solution.py:174
  47.0 4.5 %all-to-all-start.1 = ((bf16[16,176,128]{2,1,0:T(8,128)(2,1)}), bf16[16,176,128]{2,1,0:T(8,128)(2,1)S(1)}, u32[]{:S(2)}, u32[]{:S(2)}) async-start(bf16[16,176,128]{2,1,0:T(8,128)(2,1)} %attend.1), calls=%async_computation.1 | async-start | bytes 1441792 | tf_op jit(solution)/shard_map/all_to_all | solution.py:295
  51.5 0.0 copy-done.5
  51.5 5.1 %collective-permute-start = (bf16[32,1024]{1,0:T(8,128)(2,1)S(1)}, bf16[32,1024]{1,0:T(8,128)(2,1)S(1)}, u32[]{:S(2)}, u32[]{:S(2)}) collective-permute-start(bf16[32,1024]{1,0:T(8,128)(2,1)S(1)} %slice_bitcast_fusion), channel_id=1, source_target_pairs={{0,16},{16,32},{32,48},{48,64},{64,80},{80,96},{96,112},{112,128},... | collective-permute-start | bytes 196616 | tf_op jit(solution)/shard_map/ppermute | solution.py:322
  56.6 1.9 %collective-permute-start.1 = (bf16[16,1024]{1,0:T(8,128)(2,1)S(1)}, bf16[16,1024]{1,0:T(8,128)(2,1)S(1)}, u32[]{:S(2)}, u32[]{:S(2)}) collective-permute-start(bf16[16,1024]{1,0:T(8,128)(2,1)S(1)} %slice_bitcast_fusion.1), channel_id=1, source_target_pairs={{16,0},{32,16},{48,32},{64,48},{80,64},{96,80},{112,96},{128,112},... | collective-permute-start | bytes 98312 | tf_op jit(solution)/shard_map/ppermute | solution.py:323
  58.6 6.5 %collective-permute-done.1.after_ref = bf16[16,1024]{1,0:T(8,128)(2,1)S(1)} collective-permute-done((bf16[16,1024]{1,0:T(8,128)(2,1)S(1)}, bf16[16,1024]{1,0:T(8,128)(2,1)S(1)}, u32[]{:S(2)}, u32[]{:S(2)}) %collective-permute-start.1) | collective-permute-done | bytes 32800 | tf_op jit(solution)/shard_map/ppermute | solution.py:323
  65.0 0.0 collective-permute-done.before_ref
  65.0 0.0 all-to-all-done.1.ctx_ref
  65.1 0.0 copy-done.7
  65.1 9.0 %finish.1 = (bf16[128,1024]{1,0:T(8,128)(2,1)}, bf16[128,1024]{1,0:T(8,128)(2,1)}, f32[16,16,128]{2,1,0:T(8,128)S(1)}) custom-call(s32[1]{0:T(128)} %bitcast.place_ref, s32[1]{0:T(128)S(6)} %copy.17.length_ref, bf16[16,176,128]{2,1,0:T(8,128)(2,1)S(1)} %all-to-all-done.1.ctx_ref, bf16[32,1024]{1,0:T(8,128)(2,1)S(1)} %collective-permute-done.before_ref, ...), custom_call_target="tpu_custom_call" | custom-call | tf_op jit(solution)/shard_map/finish/pallas_call | solution.py:275
  74.0 11.7 %all_to_all.25 = f32[16,16,128]{2,1,0:T(8,128)S(1)} all-to-all(f32[16,16,128]{2,1,0:T(8,128)S(1)} %get-tuple-element.8), channel_id=1, replica_groups=mesh['seq'=16,'dp'=16] {'seq'}, dimensions={0} | all-to-all | bytes 262144 | tf_op jit(solution)/shard_map/all_to_all | solution.py:295
  85.8 16.6 %all_to_all.26 = f32[16,16,128]{2,1,0:T(8,128)S(1)} all-to-all(f32[16,16,128]{2,1,0:T(8,128)S(1)} %broadcast_in_dim.28), channel_id=1, replica_groups=mesh['seq'=16,'dp'=16] {'dp'}, dimensions={0} | all-to-all | bytes 262144 | tf_op jit(solution)/shard_map/all_to_all | solution.py:295
  102.5 12.8 %all_to_all.27 = f32[16,16,128]{2,1,0:T(8,128)S(1)} all-to-all(f32[16,16,128]{2,1,0:T(8,128)S(1)} %broadcast_in_dim.29), channel_id=1, replica_groups=mesh['seq'=16,'dp'=16] {'seq'}, dimensions={0} | all-to-all | bytes 262144 | tf_op jit(solution)/shard_map/all_to_all | solution.py:295
  115.3 0.1 copy.15
  115.4 0.7 copy.16
  (18 shorter events, 0.1 us)
Async XLA Ops:
  0.6 1.6 %copy-start = (bf16[1024,1024]{1,0:T(8,128)(2,1)S(1)}, bf16[1024,1024]{1,0:T(8,128)(2,1)}, u32[]{:S(2)}) copy-start(bf16[1024,1024]{1,0:T(8,128)(2,1)} %wq_ref.1) | copy-start | bytes 6291460
  2.2 1.6 %copy-start.1 = (bf16[1024,1024]{1,0:T(8,128)(2,1)S(1)}, bf16[1024,1024]{1,0:T(8,128)(2,1)}, u32[]{:S(2)}) copy-start(bf16[1024,1024]{1,0:T(8,128)(2,1)} %wk_ref.1) | copy-start | bytes 6291460
  3.8 1.6 %copy-start.2 = (bf16[1024,1024]{1,0:T(8,128)(2,1)S(1)}, bf16[1024,1024]{1,0:T(8,128)(2,1)}, u32[]{:S(2)}) copy-start(bf16[1024,1024]{1,0:T(8,128)(2,1)} %wv_ref.1) | copy-start | bytes 6291460
  5.4 0.9 copy-start.4
  6.4 0.7 copy-start.6
  10.7 40.8 %copy-start.5 = (bf16[1,128,1024]{2,1,0:T(8,128)(2,1)S(1)}, bf16[1,128,1024]{2,1,0:T(8,128)(2,1)}, u32[]{:S(2)}) copy-start(bf16[1,128,1024]{2,1,0:T(8,128)(2,1)} %param.11) | copy-start | bytes 786436
  10.7 47.8 %copy-start.8 = (bf16[31,1024]{1,0:T(8,128)(2,1)S(1)}, bf16[31,1024]{1,0:T(8,128)(2,1)}, u32[]{:S(2)}) copy-start(bf16[31,1024]{1,0:T(8,128)(2,1)} %param.21) | copy-start | bytes 190468
  10.7 54.3 %copy-start.3 = (bf16[1024,1024]{1,0:T(8,128)(2,1)S(1)}, bf16[1024,1024]{1,0:T(8,128)(2,1)}, u32[]{:S(2)}) copy-start(bf16[1024,1024]{1,0:T(8,128)(2,1)} %wo_ref.1) | copy-start | bytes 6291460
  10.7 54.3 %copy-start.7 = (f32[1024]{0:T(1024)S(1)}, f32[1024]{0:T(1024)}, u32[]{:S(2)}) copy-start(f32[1024]{0:T(1024)} %param.16) | copy-start | bytes 12292
  10.7 22.8 %all-to-all-start = ((bf16[16,192,128]{2,1,0:T(8,128)(2,1)}), bf16[16,192,128]{2,1,0:T(8,128)(2,1)S(1)}, u32[]{:S(2)}, u32[]{:S(2)}) async-start(bf16[16,192,128]{2,1,0:T(8,128)(2,1)} %project.1), calls=%async_computation | async-start | bytes 1572864 | tf_op jit(solution)/shard_map/all_to_all | solution.py:295
  47.0 18.1 %all-to-all-start.1 = ((bf16[16,176,128]{2,1,0:T(8,128)(2,1)}), bf16[16,176,128]{2,1,0:T(8,128)(2,1)S(1)}, u32[]{:S(2)}, u32[]{:S(2)}) async-start(bf16[16,176,128]{2,1,0:T(8,128)(2,1)} %attend.1), calls=%async_computation.1 | async-start | bytes 1441792 | tf_op jit(solution)/shard_map/all_to_all | solution.py:295
  51.5 13.5 %collective-permute-start = (bf16[32,1024]{1,0:T(8,128)(2,1)S(1)}, bf16[32,1024]{1,0:T(8,128)(2,1)S(1)}, u32[]{:S(2)}, u32[]{:S(2)}) collective-permute-start(bf16[32,1024]{1,0:T(8,128)(2,1)S(1)} %slice_bitcast_fusion), channel_id=1, source_target_pairs={{0,16},{16,32},{32,48},{48,64},{64,80},{80,96},{96,112},{112,128},... | collective-permute-start | bytes 196616 | tf_op jit(solution)/shard_map/ppermute | solution.py:322
  56.6 8.4 %collective-permute-start.1 = (bf16[16,1024]{1,0:T(8,128)(2,1)S(1)}, bf16[16,1024]{1,0:T(8,128)(2,1)S(1)}, u32[]{:S(2)}, u32[]{:S(2)}) collective-permute-start(bf16[16,1024]{1,0:T(8,128)(2,1)S(1)} %slice_bitcast_fusion.1), channel_id=1, source_target_pairs={{16,0},{32,16},{48,32},{64,48},{80,64},{96,80},{112,96},{128,112},... | collective-permute-start | bytes 98312 | tf_op jit(solution)/shard_map/ppermute | solution.py:323

commit v2 on v1

v2 whole, which is shorter than its diff:
```python
import jax
import jax.numpy as jnp
from jax import lax
from jax.experimental import pallas as pl
from jax.experimental.pallas import tpu as pltpu
from jax.sharding import PartitionSpec as P

HEADS = 16
DEPTH = 64
KERNEL = 31
LEFT = 64
EPSILON = 1e-05
FLOOR_SCORE = -1e30
BEFORE = 32
AFTER = 16
LANES = 128
PIECES = 4
QUERIES = 256
SHORTEST = 1024
F32 = jnp.float32
BF16 = jnp.bfloat16
SMEM_SPEC = pl.BlockSpec(memory_space=pltpu.SMEM)
VMEM_SPEC = pl.BlockSpec(memory_space=pltpu.VMEM)


def cost(flops, accessed):
    return pl.CostEstimate(flops=flops, bytes_accessed=accessed, transcendentals=0)


def norm_rows(values, gain):
    center = values - jnp.mean(values, axis=-1, keepdims=True)
    spread = jnp.mean(center * center, axis=-1, keepdims=True)
    return center * lax.rsqrt(spread + EPSILON) * gain


def low_lanes(rows):
    return lax.broadcasted_iota(jnp.int32, (rows, LANES), 1) < DEPTH


def half_turn(value):
    return pltpu.roll(value, DEPTH, 1)


def dot_rows(left, right):
    return lax.dot_general(left, right, (((1,), (1,)), ((), ())), preferred_element_type=F32)


def project_kernel(frames_hbm, gain_ref, wq_hbm, wk_hbm, wv_hbm, out_ref, frames_ref, w_ref, sem):
    rows, width = frames_ref.shape
    half = rows // 2
    deep = width // PIECES
    first = pltpu.make_async_copy(frames_hbm, frames_ref, sem.at[3 * PIECES])
    first.start()
    copies = []
    for index, hbm in enumerate((wk_hbm, wv_hbm, wq_hbm)):
        for piece in range(PIECES):
            span = slice(piece * deep, (piece + 1) * deep)
            copy = pltpu.make_async_copy(
                hbm.at[span], w_ref.at[index, span], sem.at[index * PIECES + piece]
            )
            copy.start()
            copies.append(copy)
    first.wait()
    normed = norm_rows(frames_ref[...].astype(F32), gain_ref[...]).astype(BF16)
    products = []
    for index in range(3):
        total = None
        for piece in range(PIECES):
            span = slice(piece * deep, (piece + 1) * deep)
            copies[index * PIECES + piece].wait()
            term = jnp.dot(normed[:, span], w_ref[index, span], preferred_element_type=F32)
            total = term if total is None else total + term
        products.append(total)
    key, value, query = products
    query = query * (DEPTH**-0.5)
    low = low_lanes(rows)
    low_half = low_lanes(half)
    for pair in range(HEADS // 2):
        cols = slice(pair * LANES, (pair + 1) * LANES)
        k, v, q = key[:, cols], value[:, cols], query[:, cols]
        kr, vr, qr = half_turn(k), half_turn(v), half_turn(q)
        out_ref[2 * pair, :rows] = jnp.where(low, k, vr).astype(BF16)
        out_ref[2 * pair + 1, :rows] = jnp.where(low, kr, v).astype(BF16)
        out_ref[2 * pair, rows:] = jnp.where(low_half, q[:half], qr[half:]).astype(BF16)
        out_ref[2 * pair + 1, rows:] = jnp.where(low_half, qr[:half], q[half:]).astype(BF16)


def project(frames, gain, wq, wk, wv):
    rows, width = frames.shape
    hbm = pl.BlockSpec(memory_space=pltpu.HBM)
    return pl.pallas_call(
        project_kernel,
        in_specs=[hbm, VMEM_SPEC, hbm, hbm, hbm],
        out_specs=VMEM_SPEC,
        out_shape=jax.ShapeDtypeStruct((HEADS, rows + rows // 2, LANES), BF16),
        scratch_shapes=[
            pltpu.VMEM((rows, width), BF16),
            pltpu.VMEM((3, width, width), BF16),
            pltpu.SemaphoreType.DMA((3 * PIECES + 1,)),
        ],
        compiler_params=pltpu.CompilerParams(vmem_limit_bytes=62 << 20),
        cost_estimate=cost(6 * rows * width * width, 6 * width * width),
        name="project",
    )(frames, gain, wq, wk, wv)


def row_softmax(scores):
    highest = jnp.max(scores, axis=-1, keepdims=True)
    expo = jnp.exp(scores - highest)
    return expo.astype(BF16), jnp.sum(expo, axis=-1, keepdims=True)


def attend_kernel(
    length_ref, stretch_ref, look_ref, packed_ref, out_ref,
    q_ref, bias_ref, s0_ref, s1_ref, full_ref, near_ref,
):
    blocks, packed_rows, _ = packed_ref.shape
    rows = packed_rows * 2 // 3
    half = rows // 2
    total = blocks * rows
    steps = total // QUERIES
    share = QUERIES // rows
    length = length_ref[0]
    length_f = length.astype(F32)
    stretch = stretch_ref[0].astype(F32)
    look = look_ref[0].astype(F32)
    low_half = low_lanes(half)
    for block in range(blocks):
        q = packed_ref[block, rows:].astype(F32)
        start = block * rows
        q_ref[start : start + half] = jnp.where(low_half, q, 0.0).astype(BF16)
        q_ref[start + half : start + rows] = jnp.where(low_half, half_turn(q), 0.0).astype(BF16)
    near_ref[:BEFORE] = jnp.zeros((BEFORE, LANES), BF16)
    full_ref[:AFTER] = jnp.zeros((AFTER, LANES), BF16)
    full_ref[AFTER + total :] = jnp.zeros((AFTER, LANES), BF16)
    key_pos = lax.broadcasted_iota(jnp.int32, (8, total), 1)
    bias_ref[...] = jnp.where(key_pos < length, 0.0, FLOOR_SCORE)
    row = lax.broadcasted_iota(jnp.int32, (rows, LANES), 0)
    lane = lax.broadcasted_iota(jnp.int32, (rows, LANES), 1)
    lane_f = lane.astype(F32)
    row_f = lax.broadcasted_iota(jnp.int32, (rows, 1), 0).astype(F32)

    def at(index):
        return pl.ds(pl.multiple_of(index * QUERIES, QUERIES), QUERIES)

    def keys(first, count):
        return jnp.concatenate([packed_ref[b, :rows] for b in range(first, first + count)], axis=0)

    def score(index, s_ref):
        q = q_ref[at(index)]
        always = SHORTEST // rows
        s_ref[:, :SHORTEST] = dot_rows(q, keys(0, always))
        s_ref[:, SHORTEST:] = dot_rows(q, keys(always, blocks - always)) + bias_ref[0:1, SHORTEST:]

    def own(index, s_ref):
        @pl.when((index + 1) * QUERIES > length)
        def _():
            for part in range(share):
                block = index * share + part
                start = pl.multiple_of(block * rows, rows)
                raw = dot_rows(q_ref[pl.ds(start, rows)], packed_ref[block, :rows])
                seen = (lane == row) | (lane + start < length)
                s_ref[part * rows : (part + 1) * rows, pl.ds(start, rows)] = jnp.where(
                    seen, raw, FLOOR_SCORE
                )

    def mix(index, s_ref):
        weights, totals = row_softmax(s_ref[...])
        mixed = jnp.dot(weights, keys(0, blocks), preferred_element_type=F32)
        full_ref[pl.ds(pl.multiple_of(index * QUERIES + AFTER, AFTER), QUERIES)] = half_turn(
            mixed / totals
        ).astype(BF16)

    def near(block):
        start = pl.multiple_of(block * rows, rows)
        base = (block * rows).astype(F32) if not isinstance(block, int) else float(block * rows)
        pos = row_f + base
        begin = jnp.floor((pos + 0.5) / stretch) * stretch
        first = jnp.broadcast_to(jnp.maximum(begin - LEFT, 0.0) - base, (rows, LANES))
        last = jnp.broadcast_to(jnp.minimum(begin + stretch + look, length_f) - base, (rows, LANES))
        around = (jnp.maximum(block - 1, 0), block, jnp.minimum(block + 1, blocks - 1))
        window = jnp.concatenate([packed_ref[b, :rows] for b in around], axis=0)
        raw = dot_rows(q_ref[pl.ds(start, rows)], window)
        parts = []
        for part in range(3):
            key_at = lane_f + float((part - 1) * rows)
            inside = (key_at >= first) & (key_at < last)
            if part == 1:
                inside = inside | (lane == row)
            parts.append(jnp.where(inside, raw[:, part * rows : (part + 1) * rows], FLOOR_SCORE))
        weights, totals = row_softmax(jnp.concatenate(parts, axis=1))
        mixed = jnp.dot(weights, window, preferred_element_type=F32)
        near_ref[pl.ds(pl.multiple_of(start + BEFORE, BEFORE), rows)] = (mixed / totals).astype(
            BF16
        )

    def nears(index):
        for part in range(share):
            near(index * share + part)

    score(0, s0_ref)
    own(0, s0_ref)

    def body(step, carry):
        score(2 * step + 1, s1_ref)
        mix(2 * step, s0_ref)
        nears(2 * step)
        own(2 * step + 1, s1_ref)
        score(2 * step + 2, s0_ref)
        mix(2 * step + 1, s1_ref)
        nears(2 * step + 1)
        own(2 * step + 2, s0_ref)
        return carry

    lax.fori_loop(0, steps // 2 - 1, body, 0)
    score(steps - 1, s1_ref)
    mix(steps - 2, s0_ref)
    nears(jnp.int32(steps - 2))
    own(steps - 1, s1_ref)
    mix(steps - 1, s1_ref)
    nears(jnp.int32(steps - 1))
    ext = BEFORE + rows
    low = low_lanes(ext)
    for block in range(blocks):
        span = slice(block * rows, block * rows + ext)
        out_ref[block] = jnp.where(
            low, full_ref[span].astype(F32), near_ref[span].astype(F32)
        ).astype(BF16)


def attend(length, stretch, look, packed):
    blocks, packed_rows, _ = packed.shape
    rows = packed_rows * 2 // 3
    total = blocks * rows
    return pl.pallas_call(
        attend_kernel,
        in_specs=[SMEM_SPEC] * 3 + [VMEM_SPEC],
        out_specs=VMEM_SPEC,
        out_shape=jax.ShapeDtypeStruct((blocks, BEFORE + rows, LANES), BF16),
        scratch_shapes=[
            pltpu.VMEM((total, LANES), BF16),
            pltpu.VMEM((8, total), F32),
            pltpu.VMEM((QUERIES, total), F32),
            pltpu.VMEM((QUERIES, total), F32),
            pltpu.VMEM((total + 2 * AFTER, LANES), BF16),
            pltpu.VMEM((BEFORE + total, LANES), BF16),
        ],
        compiler_params=pltpu.CompilerParams(vmem_limit_bytes=32 << 20),
        cost_estimate=cost(4 * total * (total + 3 * rows) * LANES, 2 << 20),
        name="attend",
    )(length, stretch, look, packed)


def turns(first):
    for turn in range(8):
        offsets = [k for k in range(KERNEL) if (first + k) % 8 == turn]
        yield offsets, first + offsets[0], offsets[-1] - offsets[0]


def convolve(x_ref, taps_ref, first, rows, cols):
    total = jnp.zeros((rows, LANES), F32)
    for offsets, low_at, extra in turns(first):
        piece = x_ref[low_at : low_at + extra + rows, cols]
        for k in offsets:
            skip = k - offsets[0]
            total = total + taps_ref[k : k + 1, cols] * piece[skip : skip + rows]
    return total


def finish_kernel(
    place_ref, length_ref, ctx_ref, before_ref, frames_ref, after_ref, wo_ref, gain_ref, taps_ref,
    full_ref, near_ref, grad_ref, c_ref, res_ref, x_ref,
):
    rows, width = frames_ref.shape
    ext = BEFORE + rows
    length = length_ref[0]
    start = place_ref[0] * rows
    low = low_lanes(ext)
    for pair in range(HEADS // 2):
        cols = slice(pair * LANES, (pair + 1) * LANES)
        one, two = ctx_ref[2 * pair].astype(F32), ctx_ref[2 * pair + 1].astype(F32)
        c_ref[:ext, cols] = jnp.where(low, one, half_turn(two)).astype(BF16)
        c_ref[ext:, cols] = jnp.where(low, half_turn(one), two).astype(BF16)
    frames = frames_ref[...]
    source = jnp.concatenate(
        [before_ref[BEFORE - AFTER :], frames, after_ref[...], before_ref[...], frames], axis=0
    ).astype(F32)
    residual = source + jnp.dot(c_ref[...], wo_ref[...], preferred_element_type=F32)
    res_ref[...] = residual
    normed = norm_rows(residual, gain_ref[...])
    line = lax.broadcasted_iota(jnp.int32, (2 * ext, 1), 0)
    pos = start + jnp.where(line < ext, line - AFTER, line - ext - BEFORE)
    valid = (pos >= 0) & (pos < length)
    x_ref[...] = jnp.where(valid, normed, 0.0).astype(BF16).astype(F32)
    inner = lax.broadcasted_iota(jnp.int32, (rows, 1), 0) + start
    factor = jnp.where(inner < length, 2.0 / jnp.sqrt(jnp.full((rows, 1), length.astype(F32))), 0.0)
    near_first = ext + BEFORE - (KERNEL - 1)

    def column(step, carry):
        cols = pl.ds(pl.multiple_of(step * LANES, LANES), LANES)
        conv = convolve(x_ref, taps_ref, AFTER - KERNEL // 2, rows, cols)
        out_full = res_ref[AFTER : AFTER + rows, cols] + conv / (1.0 + jnp.exp(-conv))
        full_ref[:, cols] = out_full.astype(BF16)
        conv = convolve(x_ref, taps_ref, near_first, rows, cols)
        sigma = 1.0 / (1.0 + jnp.exp(-conv))
        out_near = res_ref[ext + BEFORE :, cols] + conv * sigma
        near_ref[:, cols] = out_near.astype(BF16)
        slope = (out_near - out_full) * factor * (sigma * (1.0 + conv * (1.0 - sigma)))
        for offsets, low_at, extra in turns(near_first):
            piece = x_ref[low_at : low_at + extra + rows, cols]
            for k in offsets:
                skip = k - offsets[0]
                term = jnp.sum(slope * piece[skip : skip + rows], axis=0, keepdims=True)
                grad_ref[2 * step + k // 16, k % 16 : k % 16 + 1] = term
        grad_ref[2 * step + 1, 15:16] = jnp.zeros((1, LANES), F32)
        return carry

    lax.fori_loop(0, width // LANES, column, 0)


def finish(place, length, ctx, before, frames, after, wo, gain, taps):
    rows, width = frames.shape
    ext = BEFORE + rows
    return pl.pallas_call(
        finish_kernel,
        in_specs=[SMEM_SPEC] * 2 + [VMEM_SPEC] * 7,
        out_specs=[VMEM_SPEC] * 3,
        out_shape=[
            jax.ShapeDtypeStruct((rows, width), BF16),
            jax.ShapeDtypeStruct((rows, width), BF16),
            jax.ShapeDtypeStruct((width // 64, 16, LANES), F32),
        ],
        scratch_shapes=[
            pltpu.VMEM((2 * ext, width), BF16),
            pltpu.VMEM((2 * ext, width), F32),
            pltpu.VMEM((2 * ext, width), F32),
        ],
        compiler_params=pltpu.CompilerParams(vmem_limit_bytes=40 << 20),
        cost_estimate=cost(4 * ext * width * width, 6 << 20),
        name="finish",
    )(place, length, ctx, before, frames, after, wo, gain, taps)


def swap(value, axis):
    return lax.all_to_all(value, axis, 0, 0, tiled=True)


def spread_out(value, axis):
    size = lax.axis_size(axis)
    return swap(jnp.broadcast_to(value[None], (size,) + value.shape), axis)


def per_device(
    frames,
    lengths,
    stretch_sizes,
    look_ahead,
    norm_one,
    norm_two,
    w_query,
    w_key,
    w_value,
    w_out,
    conv_kernel,
):
    source = frames[0]
    rows, width = source.shape
    size = lax.axis_size("seq")
    place = lax.axis_index("seq").reshape(1).astype(jnp.int32)
    up = [(i, i + 1) for i in range(size - 1)]
    down = [(j, i) for i, j in up]
    before = lax.ppermute(source[rows - BEFORE :], "seq", up)
    after = lax.ppermute(source[:AFTER], "seq", down)
    taps = jnp.pad(conv_kernel.astype(F32), ((0, 1), (0, 0)))
    packed = project(source, norm_one[None], w_query, w_key, w_value)
    packed = swap(packed, "seq")
    packed, before, after = lax.optimization_barrier((packed, before, after))
    gain = norm_two[None]
    ctx = swap(attend(lengths, stretch_sizes, look_ahead, packed), "seq")
    full, near, grad = finish(place, lengths, ctx, before, source, after, w_out, gain, taps)
    piece = jnp.sum(swap(grad, "seq"), axis=0)
    piece = jnp.sum(spread_out(piece, "dp"), axis=0)
    grads = spread_out(piece, "seq")
    grads = grads.reshape(width // LANES, 32, LANES).transpose(1, 0, 2).reshape(32, width)
    return full[None], near[None], grads[:KERNEL]


def solution(mesh):
    in_specs = (P("dp", "seq", None), P("dp"), P("dp"), P("dp"), P(), P(), P(), P(), P(), P(), P())
    out_specs = (P("dp", "seq", None), P("dp", "seq", None), P())
    return jax.shard_map(
        per_device, mesh=mesh, in_specs=in_specs, out_specs=out_specs, check_vma=False
    )
```

time: 117 us -> 111 us (0.949)
  local copies, waits for them, and re-layouts: 7.22 us -> 3.67 us
  Pallas kernels: 26.1 us -> 24.8 us
    unnamed x20 -> x16, local copies, waits for them, and re-layouts: 7.11 us -> 3.56 us
    pallas_call x3, Pallas kernels: 26.1 us -> 24.8 us  [the longest x1 11 us: attend(): pl.pallas_call(attend_kernel, in_specs=[SMEM_SPEC] * 3 + [VMEM_SPEC], out...]
where the time goes in v2:
time: 111 us
  blocking collectives  41.8 us (38%)
  Pallas kernels  24.8 us (22%)
  starting transfers between devices  19.7 us (18%)
  waiting for transfers between devices  17.8 us (16%)
  local copies, waits for them, and re-layouts  3.67 us (3%)
  between operations  2.7 us (2%)
    all_to_all x3, blocking collectives, swap(): return lax.all_to_all(value, axis, 0, 0, tiled=True)  41.8 us
    all_to_all x2, starting transfers between devices, swap(): return lax.all_to_all(value, axis, 0, 0, tiled=True)  12.8 us
    all_to_all x2, waiting for transfers between devices, swap(): return lax.all_to_all(value, axis, 0, 0, tiled=True)  12.4 us
    pallas_call x1, Pallas kernels, attend(): pl.pallas_call(attend_kernel, in_specs=[SMEM_SPEC] * 3 + [VMEM_SPEC], out...  11 us
    pallas_call x1, Pallas kernels, finish(): pl.pallas_call(finish_kernel, in_specs=[SMEM_SPEC] * 2 + [VMEM_SPEC] * 7,...  8.9 us
    ppermute x1, waiting for transfers between devices, per_device(): after = lax.ppermute(source[:AFTER], 'seq', down)  5.37 us
    ppermute x1, starting transfers between devices, per_device(): before = lax.ppermute(source[rows - BEFORE:], 'seq', up)  5.04 us
    pallas_call x1, Pallas kernels, project(): pl.pallas_call(project_kernel, in_specs=[hbm, VMEM_SPEC, hbm, hbm, hbm],...  4.91 us
  transfers between devices with their start and end apart: 4, of which 2 were waited for; matrix products, arithmetic and copies ran while one was open for 0% of the time, Pallas kernels for 0%

profile of v2, /device:TPU:1, one launch (start us, length us, event | category | flops | bytes accessed | tf_op | source)
XLA Modules:
  0.0 110.6 jit_solution(9114154238484563628)
XLA Ops:
  0.6 0.0 copy-start.1
  0.6 4.9 %project.1 = bf16[16,192,128]{2,1,0:T(8,128)(2,1)} custom-call(bf16[128,1024]{1,0:T(8,128)(2,1)} %bitcast.17, f32[1,1024]{1,0:T(1,128)} %bitcast.23, bf16[1024,1024]{1,0:T(8,128)(2,1)} %wq_hbm.1, bf16[1024,1024]{1,0:T(8,128)(2,1)} %wk_hbm.1, bf16[1024,1024]{1,0:T(8,128)(2,1)} %wv_hbm.1), custom_call_target="tpu_custom_call" | custom-call | flops 805306368 | bytes 6291456 | tf_op jit(solution)/shard_map/project/pallas_call | solution.py:91
  5.6 8.5 %all-to-all-start = ((bf16[16,192,128]{2,1,0:T(8,128)(2,1)}), bf16[16,192,128]{2,1,0:T(8,128)(2,1)S(1)}, u32[]{:S(2)}, u32[]{:S(2)}) async-start(bf16[16,192,128]{2,1,0:T(8,128)(2,1)} %project.1), calls=%async_computation | async-start | bytes 1572864 | tf_op jit(solution)/shard_map/all_to_all | solution.py:345
  14.0 0.0 copy-done.1
  14.0 5.0 %collective-permute-start = (bf16[32,1024]{1,0:T(8,128)(2,1)S(1)}, bf16[32,1024]{1,0:T(8,128)(2,1)S(1)}, u32[]{:S(2)}, u32[]{:S(2)}) collective-permute-start(bf16[32,1024]{1,0:T(8,128)(2,1)S(1)} %slice_bitcast_fusion), channel_id=1, source_target_pairs={{0,16},{16,32},{32,48},{48,64},{64,80},{80,96},{96,112},{112,128},... | collective-permute-start | bytes 196616 | tf_op jit(solution)/shard_map/ppermute | solution.py:372
  19.1 1.9 %collective-permute-start.1 = (bf16[16,1024]{1,0:T(8,128)(2,1)S(1)}, bf16[16,1024]{1,0:T(8,128)(2,1)S(1)}, u32[]{:S(2)}, u32[]{:S(2)}) collective-permute-start(bf16[16,1024]{1,0:T(8,128)(2,1)S(1)} %slice_bitcast_fusion.1), channel_id=1, source_target_pairs={{16,0},{32,16},{48,32},{64,48},{80,64},{96,80},{112,96},{128,112},... | collective-permute-start | bytes 98312 | tf_op jit(solution)/shard_map/ppermute | solution.py:373
  23.0 5.4 %collective-permute-done.1.after_ref = bf16[16,1024]{1,0:T(8,128)(2,1)S(1)} collective-permute-done((bf16[16,1024]{1,0:T(8,128)(2,1)S(1)}, bf16[16,1024]{1,0:T(8,128)(2,1)S(1)}, u32[]{:S(2)}, u32[]{:S(2)}) %collective-permute-start.1) | collective-permute-done | bytes 32800 | tf_op jit(solution)/shard_map/ppermute | solution.py:373
  28.3 0.0 collective-permute-done.before_ref
  28.3 0.0 all-to-all-done.packed_ref
  28.4 0.9 copy-done.2
  29.2 1.1 %copy-done.3 = bf16[16,192,128]{2,1,0:T(8,128)(2,1)S(1)} copy-done((bf16[16,192,128]{2,1,0:T(8,128)(2,1)S(1)}, bf16[16,192,128]{2,1,0:T(8,128)(2,1)}, u32[]{:S(2)}) %copy-start.3) | copy-done | bytes 786456
  30.4 11.0 %attend.1 = bf16[16,160,128]{2,1,0:T(8,128)(2,1)S(1)} custom-call(s32[1]{0:T(128)S(6)} %copy.17.length_ref, s32[1]{0:T(128)S(6)} %copy.18.stretch_ref, s32[1]{0:T(128)S(6)} %copy.19.look_ref, bf16[16,192,128]{2,1,0:T(8,128)(2,1)S(1)} %copy-done.3), custom_call_target="tpu_custom_call" | custom-call | flops 2550136832 | bytes 2097152 | tf_op jit(solution)/shard_map/attend/pallas_call | solution.py:235
  41.4 0.0 copy-start.4
  41.4 0.8 copy-done.4
  42.3 4.3 %all-to-all-start.1 = ((bf16[16,160,128]{2,1,0:T(8,128)(2,1)}), bf16[16,160,128]{2,1,0:T(8,128)(2,1)S(1)}, u32[]{:S(2)}, u32[]{:S(2)}) async-start(bf16[16,160,128]{2,1,0:T(8,128)(2,1)} %copy-done.4), calls=%async_computation.1 | async-start | bytes 1310720 | tf_op jit(solution)/shard_map/all_to_all | solution.py:345
  46.6 0.0 copy-done.6
  46.6 12.4 %all-to-all-done.1.ctx_ref = bf16[16,160,128]{2,1,0:T(8,128)(2,1)S(1)} async-done(((bf16[16,160,128]{2,1,0:T(8,128)(2,1)}), bf16[16,160,128]{2,1,0:T(8,128)(2,1)S(1)}, u32[]{:S(2)}, u32[]{:S(2)}) %all-to-all-start.1) | async-done | bytes 655392 | tf_op jit(solution)/shard_map/all_to_all | solution.py:345
  59.0 0.0 copy-done.5
  59.0 8.9 %finish.1 = (bf16[128,1024]{1,0:T(8,128)(2,1)}, bf16[128,1024]{1,0:T(8,128)(2,1)}, f32[16,16,128]{2,1,0:T(8,128)S(1)}) custom-call(s32[1]{0:T(128)} %bitcast.place_ref, s32[1]{0:T(128)S(6)} %copy.17.length_ref, bf16[16,160,128]{2,1,0:T(8,128)(2,1)S(1)} %all-to-all-done.1.ctx_ref, bf16[32,1024]{1,0:T(8,128)(2,1)S(1)} %collective-permute-done.before_ref, ...), custom_call_target="tpu_custom_call" | custom-call | flops 671088640 | bytes 6291456 | tf_op jit(solution)/shard_map/finish/pallas_call | solution.py:324
  67.9 11.6 %all_to_all.25 = f32[16,16,128]{2,1,0:T(8,128)S(1)} all-to-all(f32[16,16,128]{2,1,0:T(8,128)S(1)} %get-tuple-element.14), channel_id=1, replica_groups=mesh['seq'=16,'dp'=16] {'seq'}, dimensions={0} | all-to-all | bytes 262144 | tf_op jit(solution)/shard_map/all_to_all | solution.py:345
  79.6 17.4 %all_to_all.26 = f32[16,16,128]{2,1,0:T(8,128)S(1)} all-to-all(f32[16,16,128]{2,1,0:T(8,128)S(1)} %broadcast_in_dim.28), channel_id=1, replica_groups=mesh['seq'=16,'dp'=16] {'dp'}, dimensions={0} | all-to-all | bytes 262144 | tf_op jit(solution)/shard_map/all_to_all | solution.py:345
  97.0 12.8 %all_to_all.27 = f32[16,16,128]{2,1,0:T(8,128)S(1)} all-to-all(f32[16,16,128]{2,1,0:T(8,128)S(1)} %broadcast_in_dim.29), channel_id=1, replica_groups=mesh['seq'=16,'dp'=16] {'seq'}, dimensions={0} | all-to-all | bytes 262144 | tf_op jit(solution)/shard_map/all_to_all | solution.py:345
  109.9 0.1 copy.15
  110.0 0.7 copy.16
  (14 shorter events, 0.1 us)
Async XLA Ops:
  0.6 13.4 %copy-start.1 = (bf16[1,128,1024]{2,1,0:T(8,128)(2,1)S(1)}, bf16[1,128,1024]{2,1,0:T(8,128)(2,1)}, u32[]{:S(2)}) copy-start(bf16[1,128,1024]{2,1,0:T(8,128)(2,1)} %param.11) | copy-start | bytes 786436
  5.6 22.8 %all-to-all-start = ((bf16[16,192,128]{2,1,0:T(8,128)(2,1)}), bf16[16,192,128]{2,1,0:T(8,128)(2,1)S(1)}, u32[]{:S(2)}, u32[]{:S(2)}) async-start(bf16[16,192,128]{2,1,0:T(8,128)(2,1)} %project.1), calls=%async_computation | async-start | bytes 1572864 | tf_op jit(solution)/shard_map/all_to_all | solution.py:345
  14.0 14.3 %collective-permute-start = (bf16[32,1024]{1,0:T(8,128)(2,1)S(1)}, bf16[32,1024]{1,0:T(8,128)(2,1)S(1)}, u32[]{:S(2)}, u32[]{:S(2)}) collective-permute-start(bf16[32,1024]{1,0:T(8,128)(2,1)S(1)} %slice_bitcast_fusion), channel_id=1, source_target_pairs={{0,16},{16,32},{32,48},{48,64},{64,80},{80,96},{96,112},{112,128},... | collective-permute-start | bytes 196616 | tf_op jit(solution)/shard_map/ppermute | solution.py:372
  19.1 9.2 %collective-permute-start.1 = (bf16[16,1024]{1,0:T(8,128)(2,1)S(1)}, bf16[16,1024]{1,0:T(8,128)(2,1)S(1)}, u32[]{:S(2)}, u32[]{:S(2)}) collective-permute-start(bf16[16,1024]{1,0:T(8,128)(2,1)S(1)} %slice_bitcast_fusion.1), channel_id=1, source_target_pairs={{16,0},{32,16},{48,32},{64,48},{80,64},{96,80},{112,96},{128,112},... | collective-permute-start | bytes 98312 | tf_op jit(solution)/shard_map/ppermute | solution.py:373
  28.4 0.9 copy-start.2
  29.2 1.1 %copy-start.3 = (bf16[16,192,128]{2,1,0:T(8,128)(2,1)S(1)}, bf16[16,192,128]{2,1,0:T(8,128)(2,1)}, u32[]{:S(2)}) copy-start(bf16[16,192,128]{2,1,0:T(8,128)(2,1)} %copy-done.2) | copy-start | bytes 2359300
  30.4 16.2 %copy-start.6 = (bf16[31,1024]{1,0:T(8,128)(2,1)S(1)}, bf16[31,1024]{1,0:T(8,128)(2,1)}, u32[]{:S(2)}) copy-start(bf16[31,1024]{1,0:T(8,128)(2,1)} %param.21) | copy-start | bytes 190468
  30.4 28.6 %copy-start = (bf16[1024,1024]{1,0:T(8,128)(2,1)S(1)}, bf16[1024,1024]{1,0:T(8,128)(2,1)}, u32[]{:S(2)}) copy-start(bf16[1024,1024]{1,0:T(8,128)(2,1)} %wo_ref.1) | copy-start | bytes 6291460
  30.4 28.6 %copy-start.5 = (f32[1024]{0:T(1024)S(1)}, f32[1024]{0:T(1024)}, u32[]{:S(2)}) copy-start(f32[1024]{0:T(1024)} %param.16) | copy-start | bytes 12292
  41.4 0.8 copy-start.4
  42.3 16.8 %all-to-all-start.1 = ((bf16[16,160,128]{2,1,0:T(8,128)(2,1)}), bf16[16,160,128]{2,1,0:T(8,128)(2,1)S(1)}, u32[]{:S(2)}, u32[]{:S(2)}) async-start(bf16[16,160,128]{2,1,0:T(8,128)(2,1)} %copy-done.4), calls=%async_computation.1 | async-start | bytes 1310720 | tf_op jit(solution)/shard_map/all_to_all | solution.py:345

commit v3 on v2

--- a/solution.py
+++ b/solution.py
@@ -14,8 +14,10 @@
 BEFORE = 32
 AFTER = 16
 LANES = 128
+TILE = 8
+STRIDE = 16
 PIECES = 4
-QUERIES = 256
+QUERIES = 512
 SHORTEST = 1024
 F32 = jnp.float32
 BF16 = jnp.bfloat16
@@ -99,7 +101,6 @@
             pltpu.SemaphoreType.DMA((3 * PIECES + 1,)),
         ],
         compiler_params=pltpu.CompilerParams(vmem_limit_bytes=62 << 20),
-        cost_estimate=cost(6 * rows * width * width, 6 * width * width),
         name="project",
     )(frames, gain, wq, wk, wv)
 
@@ -111,7 +112,7 @@
 
 
 def attend_kernel(
-    length_ref, stretch_ref, look_ref, packed_ref, out_ref,
+    length_ref, stretch_ref, look_ref, packed_ref, before_ref, after_ref, out_ref,
     q_ref, bias_ref, s0_ref, s1_ref, full_ref, near_ref,
 ):
     blocks, packed_rows, _ = packed_ref.shape
@@ -228,13 +229,13 @@
         ).astype(BF16)
 
 
-def attend(length, stretch, look, packed):
+def attend(length, stretch, look, packed, before, after):
     blocks, packed_rows, _ = packed.shape
     rows = packed_rows * 2 // 3
     total = blocks * rows
     return pl.pallas_call(
         attend_kernel,
-        in_specs=[SMEM_SPEC] * 3 + [VMEM_SPEC],
+        in_specs=[SMEM_SPEC] * 3 + [VMEM_SPEC] + [pl.BlockSpec(memory_space=pl.ANY)] * 2,
         out_specs=VMEM_SPEC,
         out_shape=jax.ShapeDtypeStruct((blocks, BEFORE + rows, LANES), BF16),
         scratch_shapes=[
@@ -246,30 +247,32 @@
             pltpu.VMEM((BEFORE + total, LANES), BF16),
         ],
         compiler_params=pltpu.CompilerParams(vmem_limit_bytes=32 << 20),
-        cost_estimate=cost(4 * total * (total + 3 * rows) * LANES, 2 << 20),
         name="attend",
-    )(length, stretch, look, packed)
-
-
-def turns(first):
-    for turn in range(8):
-        offsets = [k for k in range(KERNEL) if (first + k) % 8 == turn]
-        yield offsets, first + offsets[0], offsets[-1] - offsets[0]
-
-
-def convolve(x_ref, taps_ref, first, rows, cols):
-    total = jnp.zeros((rows, LANES), F32)
-    for offsets, low_at, extra in turns(first):
-        piece = x_ref[low_at : low_at + extra + rows, cols]
-        for k in offsets:
-            skip = k - offsets[0]
-            total = total + taps_ref[k : k + 1, cols] * piece[skip : skip + rows]
-    return total
+    )(length, stretch, look, packed, before, after)
+
+
+def frame_tile(ref, index):
+    return ref[pl.ds(pl.multiple_of(index * TILE, TILE), TILE), :]
+
+
+def cells(first, tile):
+    return pl.ds(first * TILE + tile, TILE, stride=TILE)
+
+
+def convolve(x_ref, taps, first):
+    totals = [None] * STRIDE
+    for step in range(STRIDE + KERNEL - 1):
+        x = frame_tile(x_ref, first + step)
+        for row in range(max(0, step - KERNEL + 1), min(STRIDE, step + 1)):
+            term = taps[step - row] * x
+            totals[row] = term if totals[row] is None else totals[row] + term
+    return totals
 
 
 def finish_kernel(
     place_ref, length_ref, ctx_ref, before_ref, frames_ref, after_ref, wo_ref, gain_ref, taps_ref,
-    full_ref, near_ref, grad_ref, c_ref, res_ref, x_ref,
+    full_ref, near_ref, grad_ref,
+    c_ref, res_ref, xf_ref, xn_ref, cf_ref, cn_ref, slope_ref, sums_ref,
 ):
     rows, width = frames_ref.shape
     ext = BEFORE + rows
@@ -291,31 +294,60 @@
     line = lax.broadcasted_iota(jnp.int32, (2 * ext, 1), 0)
     pos = start + jnp.where(line < ext, line - AFTER, line - ext - BEFORE)
     valid = (pos >= 0) & (pos < length)
-    x_ref[...] = jnp.where(valid, normed, 0.0).astype(BF16).astype(F32)
+    x = jnp.where(valid, normed, 0.0).astype(BF16).astype(F32)
+    for x_ref, at in ((xf_ref, 0), (xn_ref, ext)):
+        for first in range(0, ext, TILE):
+            for tile in range(width // LANES):
+                x_ref[cells(first, tile), :] = x[
+                    at + first : at + first + TILE, tile * LANES : (tile + 1) * LANES
+                ]
+    full_first = AFTER - KERNEL // 2
+    near_first = BEFORE - (KERNEL - 1)
+
+    def conv_rows(step, carry):
+        taps = [frame_tile(taps_ref, k) for k in range(KERNEL)]
+        at = step * STRIDE
+        for x_ref, first, out_ref in ((xf_ref, full_first, cf_ref), (xn_ref, near_first, cn_ref)):
+            for row, value in enumerate(convolve(x_ref, taps, at + first)):
+                out_ref[pl.ds(pl.multiple_of((at + row) * TILE, TILE), TILE), :] = value
+        return carry
+
+    lax.fori_loop(0, rows // STRIDE, conv_rows, 0)
     inner = lax.broadcasted_iota(jnp.int32, (rows, 1), 0) + start
     factor = jnp.where(inner < length, 2.0 / jnp.sqrt(jnp.full((rows, 1), length.astype(F32))), 0.0)
-    near_first = ext + BEFORE - (KERNEL - 1)
-
-    def column(step, carry):
-        cols = pl.ds(pl.multiple_of(step * LANES, LANES), LANES)
-        conv = convolve(x_ref, taps_ref, AFTER - KERNEL // 2, rows, cols)
+    for tile in range(width // LANES):
+        cols = slice(tile * LANES, (tile + 1) * LANES)
+        groups = range(0, rows, TILE)
+        conv = jnp.concatenate([cf_ref[cells(g, tile), :] for g in groups], axis=0)
         out_full = res_ref[AFTER : AFTER + rows, cols] + conv / (1.0 + jnp.exp(-conv))
         full_ref[:, cols] = out_full.astype(BF16)
-        conv = convolve(x_ref, taps_ref, near_first, rows, cols)
+        conv = jnp.concatenate([cn_ref[cells(g, tile), :] for g in groups], axis=0)
         sigma = 1.0 / (1.0 + jnp.exp(-conv))
         out_near = res_ref[ext + BEFORE :, cols] + conv * sigma
         near_ref[:, cols] = out_near.astype(BF16)
         slope = (out_near - out_full) * factor * (sigma * (1.0 + conv * (1.0 - sigma)))
-        for offsets, low_at, extra in turns(near_first):
-            piece = x_ref[low_at : low_at + extra + rows, cols]
-            for k in offsets:
-                skip = k - offsets[0]
-                term = jnp.sum(slope * piece[skip : skip + rows], axis=0, keepdims=True)
-                grad_ref[2 * step + k // 16, k % 16 : k % 16 + 1] = term
-        grad_ref[2 * step + 1, 15:16] = jnp.zeros((1, LANES), F32)
-        return carry
-
-    lax.fori_loop(0, width // LANES, column, 0)
+        for g in groups:
+            slope_ref[cells(g, tile), :] = slope[g : g + TILE]
+
+    def grad_rows(step, sums):
+        sums = list(sums)
+        at = step * STRIDE
+        slopes = [frame_tile(slope_ref, at + row) for row in range(STRIDE)]
+        for move in range(STRIDE + KERNEL - 1):
+            x = frame_tile(xn_ref, at + near_first + move)
+            for row in range(max(0, move - KERNEL + 1), min(STRIDE, move + 1)):
+                sums[move - row] = sums[move - row] + slopes[row] * x
+        return tuple(sums)
+
+    zero = jnp.zeros((TILE, LANES), F32)
+    sums = lax.fori_loop(0, rows // STRIDE, grad_rows, (zero,) * KERNEL)
+    for k, value in enumerate(sums + (zero,)):
+        sums_ref[k * TILE : (k + 1) * TILE] = value
+    for tile in range(width // LANES):
+        for group in range(4):
+            grad_ref[2 * tile + group // 2, group % 2 * TILE : group % 2 * TILE + TILE] = sums_ref[
+                cells(group * TILE, tile), :
+            ]
 
 
 def finish(place, length, ctx, before, frames, after, wo, gain, taps):
@@ -333,10 +365,14 @@
         scratch_shapes=[
             pltpu.VMEM((2 * ext, width), BF16),
             pltpu.VMEM((2 * ext, width), F32),
-            pltpu.VMEM((2 * ext, width), F32),
+            pltpu.VMEM((ext * TILE, LANES), F32),
+            pltpu.VMEM((ext * TILE, LANES), F32),
+            pltpu.VMEM((rows * TILE, LANES), F32),
+            pltpu.VMEM((rows * TILE, LANES), F32),
+            pltpu.VMEM((rows * TILE, LANES), F32),
+            pltpu.VMEM((32 * TILE, LANES), F32),
         ],
         compiler_params=pltpu.CompilerParams(vmem_limit_bytes=40 << 20),
-        cost_estimate=cost(4 * ext * width * width, 6 << 20),
         name="finish",
     )(place, length, ctx, before, frames, after, wo, gain, taps)
 
@@ -371,12 +407,11 @@
     down = [(j, i) for i, j in up]
     before = lax.ppermute(source[rows - BEFORE :], "seq", up)
     after = lax.ppermute(source[:AFTER], "seq", down)
-    taps = jnp.pad(conv_kernel.astype(F32), ((0, 1), (0, 0)))
+    taps = conv_kernel.astype(F32).reshape(KERNEL * TILE, LANES)
     packed = project(source, norm_one[None], w_query, w_key, w_value)
     packed = swap(packed, "seq")
-    packed, before, after = lax.optimization_barrier((packed, before, after))
     gain = norm_two[None]
-    ctx = swap(attend(lengths, stretch_sizes, look_ahead, packed), "seq")
+    ctx = swap(attend(lengths, stretch_sizes, look_ahead, packed, before, after), "seq")
     full, near, grad = finish(place, lengths, ctx, before, source, after, w_out, gain, taps)
     piece = jnp.sum(swap(grad, "seq"), axis=0)
     piece = jnp.sum(spread_out(piece, "dp"), axis=0)

time: 111 us -> 105 us (0.946)
  local copies, waits for them, and re-layouts: 3.67 us -> 0.89 us
  Pallas kernels: 24.8 us -> 22.3 us
    pallas_call x1, Pallas kernels: 8.9 us -> 6.04 us  [finish(): pl.pallas_call(finish_kernel, in_specs=[SMEM_SPEC] * 2 + [VMEM_SPEC] * 7,...]
    unnamed x16 -> x10, local copies, waits for them, and re-layouts: 3.56 us -> 0.71 us
where the time goes in v3:
time: 105 us
  blocking collectives  41.3 us (39%)
  Pallas kernels  22.3 us (21%)
  starting transfers between devices  19.9 us (19%)
  waiting for transfers between devices  17.7 us (17%)
  between operations  2.7 us (3%)
    all_to_all x3, blocking collectives, swap(): return lax.all_to_all(value, axis, 0, 0, tiled=True)  41.3 us
    all_to_all x2, starting transfers between devices, swap(): return lax.all_to_all(value, axis, 0, 0, tiled=True)  12.9 us
    all_to_all x2, waiting for transfers between devices, swap(): return lax.all_to_all(value, axis, 0, 0, tiled=True)  12.4 us
    pallas_call x1, Pallas kernels, attend(): pl.pallas_call(attend_kernel, in_specs=[SMEM_SPEC] * 3 + [VMEM_SPEC] + [p...  11.3 us
    pallas_call x1, Pallas kernels, finish(): pl.pallas_call(finish_kernel, in_specs=[SMEM_SPEC] * 2 + [VMEM_SPEC] * 7,...  6.04 us
    ppermute x1, waiting for transfers between devices, per_device(): after = lax.ppermute(source[:AFTER], 'seq', down)  5.37 us
    ppermute x1, starting transfers between devices, per_device(): before = lax.ppermute(source[rows - BEFORE:], 'seq', up)  5.04 us
    pallas_call x1, Pallas kernels, project(): pl.pallas_call(project_kernel, in_specs=[hbm, VMEM_SPEC, hbm, hbm, hbm],...  4.92 us
  transfers between devices with their start and end apart: 4, of which 2 were waited for; matrix products, arithmetic and copies ran while one was open for 0% of the time, Pallas kernels for 0%

profile of v3, /device:TPU:1, one launch (start us, length us, event | category | flops | bytes accessed | tf_op | source)
XLA Modules:
  0.0 104.9 jit_solution(7900681794000303476)
XLA Ops:
  0.6 0.0 copy-start.1
  0.6 4.9 %project.1 = bf16[16,192,128]{2,1,0:T(8,128)(2,1)} custom-call(bf16[128,1024]{1,0:T(8,128)(2,1)} %bitcast.17, f32[1,1024]{1,0:T(1,128)} %bitcast.23, bf16[1024,1024]{1,0:T(8,128)(2,1)} %wq_hbm.1, bf16[1024,1024]{1,0:T(8,128)(2,1)} %wk_hbm.1, bf16[1024,1024]{1,0:T(8,128)(2,1)} %wv_hbm.1), custom_call_target="tpu_custom_call" | custom-call | tf_op jit(solution)/shard_map/project/pallas_call | solution.py:93
  5.6 0.0 copy-start.3
  5.6 0.0 copy-start
  5.6 0.0 copy-start.2
  5.6 8.6 %all-to-all-start = ((bf16[16,192,128]{2,1,0:T(8,128)(2,1)}), bf16[16,192,128]{2,1,0:T(8,128)(2,1)S(1)}, u32[]{:S(2)}, u32[]{:S(2)}) async-start(bf16[16,192,128]{2,1,0:T(8,128)(2,1)} %project.1), calls=%async_computation | async-start | bytes 1572864 | tf_op jit(solution)/shard_map/all_to_all | solution.py:381
  14.2 0.0 copy-done.1
  14.2 5.0 %collective-permute-start = (bf16[32,1024]{1,0:T(8,128)(2,1)S(1)}, bf16[32,1024]{1,0:T(8,128)(2,1)S(1)}, u32[]{:S(2)}, u32[]{:S(2)}) collective-permute-start(bf16[32,1024]{1,0:T(8,128)(2,1)S(1)} %slice_bitcast_fusion), channel_id=1, source_target_pairs={{0,16},{16,32},{32,48},{48,64},{64,80},{80,96},{96,112},{112,128},... | collective-permute-start | bytes 196616 | tf_op jit(solution)/shard_map/ppermute | solution.py:408
  19.3 1.9 %collective-permute-start.1 = (bf16[16,1024]{1,0:T(8,128)(2,1)S(1)}, bf16[16,1024]{1,0:T(8,128)(2,1)S(1)}, u32[]{:S(2)}, u32[]{:S(2)}) collective-permute-start(bf16[16,1024]{1,0:T(8,128)(2,1)S(1)} %slice_bitcast_fusion.1), channel_id=1, source_target_pairs={{16,0},{32,16},{48,32},{64,48},{80,64},{96,80},{112,96},{128,112},... | collective-permute-start | bytes 98312 | tf_op jit(solution)/shard_map/ppermute | solution.py:409
  23.2 5.4 %collective-permute-done.1.after_ref = bf16[16,1024]{1,0:T(8,128)(2,1)S(1)} collective-permute-done((bf16[16,1024]{1,0:T(8,128)(2,1)S(1)}, bf16[16,1024]{1,0:T(8,128)(2,1)S(1)}, u32[]{:S(2)}, u32[]{:S(2)}) %collective-permute-start.1) | collective-permute-done | bytes 32800 | tf_op jit(solution)/shard_map/ppermute | solution.py:409
  28.5 0.0 collective-permute-done.before_ref
  28.5 0.0 all-to-all-done.packed_ref
  28.5 11.3 %attend.1 = bf16[16,160,128]{2,1,0:T(8,128)(2,1)} custom-call(s32[1]{0:T(128)S(6)} %copy.17.length_ref, s32[1]{0:T(128)S(6)} %copy.18.stretch_ref, s32[1]{0:T(128)S(6)} %copy.19.look_ref, bf16[16,192,128]{2,1,0:T(8,128)(2,1)S(1)} %all-to-all-done.packed_ref, bf16[32,1024]{1,0:T(8,128)(2,1)S(1)} %collective-permute-done.before_ref, ...), custom_call_target="tpu_custom_call" | custom-call | tf_op jit(solution)/shard_map/attend/pallas_call | solution.py:236
  39.9 4.3 %all-to-all-start.1 = ((bf16[16,160,128]{2,1,0:T(8,128)(2,1)}), bf16[16,160,128]{2,1,0:T(8,128)(2,1)S(1)}, u32[]{:S(2)}, u32[]{:S(2)}) async-start(bf16[16,160,128]{2,1,0:T(8,128)(2,1)} %attend.1), calls=%async_computation.1 | async-start | bytes 1310720 | tf_op jit(solution)/shard_map/all_to_all | solution.py:381
  44.2 0.0 copy-done.3
  44.2 0.1 reshape.28.taps_ref
  44.3 12.4 %all-to-all-done.1.ctx_ref = bf16[16,160,128]{2,1,0:T(8,128)(2,1)S(1)} async-done(((bf16[16,160,128]{2,1,0:T(8,128)(2,1)}), bf16[16,160,128]{2,1,0:T(8,128)(2,1)S(1)}, u32[]{:S(2)}, u32[]{:S(2)}) %all-to-all-start.1) | async-done | bytes 655392 | tf_op jit(solution)/shard_map/all_to_all | solution.py:381
  56.6 0.0 copy-done
  56.6 6.0 %finish.1 = (bf16[128,1024]{1,0:T(8,128)(2,1)}, bf16[128,1024]{1,0:T(8,128)(2,1)}, f32[16,16,128]{2,1,0:T(8,128)S(1)}) custom-call(s32[1]{0:T(128)} %bitcast.place_ref, s32[1]{0:T(128)S(6)} %copy.17.length_ref, bf16[16,160,128]{2,1,0:T(8,128)(2,1)S(1)} %all-to-all-done.1.ctx_ref, bf16[32,1024]{1,0:T(8,128)(2,1)S(1)} %collective-permute-done.before_ref, ...), custom_call_target="tpu_custom_call" | custom-call | tf_op jit(solution)/shard_map/finish/pallas_call | solution.py:356
  62.7 11.6 %all_to_all.25 = f32[16,16,128]{2,1,0:T(8,128)S(1)} all-to-all(f32[16,16,128]{2,1,0:T(8,128)S(1)} %get-tuple-element.8), channel_id=1, replica_groups=mesh['seq'=16,'dp'=16] {'seq'}, dimensions={0} | all-to-all | bytes 262144 | tf_op jit(solution)/shard_map/all_to_all | solution.py:381
  74.3 17.0 %all_to_all.26 = f32[16,16,128]{2,1,0:T(8,128)S(1)} all-to-all(f32[16,16,128]{2,1,0:T(8,128)S(1)} %broadcast_in_dim.28), channel_id=1, replica_groups=mesh['seq'=16,'dp'=16] {'dp'}, dimensions={0} | all-to-all | bytes 262144 | tf_op jit(solution)/shard_map/all_to_all | solution.py:381
  91.4 12.7 %all_to_all.27 = f32[16,16,128]{2,1,0:T(8,128)S(1)} all-to-all(f32[16,16,128]{2,1,0:T(8,128)S(1)} %broadcast_in_dim.29), channel_id=1, replica_groups=mesh['seq'=16,'dp'=16] {'seq'}, dimensions={0} | all-to-all | bytes 262144 | tf_op jit(solution)/shard_map/all_to_all | solution.py:381
  104.1 0.1 copy.15
  104.2 0.7 copy.16
  (8 shorter events, 0.1 us)
Async XLA Ops:
  0.6 13.6 %copy-start.1 = (bf16[1,128,1024]{2,1,0:T(8,128)(2,1)S(1)}, bf16[1,128,1024]{2,1,0:T(8,128)(2,1)}, u32[]{:S(2)}) copy-start(bf16[1,128,1024]{2,1,0:T(8,128)(2,1)} %param.11) | copy-start | bytes 786436
  5.6 38.6 %copy-start.3 = (bf16[31,1024]{1,0:T(8,128)(2,1)S(1)}, bf16[31,1024]{1,0:T(8,128)(2,1)}, u32[]{:S(2)}) copy-start(bf16[31,1024]{1,0:T(8,128)(2,1)} %param.21) | copy-start | bytes 190468
  5.6 51.0 %copy-start = (bf16[1024,1024]{1,0:T(8,128)(2,1)S(1)}, bf16[1024,1024]{1,0:T(8,128)(2,1)}, u32[]{:S(2)}) copy-start(bf16[1024,1024]{1,0:T(8,128)(2,1)} %wo_ref.1) | copy-start | bytes 6291460
  5.6 51.0 %copy-start.2 = (f32[1024]{0:T(1024)S(1)}, f32[1024]{0:T(1024)}, u32[]{:S(2)}) copy-start(f32[1024]{0:T(1024)} %param.16) | copy-start | bytes 12292
  5.6 22.9 %all-to-all-start = ((bf16[16,192,128]{2,1,0:T(8,128)(2,1)}), bf16[16,192,128]{2,1,0:T(8,128)(2,1)S(1)}, u32[]{:S(2)}, u32[]{:S(2)}) async-start(bf16[16,192,128]{2,1,0:T(8,128)(2,1)} %project.1), calls=%async_computation | async-start | bytes 1572864 | tf_op jit(solution)/shard_map/all_to_all | solution.py:381
  14.2 14.3 %collective-permute-start = (bf16[32,1024]{1,0:T(8,128)(2,1)S(1)}, bf16[32,1024]{1,0:T(8,128)(2,1)S(1)}, u32[]{:S(2)}, u32[]{:S(2)}) collective-permute-start(bf16[32,1024]{1,0:T(8,128)(2,1)S(1)} %slice_bitcast_fusion), channel_id=1, source_target_pairs={{0,16},{16,32},{32,48},{48,64},{64,80},{80,96},{96,112},{112,128},... | collective-permute-start | bytes 196616 | tf_op jit(solution)/shard_map/ppermute | solution.py:408
  19.3 9.2 %collective-permute-start.1 = (bf16[16,1024]{1,0:T(8,128)(2,1)S(1)}, bf16[16,1024]{1,0:T(8,128)(2,1)S(1)}, u32[]{:S(2)}, u32[]{:S(2)}) collective-permute-start(bf16[16,1024]{1,0:T(8,128)(2,1)S(1)} %slice_bitcast_fusion.1), channel_id=1, source_target_pairs={{16,0},{32,16},{48,32},{64,48},{80,64},{96,80},{112,96},{128,112},... | collective-permute-start | bytes 98312 | tf_op jit(solution)/shard_map/ppermute | solution.py:409
  39.9 16.8 %all-to-all-start.1 = ((bf16[16,160,128]{2,1,0:T(8,128)(2,1)}), bf16[16,160,128]{2,1,0:T(8,128)(2,1)S(1)}, u32[]{:S(2)}, u32[]{:S(2)}) async-start(bf16[16,160,128]{2,1,0:T(8,128)(2,1)} %attend.1), calls=%async_computation.1 | async-start | bytes 1310720 | tf_op jit(solution)/shard_map/all_to_all | solution.py:381

commit v4 on v3

--- a/solution.py
+++ b/solution.py
@@ -113,7 +113,7 @@
 
 def attend_kernel(
     length_ref, stretch_ref, look_ref, packed_ref, before_ref, after_ref, out_ref,
-    q_ref, bias_ref, s0_ref, s1_ref, full_ref, near_ref,
+    q_ref, bias_ref, s0_ref, s1_ref, w_ref, full_ref, near_ref,
 ):
     blocks, packed_rows, _ = packed_ref.shape
     rows = packed_rows * 2 // 3
@@ -122,7 +122,6 @@
     steps = total // QUERIES
     share = QUERIES // rows
     length = length_ref[0]
-    length_f = length.astype(F32)
     stretch = stretch_ref[0].astype(F32)
     look = look_ref[0].astype(F32)
     low_half = low_lanes(half)
@@ -131,6 +130,7 @@
         start = block * rows
         q_ref[start : start + half] = jnp.where(low_half, q, 0.0).astype(BF16)
         q_ref[start + half : start + rows] = jnp.where(low_half, half_turn(q), 0.0).astype(BF16)
+    w_ref[...] = jnp.zeros_like(w_ref)
     near_ref[:BEFORE] = jnp.zeros((BEFORE, LANES), BF16)
     full_ref[:AFTER] = jnp.zeros((AFTER, LANES), BF16)
     full_ref[AFTER + total :] = jnp.zeros((AFTER, LANES), BF16)
@@ -149,9 +149,17 @@
 
     def score(index, s_ref):
         q = q_ref[at(index)]
-        always = SHORTEST // rows
-        s_ref[:, :SHORTEST] = dot_rows(q, keys(0, always))
-        s_ref[:, SHORTEST:] = dot_rows(q, keys(always, blocks - always)) + bias_ref[0:1, SHORTEST:]
+        top = None
+        for first in range(0, total, 512):
+            cols = slice(first, first + 512)
+            part = dot_rows(q, keys(first // rows, 512 // rows))
+            if first >= SHORTEST:
+                part = part + bias_ref[0:1, cols]
+            s_ref[:, cols] = part
+            for lane_at in range(0, 512, LANES):
+                piece = part[:, lane_at : lane_at + LANES]
+                top = piece if top is None else jnp.maximum(top, piece)
+        s_ref[:, total:] = top
 
     def own(index, s_ref):
         @pl.when((index + 1) * QUERIES > length)
@@ -161,43 +169,53 @@
                 start = pl.multiple_of(block * rows, rows)
                 raw = dot_rows(q_ref[pl.ds(start, rows)], packed_ref[block, :rows])
                 seen = (lane == row) | (lane + start < length)
-                s_ref[part * rows : (part + 1) * rows, pl.ds(start, rows)] = jnp.where(
-                    seen, raw, FLOOR_SCORE
-                )
+                raw = jnp.where(seen, raw, FLOOR_SCORE)
+                span = slice(part * rows, (part + 1) * rows)
+                s_ref[span, pl.ds(start, rows)] = raw
+                s_ref[span, total:] = jnp.maximum(s_ref[span, total:], raw)
 
     def mix(index, s_ref):
-        weights, totals = row_softmax(s_ref[...])
+        highest = jnp.max(s_ref[:, total:], axis=-1, keepdims=True)
+        expo = jnp.exp(s_ref[:, :total] - highest)
+        totals = jnp.sum(expo, axis=-1, keepdims=True)
+        weights = expo.astype(BF16)
         mixed = jnp.dot(weights, keys(0, blocks), preferred_element_type=F32)
         full_ref[pl.ds(pl.multiple_of(index * QUERIES + AFTER, AFTER), QUERIES)] = half_turn(
             mixed / totals
         ).astype(BF16)
 
-    def near(block):
-        start = pl.multiple_of(block * rows, rows)
-        base = (block * rows).astype(F32) if not isinstance(block, int) else float(block * rows)
-        pos = row_f + base
-        begin = jnp.floor((pos + 0.5) / stretch) * stretch
-        first = jnp.broadcast_to(jnp.maximum(begin - LEFT, 0.0) - base, (rows, LANES))
-        last = jnp.broadcast_to(jnp.minimum(begin + stretch + look, length_f) - base, (rows, LANES))
-        around = (jnp.maximum(block - 1, 0), block, jnp.minimum(block + 1, blocks - 1))
-        window = jnp.concatenate([packed_ref[b, :rows] for b in around], axis=0)
-        raw = dot_rows(q_ref[pl.ds(start, rows)], window)
-        parts = []
-        for part in range(3):
-            key_at = lane_f + float((part - 1) * rows)
-            inside = (key_at >= first) & (key_at < last)
-            if part == 1:
-                inside = inside | (lane == row)
-            parts.append(jnp.where(inside, raw[:, part * rows : (part + 1) * rows], FLOOR_SCORE))
-        weights, totals = row_softmax(jnp.concatenate(parts, axis=1))
-        mixed = jnp.dot(weights, window, preferred_element_type=F32)
-        near_ref[pl.ds(pl.multiple_of(start + BEFORE, BEFORE), rows)] = (mixed / totals).astype(
-            BF16
-        )
-
-    def nears(index):
+    def near(index, s_ref):
+        sums = []
         for part in range(share):
-            near(index * share + part)
+            block = index * share + part
+            base = (block * rows).astype(F32)
+            begin = jnp.floor((row_f + base + 0.5) / stretch) * stretch
+            first = jnp.broadcast_to(jnp.maximum(begin - LEFT, 0.0) - base, (rows, LANES))
+            last = jnp.broadcast_to(
+                jnp.minimum(begin + stretch + look, float(total)) - base, (rows, LANES)
+            )
+            span = slice(part * rows, (part + 1) * rows)
+            around = (jnp.maximum(block - 1, 0), block, jnp.minimum(block + 1, blocks - 1))
+            pieces = []
+            for place, other in enumerate(around):
+                key_at = lane_f + float((place - 1) * rows)
+                if place == 0:
+                    inside = key_at >= first
+                elif place == 1:
+                    inside = (key_at >= first) & (key_at < last)
+                else:
+                    inside = key_at < last
+                raw = s_ref[span, pl.ds(pl.multiple_of(other * rows, rows), rows)]
+                pieces.append(jnp.where(inside, raw, FLOOR_SCORE))
+            weights, totals = row_softmax(jnp.concatenate(pieces, axis=1))
+            w_ref[span, part * rows : (part + 3) * rows] = weights
+            sums.append(totals)
+        others = [jnp.clip(index * share + b, 0, blocks - 1) for b in range(-1, share + 1)]
+        window = jnp.concatenate([packed_ref[b, :rows] for b in others], axis=0)
+        mixed = jnp.dot(w_ref[...], window, preferred_element_type=F32)
+        near_ref[pl.ds(pl.multiple_of(index * QUERIES + BEFORE, BEFORE), QUERIES)] = (
+            mixed / jnp.concatenate(sums, axis=0)
+        ).astype(BF16)
 
     score(0, s0_ref)
     own(0, s0_ref)
@@ -205,28 +223,26 @@
     def body(step, carry):
         score(2 * step + 1, s1_ref)
         mix(2 * step, s0_ref)
-        nears(2 * step)
+        near(2 * step, s0_ref)
         own(2 * step + 1, s1_ref)
         score(2 * step + 2, s0_ref)
         mix(2 * step + 1, s1_ref)
-        nears(2 * step + 1)
+        near(2 * step + 1, s1_ref)
         own(2 * step + 2, s0_ref)
         return carry
 
     lax.fori_loop(0, steps // 2 - 1, body, 0)
     score(steps - 1, s1_ref)
     mix(steps - 2, s0_ref)
-    nears(jnp.int32(steps - 2))
+    near(jnp.int32(steps - 2), s0_ref)
     own(steps - 1, s1_ref)
     mix(steps - 1, s1_ref)
-    nears(jnp.int32(steps - 1))
+    near(jnp.int32(steps - 1), s1_ref)
     ext = BEFORE + rows
     low = low_lanes(ext)
     for block in range(blocks):
         span = slice(block * rows, block * rows + ext)
-        out_ref[block] = jnp.where(
-            low, full_ref[span].astype(F32), near_ref[span].astype(F32)
-        ).astype(BF16)
+        out_ref[block] = jnp.where(low, full_ref[span], near_ref[span])
 
 
 def attend(length, stretch, look, packed, before, after):
@@ -241,8 +257,9 @@
         scratch_shapes=[
             pltpu.VMEM((total, LANES), BF16),
             pltpu.VMEM((8, total), F32),
-            pltpu.VMEM((QUERIES, total), F32),
-            pltpu.VMEM((QUERIES, total), F32),
+            pltpu.VMEM((QUERIES, total + LANES), F32),
+            pltpu.VMEM((QUERIES, total + LANES), F32),
+            pltpu.VMEM((QUERIES, QUERIES + 2 * rows), BF16),
             pltpu.VMEM((total + 2 * AFTER, LANES), BF16),
             pltpu.VMEM((BEFORE + total, LANES), BF16),
         ],

time: 105 us -> 104 us (level)
  Pallas kernels: 22.3 us -> 21.1 us
    pallas_call x1, Pallas kernels: 11.3 us -> 10.1 us  [attend(): pl.pallas_call(attend_kernel, in_specs=[SMEM_SPEC] * 3 + [VMEM_SPEC] + [p...]
where the time goes in v4:
time: 104 us
  blocking collectives  41.3 us (40%)
  Pallas kernels  21.1 us (20%)
  starting transfers between devices  19.9 us (19%)
  waiting for transfers between devices  17.7 us (17%)
  between operations  2.7 us (3%)
    all_to_all x3, blocking collectives, swap(): return lax.all_to_all(value, axis, 0, 0, tiled=True)  41.3 us
    all_to_all x2, starting transfers between devices, swap(): return lax.all_to_all(value, axis, 0, 0, tiled=True)  12.9 us
    all_to_all x2, waiting for transfers between devices, swap(): return lax.all_to_all(value, axis, 0, 0, tiled=True)  12.4 us
    pallas_call x1, Pallas kernels, attend(): pl.pallas_call(attend_kernel, in_specs=[SMEM_SPEC] * 3 + [VMEM_SPEC] + [p...  10.1 us
    pallas_call x1, Pallas kernels, finish(): pl.pallas_call(finish_kernel, in_specs=[SMEM_SPEC] * 2 + [VMEM_SPEC] * 7,...  6.04 us
    ppermute x1, waiting for transfers between devices, per_device(): after = lax.ppermute(source[:AFTER], 'seq', down)  5.37 us
    ppermute x1, starting transfers between devices, per_device(): before = lax.ppermute(source[rows - BEFORE:], 'seq', up)  5.04 us
    pallas_call x1, Pallas kernels, project(): pl.pallas_call(project_kernel, in_specs=[hbm, VMEM_SPEC, hbm, hbm, hbm],...  4.92 us
  transfers between devices with their start and end apart: 4, of which 2 were waited for; matrix products, arithmetic and copies ran while one was open for 0% of the time, Pallas kernels for 0%

profile of v4, /device:TPU:1, one launch (start us, length us, event | category | flops | bytes accessed | tf_op | source)
XLA Modules:
  0.0 103.6 jit_solution(13870416429477976542)
XLA Ops:
  0.6 0.0 copy-start.1
  0.6 4.9 %project.1 = bf16[16,192,128]{2,1,0:T(8,128)(2,1)} custom-call(bf16[128,1024]{1,0:T(8,128)(2,1)} %bitcast.17, f32[1,1024]{1,0:T(1,128)} %bitcast.23, bf16[1024,1024]{1,0:T(8,128)(2,1)} %wq_hbm.1, bf16[1024,1024]{1,0:T(8,128)(2,1)} %wk_hbm.1, bf16[1024,1024]{1,0:T(8,128)(2,1)} %wv_hbm.1), custom_call_target="tpu_custom_call" | custom-call | tf_op jit(solution)/shard_map/project/pallas_call | solution.py:93
  5.6 0.0 copy-start.3
  5.6 0.0 copy-start
  5.6 0.0 copy-start.2
  5.6 8.6 %all-to-all-start = ((bf16[16,192,128]{2,1,0:T(8,128)(2,1)}), bf16[16,192,128]{2,1,0:T(8,128)(2,1)S(1)}, u32[]{:S(2)}, u32[]{:S(2)}) async-start(bf16[16,192,128]{2,1,0:T(8,128)(2,1)} %project.1), calls=%async_computation | async-start | bytes 1572864 | tf_op jit(solution)/shard_map/all_to_all | solution.py:398
  14.2 0.0 copy-done.1
  14.2 5.0 %collective-permute-start = (bf16[32,1024]{1,0:T(8,128)(2,1)S(1)}, bf16[32,1024]{1,0:T(8,128)(2,1)S(1)}, u32[]{:S(2)}, u32[]{:S(2)}) collective-permute-start(bf16[32,1024]{1,0:T(8,128)(2,1)S(1)} %slice_bitcast_fusion), channel_id=1, source_target_pairs={{0,16},{16,32},{32,48},{48,64},{64,80},{80,96},{96,112},{112,128},... | collective-permute-start | bytes 196616 | tf_op jit(solution)/shard_map/ppermute | solution.py:425
  19.3 1.9 %collective-permute-start.1 = (bf16[16,1024]{1,0:T(8,128)(2,1)S(1)}, bf16[16,1024]{1,0:T(8,128)(2,1)S(1)}, u32[]{:S(2)}, u32[]{:S(2)}) collective-permute-start(bf16[16,1024]{1,0:T(8,128)(2,1)S(1)} %slice_bitcast_fusion.1), channel_id=1, source_target_pairs={{16,0},{32,16},{48,32},{64,48},{80,64},{96,80},{112,96},{128,112},... | collective-permute-start | bytes 98312 | tf_op jit(solution)/shard_map/ppermute | solution.py:426
  23.2 5.4 %collective-permute-done.1.after_ref = bf16[16,1024]{1,0:T(8,128)(2,1)S(1)} collective-permute-done((bf16[16,1024]{1,0:T(8,128)(2,1)S(1)}, bf16[16,1024]{1,0:T(8,128)(2,1)S(1)}, u32[]{:S(2)}, u32[]{:S(2)}) %collective-permute-start.1) | collective-permute-done | bytes 32800 | tf_op jit(solution)/shard_map/ppermute | solution.py:426
  28.5 0.0 collective-permute-done.before_ref
  28.5 0.0 all-to-all-done.packed_ref
  28.5 10.1 %attend.1 = bf16[16,160,128]{2,1,0:T(8,128)(2,1)} custom-call(s32[1]{0:T(128)S(6)} %copy.17.length_ref, s32[1]{0:T(128)S(6)} %copy.18.stretch_ref, s32[1]{0:T(128)S(6)} %copy.19.look_ref, bf16[16,192,128]{2,1,0:T(8,128)(2,1)S(1)} %all-to-all-done.packed_ref, bf16[32,1024]{1,0:T(8,128)(2,1)S(1)} %collective-permute-done.before_ref, ...), custom_call_target="tpu_custom_call" | custom-call | tf_op jit(solution)/shard_map/attend/pallas_call | solution.py:252
  38.6 4.3 %all-to-all-start.1 = ((bf16[16,160,128]{2,1,0:T(8,128)(2,1)}), bf16[16,160,128]{2,1,0:T(8,128)(2,1)S(1)}, u32[]{:S(2)}, u32[]{:S(2)}) async-start(bf16[16,160,128]{2,1,0:T(8,128)(2,1)} %attend.1), calls=%async_computation.1 | async-start | bytes 1310720 | tf_op jit(solution)/shard_map/all_to_all | solution.py:398
  43.0 0.0 copy-done.3
  43.0 0.1 reshape.28.taps_ref
  43.0 12.4 %all-to-all-done.1.ctx_ref = bf16[16,160,128]{2,1,0:T(8,128)(2,1)S(1)} async-done(((bf16[16,160,128]{2,1,0:T(8,128)(2,1)}), bf16[16,160,128]{2,1,0:T(8,128)(2,1)S(1)}, u32[]{:S(2)}, u32[]{:S(2)}) %all-to-all-start.1) | async-done | bytes 655392 | tf_op jit(solution)/shard_map/all_to_all | solution.py:398
  55.4 0.0 copy-done
  55.4 6.0 %finish.1 = (bf16[128,1024]{1,0:T(8,128)(2,1)}, bf16[128,1024]{1,0:T(8,128)(2,1)}, f32[16,16,128]{2,1,0:T(8,128)S(1)}) custom-call(s32[1]{0:T(128)} %bitcast.place_ref, s32[1]{0:T(128)S(6)} %copy.17.length_ref, bf16[16,160,128]{2,1,0:T(8,128)(2,1)S(1)} %all-to-all-done.1.ctx_ref, bf16[32,1024]{1,0:T(8,128)(2,1)S(1)} %collective-permute-done.before_ref, ...), custom_call_target="tpu_custom_call" | custom-call | tf_op jit(solution)/shard_map/finish/pallas_call | solution.py:373
  61.4 11.6 %all_to_all.25 = f32[16,16,128]{2,1,0:T(8,128)S(1)} all-to-all(f32[16,16,128]{2,1,0:T(8,128)S(1)} %get-tuple-element.8), channel_id=1, replica_groups=mesh['seq'=16,'dp'=16] {'seq'}, dimensions={0} | all-to-all | bytes 262144 | tf_op jit(solution)/shard_map/all_to_all | solution.py:398
  73.1 17.0 %all_to_all.26 = f32[16,16,128]{2,1,0:T(8,128)S(1)} all-to-all(f32[16,16,128]{2,1,0:T(8,128)S(1)} %broadcast_in_dim.28), channel_id=1, replica_groups=mesh['seq'=16,'dp'=16] {'dp'}, dimensions={0} | all-to-all | bytes 262144 | tf_op jit(solution)/shard_map/all_to_all | solution.py:398
  90.2 12.7 %all_to_all.27 = f32[16,16,128]{2,1,0:T(8,128)S(1)} all-to-all(f32[16,16,128]{2,1,0:T(8,128)S(1)} %broadcast_in_dim.29), channel_id=1, replica_groups=mesh['seq'=16,'dp'=16] {'seq'}, dimensions={0} | all-to-all | bytes 262144 | tf_op jit(solution)/shard_map/all_to_all | solution.py:398
  102.9 0.1 copy.15
  103.0 0.7 copy.16
  (8 shorter events, 0.1 us)
Async XLA Ops:
  0.6 13.6 %copy-start.1 = (bf16[1,128,1024]{2,1,0:T(8,128)(2,1)S(1)}, bf16[1,128,1024]{2,1,0:T(8,128)(2,1)}, u32[]{:S(2)}) copy-start(bf16[1,128,1024]{2,1,0:T(8,128)(2,1)} %param.11) | copy-start | bytes 786436
  5.6 37.4 %copy-start.3 = (bf16[31,1024]{1,0:T(8,128)(2,1)S(1)}, bf16[31,1024]{1,0:T(8,128)(2,1)}, u32[]{:S(2)}) copy-start(bf16[31,1024]{1,0:T(8,128)(2,1)} %param.21) | copy-start | bytes 190468
  5.6 49.8 %copy-start = (bf16[1024,1024]{1,0:T(8,128)(2,1)S(1)}, bf16[1024,1024]{1,0:T(8,128)(2,1)}, u32[]{:S(2)}) copy-start(bf16[1024,1024]{1,0:T(8,128)(2,1)} %wo_ref.1) | copy-start | bytes 6291460
  5.6 49.8 %copy-start.2 = (f32[1024]{0:T(1024)S(1)}, f32[1024]{0:T(1024)}, u32[]{:S(2)}) copy-start(f32[1024]{0:T(1024)} %param.16) | copy-start | bytes 12292
  5.6 22.9 %all-to-all-start = ((bf16[16,192,128]{2,1,0:T(8,128)(2,1)}), bf16[16,192,128]{2,1,0:T(8,128)(2,1)S(1)}, u32[]{:S(2)}, u32[]{:S(2)}) async-start(bf16[16,192,128]{2,1,0:T(8,128)(2,1)} %project.1), calls=%async_computation | async-start | bytes 1572864 | tf_op jit(solution)/shard_map/all_to_all | solution.py:398
  14.2 14.3 %collective-permute-start = (bf16[32,1024]{1,0:T(8,128)(2,1)S(1)}, bf16[32,1024]{1,0:T(8,128)(2,1)S(1)}, u32[]{:S(2)}, u32[]{:S(2)}) collective-permute-start(bf16[32,1024]{1,0:T(8,128)(2,1)S(1)} %slice_bitcast_fusion), channel_id=1, source_target_pairs={{0,16},{16,32},{32,48},{48,64},{64,80},{80,96},{96,112},{112,128},... | collective-permute-start | bytes 196616 | tf_op jit(solution)/shard_map/ppermute | solution.py:425
  19.3 9.2 %collective-permute-start.1 = (bf16[16,1024]{1,0:T(8,128)(2,1)S(1)}, bf16[16,1024]{1,0:T(8,128)(2,1)S(1)}, u32[]{:S(2)}, u32[]{:S(2)}) collective-permute-start(bf16[16,1024]{1,0:T(8,128)(2,1)S(1)} %slice_bitcast_fusion.1), channel_id=1, source_target_pairs={{16,0},{32,16},{48,32},{64,48},{80,64},{96,80},{112,96},{128,112},... | collective-permute-start | bytes 98312 | tf_op jit(solution)/shard_map/ppermute | solution.py:426
  38.6 16.8 %all-to-all-start.1 = ((bf16[16,160,128]{2,1,0:T(8,128)(2,1)}), bf16[16,160,128]{2,1,0:T(8,128)(2,1)S(1)}, u32[]{:S(2)}, u32[]{:S(2)}) async-start(bf16[16,160,128]{2,1,0:T(8,128)(2,1)} %attend.1), calls=%async_computation.1 | async-start | bytes 1310720 | tf_op jit(solution)/shard_map/all_to_all | solution.py:398

commit v5 on v4

--- a/solution.py
+++ b/solution.py
@@ -361,10 +361,9 @@
     for k, value in enumerate(sums + (zero,)):
         sums_ref[k * TILE : (k + 1) * TILE] = value
     for tile in range(width // LANES):
-        for group in range(4):
-            grad_ref[2 * tile + group // 2, group % 2 * TILE : group % 2 * TILE + TILE] = sums_ref[
-                cells(group * TILE, tile), :
-            ]
+        for part in range(2):
+            groups = [sums_ref[cells((2 * part + g) * TILE, tile), :] for g in range(2)]
+            grad_ref[2 * tile + part] = jnp.concatenate(groups, axis=0).astype(BF16)
 
 
 def finish(place, length, ctx, before, frames, after, wo, gain, taps):
@@ -377,7 +376,7 @@
         out_shape=[
             jax.ShapeDtypeStruct((rows, width), BF16),
             jax.ShapeDtypeStruct((rows, width), BF16),
-            jax.ShapeDtypeStruct((width // 64, 16, LANES), F32),
+            jax.ShapeDtypeStruct((width // 64, 16, LANES), BF16),
         ],
         scratch_shapes=[
             pltpu.VMEM((2 * ext, width), BF16),
@@ -401,6 +400,33 @@
 def spread_out(value, axis):
     size = lax.axis_size(axis)
     return swap(jnp.broadcast_to(value[None], (size,) + value.shape), axis)
+
+
+def add_up(terms):
+    total = terms[0].astype(F32)
+    for index in range(1, terms.shape[0]):
+        total = total + terms[index].astype(F32)
+    return total.astype(BF16)
+
+
+def unfold_kernel(pieces_ref, out_ref):
+    taps = out_ref.shape[0]
+    for piece in range(pieces_ref.shape[0]):
+        tile, part = piece // 2, piece % 2
+        value = pieces_ref[piece].astype(F32)
+        first = part * value.shape[0]
+        count = min(value.shape[0], taps - first)
+        out_ref[first : first + count, tile * LANES : (tile + 1) * LANES] = value[:count]
+
+
+def unfold(pieces):
+    return pl.pallas_call(
+        unfold_kernel,
+        in_specs=[VMEM_SPEC],
+        out_specs=VMEM_SPEC,
+        out_shape=jax.ShapeDtypeStruct((KERNEL, pieces.shape[0] // 2 * LANES), F32),
+        name="unfold",
+    )(pieces)
 
 
 def per_device(
@@ -430,11 +456,10 @@
     gain = norm_two[None]
     ctx = swap(attend(lengths, stretch_sizes, look_ahead, packed, before, after), "seq")
     full, near, grad = finish(place, lengths, ctx, before, source, after, w_out, gain, taps)
-    piece = jnp.sum(swap(grad, "seq"), axis=0)
-    piece = jnp.sum(spread_out(piece, "dp"), axis=0)
-    grads = spread_out(piece, "seq")
-    grads = grads.reshape(width // LANES, 32, LANES).transpose(1, 0, 2).reshape(32, width)
-    return full[None], near[None], grads[:KERNEL]
+    piece = add_up(swap(grad, "seq"))
+    piece = add_up(spread_out(piece, "dp"))
+    grads = unfold(spread_out(piece, "seq"))
+    return full[None], near[None], grads
 
 
 def solution(mesh):

time: 104 us -> 103 us (level)
  Pallas kernels: 21.1 us -> 22.4 us
  blocking collectives: 41.3 us -> 40.2 us
    pallas_call x0 -> x1, Pallas kernels: none -> 1.5 us  [unfold(): pl.pallas_call(unfold_kernel, in_specs=[VMEM_SPEC], out_specs=VMEM_SPEC,...]
    all_to_all x3, blocking collectives: 41.3 us -> 40.2 us  [swap(): return lax.all_to_all(value, axis, 0, 0, tiled=True)]
where the time goes in v5:
time: 103 us
  blocking collectives  40.2 us (39%)
  Pallas kernels  22.4 us (22%)
  starting transfers between devices  19.9 us (19%)
  waiting for transfers between devices  17.7 us (17%)
  between operations  2.69 us (3%)
    all_to_all x3, blocking collectives, swap(): return lax.all_to_all(value, axis, 0, 0, tiled=True)  40.2 us
    all_to_all x2, starting transfers between devices, swap(): return lax.all_to_all(value, axis, 0, 0, tiled=True)  12.9 us
    all_to_all x2, waiting for transfers between devices, swap(): return lax.all_to_all(value, axis, 0, 0, tiled=True)  12.4 us
    pallas_call x1, Pallas kernels, attend(): pl.pallas_call(attend_kernel, in_specs=[SMEM_SPEC] * 3 + [VMEM_SPEC] + [p...  10 us
    pallas_call x1, Pallas kernels, finish(): pl.pallas_call(finish_kernel, in_specs=[SMEM_SPEC] * 2 + [VMEM_SPEC] * 7,...  6 us
    ppermute x1, waiting for transfers between devices, per_device(): after = lax.ppermute(source[:AFTER], 'seq', down)  5.37 us
    ppermute x1, starting transfers between devices, per_device(): before = lax.ppermute(source[rows - BEFORE:], 'seq', up)  5.04 us
    pallas_call x1, Pallas kernels, project(): pl.pallas_call(project_kernel, in_specs=[hbm, VMEM_SPEC, hbm, hbm, hbm],...  4.9 us
  transfers between devices with their start and end apart: 4, of which 2 were waited for; matrix products, arithmetic and copies ran while one was open for 0% of the time, Pallas kernels for 0%

profile of v5, /device:TPU:1, one launch (start us, length us, event | category | flops | bytes accessed | tf_op | source)
XLA Modules:
  0.0 103.1 jit_solution(9936955527506148811)
XLA Ops:
  0.6 0.0 copy-start.1
  0.6 4.9 %project.1 = bf16[16,192,128]{2,1,0:T(8,128)(2,1)} custom-call(bf16[128,1024]{1,0:T(8,128)(2,1)} %bitcast.14, f32[1,1024]{1,0:T(1,128)} %bitcast.17, bf16[1024,1024]{1,0:T(8,128)(2,1)} %wq_hbm.1, bf16[1024,1024]{1,0:T(8,128)(2,1)} %wk_hbm.1, bf16[1024,1024]{1,0:T(8,128)(2,1)} %wv_hbm.1), custom_call_target="tpu_custom_call" | custom-call | tf_op jit(solution)/shard_map/project/pallas_call | solution.py:93
  5.6 0.0 copy-start.3
  5.6 0.0 copy-start
  5.6 0.0 copy-start.2
  5.6 8.6 %all-to-all-start = ((bf16[16,192,128]{2,1,0:T(8,128)(2,1)}), bf16[16,192,128]{2,1,0:T(8,128)(2,1)S(1)}, u32[]{:S(2)}, u32[]{:S(2)}) async-start(bf16[16,192,128]{2,1,0:T(8,128)(2,1)} %project.1), calls=%async_computation | async-start | bytes 1572864 | tf_op jit(solution)/shard_map/all_to_all | solution.py:397
  14.2 0.0 copy-done.1
  14.2 5.0 %collective-permute-start = (bf16[32,1024]{1,0:T(8,128)(2,1)S(1)}, bf16[32,1024]{1,0:T(8,128)(2,1)S(1)}, u32[]{:S(2)}, u32[]{:S(2)}) collective-permute-start(bf16[32,1024]{1,0:T(8,128)(2,1)S(1)} %slice_bitcast_fusion), channel_id=1, source_target_pairs={{0,16},{16,32},{32,48},{48,64},{64,80},{80,96},{96,112},{112,128},... | collective-permute-start | bytes 196616 | tf_op jit(solution)/shard_map/ppermute | solution.py:451
  19.3 1.9 %collective-permute-start.1 = (bf16[16,1024]{1,0:T(8,128)(2,1)S(1)}, bf16[16,1024]{1,0:T(8,128)(2,1)S(1)}, u32[]{:S(2)}, u32[]{:S(2)}) collective-permute-start(bf16[16,1024]{1,0:T(8,128)(2,1)S(1)} %slice_bitcast_fusion.1), channel_id=1, source_target_pairs={{16,0},{32,16},{48,32},{64,48},{80,64},{96,80},{112,96},{128,112},... | collective-permute-start | bytes 98312 | tf_op jit(solution)/shard_map/ppermute | solution.py:452
  23.1 5.4 %collective-permute-done.1.after_ref = bf16[16,1024]{1,0:T(8,128)(2,1)S(1)} collective-permute-done((bf16[16,1024]{1,0:T(8,128)(2,1)S(1)}, bf16[16,1024]{1,0:T(8,128)(2,1)S(1)}, u32[]{:S(2)}, u32[]{:S(2)}) %collective-permute-start.1) | collective-permute-done | bytes 32800 | tf_op jit(solution)/shard_map/ppermute | solution.py:452
  28.5 0.0 collective-permute-done.before_ref
  28.5 0.0 all-to-all-done.packed_ref
  28.5 10.0 %attend.1 = bf16[16,160,128]{2,1,0:T(8,128)(2,1)} custom-call(s32[1]{0:T(128)S(6)} %copy.14.length_ref, s32[1]{0:T(128)S(6)} %copy.15.stretch_ref, s32[1]{0:T(128)S(6)} %copy.16.look_ref, bf16[16,192,128]{2,1,0:T(8,128)(2,1)S(1)} %all-to-all-done.packed_ref, bf16[32,1024]{1,0:T(8,128)(2,1)S(1)} %collective-permute-done.before_ref, ...), custom_call_target="tpu_custom_call" | custom-call | tf_op jit(solution)/shard_map/attend/pallas_call | solution.py:252
  38.5 4.3 %all-to-all-start.1 = ((bf16[16,160,128]{2,1,0:T(8,128)(2,1)}), bf16[16,160,128]{2,1,0:T(8,128)(2,1)S(1)}, u32[]{:S(2)}, u32[]{:S(2)}) async-start(bf16[16,160,128]{2,1,0:T(8,128)(2,1)} %attend.1), calls=%async_computation.1 | async-start | bytes 1310720 | tf_op jit(solution)/shard_map/all_to_all | solution.py:397
  42.9 0.0 copy-done.3
  42.9 0.1 reshape.20.taps_ref
  42.9 12.4 %all-to-all-done.1.ctx_ref = bf16[16,160,128]{2,1,0:T(8,128)(2,1)S(1)} async-done(((bf16[16,160,128]{2,1,0:T(8,128)(2,1)}), bf16[16,160,128]{2,1,0:T(8,128)(2,1)S(1)}, u32[]{:S(2)}, u32[]{:S(2)}) %all-to-all-start.1) | async-done | bytes 655392 | tf_op jit(solution)/shard_map/all_to_all | solution.py:397
  55.3 0.0 copy-done
  55.3 0.0 copy-done.2
  55.3 6.0 %finish.1 = (bf16[128,1024]{1,0:T(8,128)(2,1)}, bf16[128,1024]{1,0:T(8,128)(2,1)}, bf16[16,16,128]{2,1,0:T(8,128)(2,1)S(1)}) custom-call(s32[1]{0:T(128)} %bitcast.place_ref, s32[1]{0:T(128)S(6)} %copy.14.length_ref, bf16[16,160,128]{2,1,0:T(8,128)(2,1)S(1)} %all-to-all-done.1.ctx_ref, bf16[32,1024]{1,0:T(8,128)(2,1)S(1)} %collective-permute-done.before_ref, ...), custom_call_target="tpu_custom_call" | custom-call | tf_op jit(solution)/shard_map/finish/pallas_call | solution.py:372
  61.3 11.3 %all_to_all.25 = bf16[16,16,128]{2,1,0:T(8,128)(2,1)S(1)} all-to-all(bf16[16,16,128]{2,1,0:T(8,128)(2,1)S(1)} %get-tuple-element.8), channel_id=1, replica_groups=mesh['seq'=16,'dp'=16] {'seq'}, dimensions={0} | all-to-all | bytes 131072 | tf_op jit(solution)/shard_map/all_to_all | solution.py:397
  72.7 16.5 %all_to_all.26 = bf16[16,16,128]{2,1,0:T(8,128)(2,1)S(1)} all-to-all(bf16[16,16,128]{2,1,0:T(8,128)(2,1)S(1)} %broadcast_in_dim.33), channel_id=1, replica_groups=mesh['seq'=16,'dp'=16] {'dp'}, dimensions={0} | all-to-all | bytes 131072 | tf_op jit(solution)/shard_map/all_to_all | solution.py:397
  89.2 12.3 %all_to_all.27.pieces_ref = bf16[16,16,128]{2,1,0:T(8,128)(2,1)} all-to-all(bf16[16,16,128]{2,1,0:T(8,128)(2,1)S(1)} %broadcast_in_dim.35), channel_id=1, replica_groups=mesh['seq'=16,'dp'=16] {'seq'}, dimensions={0} | all-to-all | bytes 131072 | tf_op jit(solution)/shard_map/all_to_all | solution.py:397
  101.5 1.5 %unfold.1 = f32[31,1024]{1,0:T(8,128)} custom-call(bf16[16,16,128]{2,1,0:T(8,128)(2,1)} %all_to_all.27.pieces_ref), custom_call_target="tpu_custom_call" | custom-call | tf_op jit(solution)/shard_map/unfold/pallas_call | solution.py:423
  (6 shorter events, 0.1 us)
Async XLA Ops:
  0.6 13.6 %copy-start.1 = (bf16[1,128,1024]{2,1,0:T(8,128)(2,1)S(1)}, bf16[1,128,1024]{2,1,0:T(8,128)(2,1)}, u32[]{:S(2)}) copy-start(bf16[1,128,1024]{2,1,0:T(8,128)(2,1)} %param.11) | copy-start | bytes 786436
  5.6 37.3 %copy-start.3 = (bf16[31,1024]{1,0:T(8,128)(2,1)S(1)}, bf16[31,1024]{1,0:T(8,128)(2,1)}, u32[]{:S(2)}) copy-start(bf16[31,1024]{1,0:T(8,128)(2,1)} %param.21) | copy-start | bytes 190468
  5.6 49.7 %copy-start = (bf16[1024,1024]{1,0:T(8,128)(2,1)S(1)}, bf16[1024,1024]{1,0:T(8,128)(2,1)}, u32[]{:S(2)}) copy-start(bf16[1024,1024]{1,0:T(8,128)(2,1)} %wo_ref.1) | copy-start | bytes 6291460
  5.6 49.7 %copy-start.2 = (f32[1024]{0:T(1024)S(1)}, f32[1024]{0:T(1024)}, u32[]{:S(2)}) copy-start(f32[1024]{0:T(1024)} %param.16) | copy-start | bytes 12292
  5.6 22.9 %all-to-all-start = ((bf16[16,192,128]{2,1,0:T(8,128)(2,1)}), bf16[16,192,128]{2,1,0:T(8,128)(2,1)S(1)}, u32[]{:S(2)}, u32[]{:S(2)}) async-start(bf16[16,192,128]{2,1,0:T(8,128)(2,1)} %project.1), calls=%async_computation | async-start | bytes 1572864 | tf_op jit(solution)/shard_map/all_to_all | solution.py:397
  14.2 14.3 %collective-permute-start = (bf16[32,1024]{1,0:T(8,128)(2,1)S(1)}, bf16[32,1024]{1,0:T(8,128)(2,1)S(1)}, u32[]{:S(2)}, u32[]{:S(2)}) collective-permute-start(bf16[32,1024]{1,0:T(8,128)(2,1)S(1)} %slice_bitcast_fusion), channel_id=1, source_target_pairs={{0,16},{16,32},{32,48},{48,64},{64,80},{80,96},{96,112},{112,128},... | collective-permute-start | bytes 196616 | tf_op jit(solution)/shard_map/ppermute | solution.py:451
  19.3 9.2 %collective-permute-start.1 = (bf16[16,1024]{1,0:T(8,128)(2,1)S(1)}, bf16[16,1024]{1,0:T(8,128)(2,1)S(1)}, u32[]{:S(2)}, u32[]{:S(2)}) collective-permute-start(bf16[16,1024]{1,0:T(8,128)(2,1)S(1)} %slice_bitcast_fusion.1), channel_id=1, source_target_pairs={{16,0},{32,16},{48,32},{64,48},{80,64},{96,80},{112,96},{128,112},... | collective-permute-start | bytes 98312 | tf_op jit(solution)/shard_map/ppermute | solution.py:452
  38.5 16.8 %all-to-all-start.1 = ((bf16[16,160,128]{2,1,0:T(8,128)(2,1)}), bf16[16,160,128]{2,1,0:T(8,128)(2,1)S(1)}, u32[]{:S(2)}, u32[]{:S(2)}) async-start(bf16[16,160,128]{2,1,0:T(8,128)(2,1)} %attend.1), calls=%async_computation.1 | async-start | bytes 1310720 | tf_op jit(solution)/shard_map/all_to_all | solution.py:397

commit v6 on v4

--- a/solution.py
+++ b/solution.py
@@ -403,6 +403,13 @@
     return swap(jnp.broadcast_to(value[None], (size,) + value.shape), axis)
 
 
+def add_up(terms):
+    total = terms[0].astype(F32)
+    for index in range(1, terms.shape[0]):
+        total = total + terms[index].astype(F32)
+    return total
+
+
 def per_device(
     frames,
     lengths,
@@ -430,8 +437,8 @@
     gain = norm_two[None]
     ctx = swap(attend(lengths, stretch_sizes, look_ahead, packed, before, after), "seq")
     full, near, grad = finish(place, lengths, ctx, before, source, after, w_out, gain, taps)
-    piece = jnp.sum(swap(grad, "seq"), axis=0)
-    piece = jnp.sum(spread_out(piece, "dp"), axis=0)
+    piece = add_up(swap(grad, "seq")).astype(BF16)
+    piece = add_up(spread_out(piece, "dp"))
     grads = spread_out(piece, "seq")
     grads = grads.reshape(width // LANES, 32, LANES).transpose(1, 0, 2).reshape(32, width)
     return full[None], near[None], grads[:KERNEL]

time: 104 us -> 103 us (level)
  no operation moved by 1% of the time
where the time goes in v6:
time: 103 us
  blocking collectives  40.7 us (40%)
  Pallas kernels  21.1 us (20%)
  starting transfers between devices  19.9 us (19%)
  waiting for transfers between devices  17.7 us (17%)
  between operations  2.7 us (3%)
    all_to_all x3, blocking collectives, swap(): return lax.all_to_all(value, axis, 0, 0, tiled=True)  40.7 us
    all_to_all x2, starting transfers between devices, swap(): return lax.all_to_all(value, axis, 0, 0, tiled=True)  12.9 us
    all_to_all x2, waiting for transfers between devices, swap(): return lax.all_to_all(value, axis, 0, 0, tiled=True)  12.4 us
    pallas_call x1, Pallas kernels, attend(): pl.pallas_call(attend_kernel, in_specs=[SMEM_SPEC] * 3 + [VMEM_SPEC] + [p...  10.1 us
    pallas_call x1, Pallas kernels, finish(): pl.pallas_call(finish_kernel, in_specs=[SMEM_SPEC] * 2 + [VMEM_SPEC] * 7,...  6.04 us
    ppermute x1, waiting for transfers between devices, per_device(): after = lax.ppermute(source[:AFTER], 'seq', down)  5.37 us
    ppermute x1, starting transfers between devices, per_device(): before = lax.ppermute(source[rows - BEFORE:], 'seq', up)  5.04 us
    pallas_call x1, Pallas kernels, project(): pl.pallas_call(project_kernel, in_specs=[hbm, VMEM_SPEC, hbm, hbm, hbm],...  4.9 us
  transfers between devices with their start and end apart: 4, of which 2 were waited for; matrix products, arithmetic and copies ran while one was open for 0% of the time, Pallas kernels for 0%

profile of v6, /device:TPU:1, one launch (start us, length us, event | category | flops | bytes accessed | tf_op | source)
XLA Modules:
  0.0 103.0 jit_solution(13139957722304374536)
XLA Ops:
  0.6 0.0 copy-start.1
  0.6 4.9 %project.1 = bf16[16,192,128]{2,1,0:T(8,128)(2,1)} custom-call(bf16[128,1024]{1,0:T(8,128)(2,1)} %bitcast.21, f32[1,1024]{1,0:T(1,128)} %bitcast.27, bf16[1024,1024]{1,0:T(8,128)(2,1)} %wq_hbm.1, bf16[1024,1024]{1,0:T(8,128)(2,1)} %wk_hbm.1, bf16[1024,1024]{1,0:T(8,128)(2,1)} %wv_hbm.1), custom_call_target="tpu_custom_call" | custom-call | tf_op jit(solution)/shard_map/project/pallas_call | solution.py:93
  5.6 0.0 copy-start.3
  5.6 0.0 copy-start
  5.6 0.0 copy-start.2
  5.6 8.6 %all-to-all-start = ((bf16[16,192,128]{2,1,0:T(8,128)(2,1)}), bf16[16,192,128]{2,1,0:T(8,128)(2,1)S(1)}, u32[]{:S(2)}, u32[]{:S(2)}) async-start(bf16[16,192,128]{2,1,0:T(8,128)(2,1)} %project.1), calls=%async_computation | async-start | bytes 1572864 | tf_op jit(solution)/shard_map/all_to_all | solution.py:398
  14.2 0.0 copy-done.1
  14.2 5.0 %collective-permute-start = (bf16[32,1024]{1,0:T(8,128)(2,1)S(1)}, bf16[32,1024]{1,0:T(8,128)(2,1)S(1)}, u32[]{:S(2)}, u32[]{:S(2)}) collective-permute-start(bf16[32,1024]{1,0:T(8,128)(2,1)S(1)} %slice_bitcast_fusion), channel_id=1, source_target_pairs={{0,16},{16,32},{32,48},{48,64},{64,80},{80,96},{96,112},{112,128},... | collective-permute-start | bytes 196616 | tf_op jit(solution)/shard_map/ppermute | solution.py:432
  19.3 1.9 %collective-permute-start.1 = (bf16[16,1024]{1,0:T(8,128)(2,1)S(1)}, bf16[16,1024]{1,0:T(8,128)(2,1)S(1)}, u32[]{:S(2)}, u32[]{:S(2)}) collective-permute-start(bf16[16,1024]{1,0:T(8,128)(2,1)S(1)} %slice_bitcast_fusion.1), channel_id=1, source_target_pairs={{16,0},{32,16},{48,32},{64,48},{80,64},{96,80},{112,96},{128,112},... | collective-permute-start | bytes 98312 | tf_op jit(solution)/shard_map/ppermute | solution.py:433
  23.1 5.4 %collective-permute-done.1.after_ref = bf16[16,1024]{1,0:T(8,128)(2,1)S(1)} collective-permute-done((bf16[16,1024]{1,0:T(8,128)(2,1)S(1)}, bf16[16,1024]{1,0:T(8,128)(2,1)S(1)}, u32[]{:S(2)}, u32[]{:S(2)}) %collective-permute-start.1) | collective-permute-done | bytes 32800 | tf_op jit(solution)/shard_map/ppermute | solution.py:433
  28.5 0.0 collective-permute-done.before_ref
  28.5 0.0 all-to-all-done.packed_ref
  28.5 10.1 %attend.1 = bf16[16,160,128]{2,1,0:T(8,128)(2,1)} custom-call(s32[1]{0:T(128)S(6)} %copy.16.length_ref, s32[1]{0:T(128)S(6)} %copy.17.stretch_ref, s32[1]{0:T(128)S(6)} %copy.18.look_ref, bf16[16,192,128]{2,1,0:T(8,128)(2,1)S(1)} %all-to-all-done.packed_ref, bf16[32,1024]{1,0:T(8,128)(2,1)S(1)} %collective-permute-done.before_ref, ...), custom_call_target="tpu_custom_call" | custom-call | tf_op jit(solution)/shard_map/attend/pallas_call | solution.py:252
  38.6 4.3 %all-to-all-start.1 = ((bf16[16,160,128]{2,1,0:T(8,128)(2,1)}), bf16[16,160,128]{2,1,0:T(8,128)(2,1)S(1)}, u32[]{:S(2)}, u32[]{:S(2)}) async-start(bf16[16,160,128]{2,1,0:T(8,128)(2,1)} %attend.1), calls=%async_computation.1 | async-start | bytes 1310720 | tf_op jit(solution)/shard_map/all_to_all | solution.py:398
  42.9 0.0 copy-done.3
  42.9 0.1 reshape.26.taps_ref
  43.0 12.4 %all-to-all-done.1.ctx_ref = bf16[16,160,128]{2,1,0:T(8,128)(2,1)S(1)} async-done(((bf16[16,160,128]{2,1,0:T(8,128)(2,1)}), bf16[16,160,128]{2,1,0:T(8,128)(2,1)S(1)}, u32[]{:S(2)}, u32[]{:S(2)}) %all-to-all-start.1) | async-done | bytes 655392 | tf_op jit(solution)/shard_map/all_to_all | solution.py:398
  55.4 0.0 copy-done
  55.4 6.0 %finish.1 = (bf16[128,1024]{1,0:T(8,128)(2,1)}, bf16[128,1024]{1,0:T(8,128)(2,1)}, f32[16,16,128]{2,1,0:T(8,128)S(1)}) custom-call(s32[1]{0:T(128)} %bitcast.place_ref, s32[1]{0:T(128)S(6)} %copy.16.length_ref, bf16[16,160,128]{2,1,0:T(8,128)(2,1)S(1)} %all-to-all-done.1.ctx_ref, bf16[32,1024]{1,0:T(8,128)(2,1)S(1)} %collective-permute-done.before_ref, ...), custom_call_target="tpu_custom_call" | custom-call | tf_op jit(solution)/shard_map/finish/pallas_call | solution.py:373
  61.4 11.6 %all_to_all.25 = f32[16,16,128]{2,1,0:T(8,128)S(1)} all-to-all(f32[16,16,128]{2,1,0:T(8,128)S(1)} %get-tuple-element.8), channel_id=1, replica_groups=mesh['seq'=16,'dp'=16] {'seq'}, dimensions={0} | all-to-all | bytes 262144 | tf_op jit(solution)/shard_map/all_to_all | solution.py:398
  73.1 16.5 %all_to_all.26 = bf16[16,16,128]{2,1,0:T(8,128)(2,1)S(1)} all-to-all(bf16[16,16,128]{2,1,0:T(8,128)(2,1)S(1)} %broadcast_in_dim.33), channel_id=1, replica_groups=mesh['seq'=16,'dp'=16] {'dp'}, dimensions={0} | all-to-all | bytes 131072 | tf_op jit(solution)/shard_map/all_to_all | solution.py:398
  89.7 12.5 %all_to_all.27 = f32[16,16,128]{2,1,0:T(8,128)S(1)} all-to-all(f32[16,16,128]{2,1,0:T(8,128)S(1)} %broadcast_in_dim.35), channel_id=1, replica_groups=mesh['seq'=16,'dp'=16] {'seq'}, dimensions={0} | all-to-all | bytes 262144 | tf_op jit(solution)/shard_map/all_to_all | solution.py:398
  102.2 0.1 copy.14
  102.3 0.7 copy.15
  (8 shorter events, 0.1 us)
Async XLA Ops:
  0.6 13.6 %copy-start.1 = (bf16[1,128,1024]{2,1,0:T(8,128)(2,1)S(1)}, bf16[1,128,1024]{2,1,0:T(8,128)(2,1)}, u32[]{:S(2)}) copy-start(bf16[1,128,1024]{2,1,0:T(8,128)(2,1)} %param.11) | copy-start | bytes 786436
  5.6 37.4 %copy-start.3 = (bf16[31,1024]{1,0:T(8,128)(2,1)S(1)}, bf16[31,1024]{1,0:T(8,128)(2,1)}, u32[]{:S(2)}) copy-start(bf16[31,1024]{1,0:T(8,128)(2,1)} %param.21) | copy-start | bytes 190468
  5.6 49.8 %copy-start = (bf16[1024,1024]{1,0:T(8,128)(2,1)S(1)}, bf16[1024,1024]{1,0:T(8,128)(2,1)}, u32[]{:S(2)}) copy-start(bf16[1024,1024]{1,0:T(8,128)(2,1)} %wo_ref.1) | copy-start | bytes 6291460
  5.6 49.8 %copy-start.2 = (f32[1024]{0:T(1024)S(1)}, f32[1024]{0:T(1024)}, u32[]{:S(2)}) copy-start(f32[1024]{0:T(1024)} %param.16) | copy-start | bytes 12292
  5.6 22.9 %all-to-all-start = ((bf16[16,192,128]{2,1,0:T(8,128)(2,1)}), bf16[16,192,128]{2,1,0:T(8,128)(2,1)S(1)}, u32[]{:S(2)}, u32[]{:S(2)}) async-start(bf16[16,192,128]{2,1,0:T(8,128)(2,1)} %project.1), calls=%async_computation | async-start | bytes 1572864 | tf_op jit(solution)/shard_map/all_to_all | solution.py:398
  14.2 14.3 %collective-permute-start = (bf16[32,1024]{1,0:T(8,128)(2,1)S(1)}, bf16[32,1024]{1,0:T(8,128)(2,1)S(1)}, u32[]{:S(2)}, u32[]{:S(2)}) collective-permute-start(bf16[32,1024]{1,0:T(8,128)(2,1)S(1)} %slice_bitcast_fusion), channel_id=1, source_target_pairs={{0,16},{16,32},{32,48},{48,64},{64,80},{80,96},{96,112},{112,128},... | collective-permute-start | bytes 196616 | tf_op jit(solution)/shard_map/ppermute | solution.py:432
  19.3 9.2 %collective-permute-start.1 = (bf16[16,1024]{1,0:T(8,128)(2,1)S(1)}, bf16[16,1024]{1,0:T(8,128)(2,1)S(1)}, u32[]{:S(2)}, u32[]{:S(2)}) collective-permute-start(bf16[16,1024]{1,0:T(8,128)(2,1)S(1)} %slice_bitcast_fusion.1), channel_id=1, source_target_pairs={{16,0},{32,16},{48,32},{64,48},{80,64},{96,80},{112,96},{128,112},... | collective-permute-start | bytes 98312 | tf_op jit(solution)/shard_map/ppermute | solution.py:433
  38.6 16.8 %all-to-all-start.1 = ((bf16[16,160,128]{2,1,0:T(8,128)(2,1)}), bf16[16,160,128]{2,1,0:T(8,128)(2,1)S(1)}, u32[]{:S(2)}, u32[]{:S(2)}) async-start(bf16[16,160,128]{2,1,0:T(8,128)(2,1)} %attend.1), calls=%async_computation.1 | async-start | bytes 1310720 | tf_op jit(solution)/shard_map/all_to_all | solution.py:398

commit v7 on v6

--- a/solution.py
+++ b/solution.py
@@ -360,11 +360,9 @@
     sums = lax.fori_loop(0, rows // STRIDE, grad_rows, (zero,) * KERNEL)
     for k, value in enumerate(sums + (zero,)):
         sums_ref[k * TILE : (k + 1) * TILE] = value
-    for tile in range(width // LANES):
-        for group in range(4):
-            grad_ref[2 * tile + group // 2, group % 2 * TILE : group % 2 * TILE + TILE] = sums_ref[
-                cells(group * TILE, tile), :
-            ]
+    for group in range(32 // TILE):
+        for tile in range(width // LANES):
+            grad_ref[group * (width // LANES) + tile] = sums_ref[cells(group * TILE, tile), :]
 
 
 def finish(place, length, ctx, before, frames, after, wo, gain, taps):
@@ -377,7 +375,7 @@
         out_shape=[
             jax.ShapeDtypeStruct((rows, width), BF16),
             jax.ShapeDtypeStruct((rows, width), BF16),
-            jax.ShapeDtypeStruct((width // 64, 16, LANES), F32),
+            jax.ShapeDtypeStruct((32 // TILE * (width // LANES), TILE, LANES), F32),
         ],
         scratch_shapes=[
             pltpu.VMEM((2 * ext, width), BF16),
@@ -394,13 +392,12 @@
     )(place, length, ctx, before, frames, after, wo, gain, taps)
 
 
-def swap(value, axis):
-    return lax.all_to_all(value, axis, 0, 0, tiled=True)
-
-
-def spread_out(value, axis):
-    size = lax.axis_size(axis)
-    return swap(jnp.broadcast_to(value[None], (size,) + value.shape), axis)
+def swap(value, axis, groups=None):
+    return lax.all_to_all(value, axis, 0, 0, tiled=True, axis_index_groups=groups)
+
+
+def spread_out(value, axis, groups):
+    return swap(jnp.broadcast_to(value[None], (len(groups[0]),) + value.shape), axis, groups)
 
 
 def add_up(terms):
@@ -437,10 +434,15 @@
     gain = norm_two[None]
     ctx = swap(attend(lengths, stretch_sizes, look_ahead, packed, before, after), "seq")
     full, near, grad = finish(place, lengths, ctx, before, source, after, w_out, gain, taps)
-    piece = add_up(swap(grad, "seq")).astype(BF16)
-    piece = add_up(spread_out(piece, "dp"))
-    grads = spread_out(piece, "seq")
-    grads = grads.reshape(width // LANES, 32, LANES).transpose(1, 0, 2).reshape(32, width)
+    pairs = lax.axis_size("dp") // 2
+    both = ("seq", "dp")
+    plane = [[s * 2 * pairs + 2 * z + y for s in range(size) for y in range(2)] for z in range(pairs)]
+    column = [[2 * z + y for z in range(pairs)] for y in range(2)]
+    piece = add_up(swap(grad, both, plane))
+    piece = add_up(spread_out(piece, "dp", column))
+    grads = spread_out(piece, both, plane)
+    grads = grads.reshape(32 // TILE, width // LANES, TILE, LANES).transpose(0, 2, 1, 3)
+    grads = grads.reshape(32, width)
     return full[None], near[None], grads[:KERNEL]
 
 

time: 103 us -> 102 us (level)
  no operation moved by 1% of the time
where the time goes in v7:
time: 102 us
  blocking collectives  39.9 us (39%)
  Pallas kernels  20.9 us (20%)
  starting transfers between devices  19.9 us (20%)
  waiting for transfers between devices  17.7 us (17%)
  between operations  2.67 us (3%)
    all_to_all x3, blocking collectives, swap(): lax.all_to_all(value, axis, 0, 0, tiled=True, axis_index_groups=groups)  39.9 us
    all_to_all x2, starting transfers between devices, swap(): lax.all_to_all(value, axis, 0, 0, tiled=True, axis_index_groups=groups)  12.9 us
    all_to_all x2, waiting for transfers between devices, swap(): lax.all_to_all(value, axis, 0, 0, tiled=True, axis_index_groups=groups)  12.4 us
    pallas_call x1, Pallas kernels, attend(): pl.pallas_call(attend_kernel, in_specs=[SMEM_SPEC] * 3 + [VMEM_SPEC] + [p...  10 us
    pallas_call x1, Pallas kernels, finish(): pl.pallas_call(finish_kernel, in_specs=[SMEM_SPEC] * 2 + [VMEM_SPEC] * 7,...  6 us
    ppermute x1, waiting for transfers between devices, per_device(): after = lax.ppermute(source[:AFTER], 'seq', down)  5.37 us
    ppermute x1, starting transfers between devices, per_device(): before = lax.ppermute(source[rows - BEFORE:], 'seq', up)  5.04 us
    pallas_call x1, Pallas kernels, project(): pl.pallas_call(project_kernel, in_specs=[hbm, VMEM_SPEC, hbm, hbm, hbm],...  4.9 us
  transfers between devices with their start and end apart: 4, of which 2 were waited for; matrix products, arithmetic and copies ran while one was open for 0% of the time, Pallas kernels for 0%

profile of v7, /device:TPU:1, one launch (start us, length us, event | category | flops | bytes accessed | tf_op | source)
XLA Modules:
  0.0 101.9 jit_solution(6388459152428927275)
XLA Ops:
  0.6 0.0 copy-start.1
  0.6 4.9 %project.1 = bf16[16,192,128]{2,1,0:T(8,128)(2,1)} custom-call(bf16[128,1024]{1,0:T(8,128)(2,1)} %bitcast.20, f32[1,1024]{1,0:T(1,128)} %bitcast.24, bf16[1024,1024]{1,0:T(8,128)(2,1)} %wq_hbm.1, bf16[1024,1024]{1,0:T(8,128)(2,1)} %wk_hbm.1, bf16[1024,1024]{1,0:T(8,128)(2,1)} %wv_hbm.1), custom_call_target="tpu_custom_call" | custom-call | tf_op jit(solution)/shard_map/project/pallas_call | solution.py:93
  5.6 0.0 copy-start.3
  5.6 0.0 copy-start
  5.6 0.0 copy-start.2
  5.6 8.6 %all-to-all-start = ((bf16[16,192,128]{2,1,0:T(8,128)(2,1)}), bf16[16,192,128]{2,1,0:T(8,128)(2,1)S(1)}, u32[]{:S(2)}, u32[]{:S(2)}) async-start(bf16[16,192,128]{2,1,0:T(8,128)(2,1)} %project.1), calls=%async_computation | async-start | bytes 1572864 | tf_op jit(solution)/shard_map/all_to_all | solution.py:396
  14.2 0.0 copy-done.1
  14.2 5.0 %collective-permute-start = (bf16[32,1024]{1,0:T(8,128)(2,1)S(1)}, bf16[32,1024]{1,0:T(8,128)(2,1)S(1)}, u32[]{:S(2)}, u32[]{:S(2)}) collective-permute-start(bf16[32,1024]{1,0:T(8,128)(2,1)S(1)} %slice_bitcast_fusion), channel_id=1, source_target_pairs={{0,16},{16,32},{32,48},{48,64},{64,80},{80,96},{96,112},{112,128},... | collective-permute-start | bytes 196616 | tf_op jit(solution)/shard_map/ppermute | solution.py:429
  19.3 1.9 %collective-permute-start.1 = (bf16[16,1024]{1,0:T(8,128)(2,1)S(1)}, bf16[16,1024]{1,0:T(8,128)(2,1)S(1)}, u32[]{:S(2)}, u32[]{:S(2)}) collective-permute-start(bf16[16,1024]{1,0:T(8,128)(2,1)S(1)} %slice_bitcast_fusion.1), channel_id=1, source_target_pairs={{16,0},{32,16},{48,32},{64,48},{80,64},{96,80},{112,96},{128,112},... | collective-permute-start | bytes 98312 | tf_op jit(solution)/shard_map/ppermute | solution.py:430
  23.1 5.4 %collective-permute-done.1.after_ref = bf16[16,1024]{1,0:T(8,128)(2,1)S(1)} collective-permute-done((bf16[16,1024]{1,0:T(8,128)(2,1)S(1)}, bf16[16,1024]{1,0:T(8,128)(2,1)S(1)}, u32[]{:S(2)}, u32[]{:S(2)}) %collective-permute-start.1) | collective-permute-done | bytes 32800 | tf_op jit(solution)/shard_map/ppermute | solution.py:430
  28.5 0.0 collective-permute-done.before_ref
  28.5 0.0 all-to-all-done.packed_ref
  28.5 10.0 %attend.1 = bf16[16,160,128]{2,1,0:T(8,128)(2,1)} custom-call(s32[1]{0:T(128)S(6)} %copy.15.length_ref, s32[1]{0:T(128)S(6)} %copy.16.stretch_ref, s32[1]{0:T(128)S(6)} %copy.17.look_ref, bf16[16,192,128]{2,1,0:T(8,128)(2,1)S(1)} %all-to-all-done.packed_ref, bf16[32,1024]{1,0:T(8,128)(2,1)S(1)} %collective-permute-done.before_ref, ...), custom_call_target="tpu_custom_call" | custom-call | tf_op jit(solution)/shard_map/attend/pallas_call | solution.py:252
  38.5 4.3 %all-to-all-start.1 = ((bf16[16,160,128]{2,1,0:T(8,128)(2,1)}), bf16[16,160,128]{2,1,0:T(8,128)(2,1)S(1)}, u32[]{:S(2)}, u32[]{:S(2)}) async-start(bf16[16,160,128]{2,1,0:T(8,128)(2,1)} %attend.1), calls=%async_computation.1 | async-start | bytes 1310720 | tf_op jit(solution)/shard_map/all_to_all | solution.py:396
  42.9 0.0 copy-done.3
  42.9 0.1 reshape.28.taps_ref
  42.9 12.4 %all-to-all-done.1.ctx_ref = bf16[16,160,128]{2,1,0:T(8,128)(2,1)S(1)} async-done(((bf16[16,160,128]{2,1,0:T(8,128)(2,1)}), bf16[16,160,128]{2,1,0:T(8,128)(2,1)S(1)}, u32[]{:S(2)}, u32[]{:S(2)}) %all-to-all-start.1) | async-done | bytes 655392 | tf_op jit(solution)/shard_map/all_to_all | solution.py:396
  55.3 0.0 copy-done
  55.3 0.0 copy-done.2
  55.3 6.0 %finish.1 = (bf16[128,1024]{1,0:T(8,128)(2,1)}, bf16[128,1024]{1,0:T(8,128)(2,1)}, f32[32,8,128]{2,1,0:T(8,128)S(1)}) custom-call(s32[1]{0:T(128)} %bitcast.place_ref, s32[1]{0:T(128)S(6)} %copy.15.length_ref, bf16[16,160,128]{2,1,0:T(8,128)(2,1)S(1)} %all-to-all-done.1.ctx_ref, bf16[32,1024]{1,0:T(8,128)(2,1)S(1)} %collective-permute-done.before_ref, ...), custom_call_target="tpu_custom_call" | custom-call | tf_op jit(solution)/shard_map/finish/pallas_call | solution.py:371
  61.3 11.9 %all_to_all.25 = f32[32,8,128]{2,1,0:T(8,128)S(1)} all-to-all(f32[32,8,128]{2,1,0:T(8,128)S(1)} %get-tuple-element.8), channel_id=1, replica_groups={{0,1,16,17,32,33,48,49,64,65,80,81,96,97,112,113,128,129,144,145,160,16..., dimensions={0} | all-to-all | bytes 262144 | tf_op jit(solution)/shard_map/all_to_all | solution.py:396
  73.2 15.3 %all_to_all.26 = f32[8,8,128]{2,1,0:T(8,128)S(1)} all-to-all(f32[8,8,128]{2,1,0:T(8,128)S(1)} %broadcast_in_dim.33), channel_id=1, replica_groups={{0,2,4,6,8,10,12,14},{1,3,5,7,9,11,13,15},{16,18,20,22,24,26,28,30},{17..., dimensions={0} | all-to-all | bytes 65536 | tf_op jit(solution)/shard_map/all_to_all | solution.py:396
  88.5 12.7 %all_to_all.27 = f32[32,8,128]{2,1,0:T(8,128)S(1)} all-to-all(f32[32,8,128]{2,1,0:T(8,128)S(1)} %broadcast_in_dim.35), channel_id=1, replica_groups={{0,1,16,17,32,33,48,49,64,65,80,81,96,97,112,113,128,129,144,145,160,16..., dimensions={0} | all-to-all | bytes 262144 | tf_op jit(solution)/shard_map/all_to_all | solution.py:396
  101.2 0.7 copy.18
  (6 shorter events, 0.1 us)
Async XLA Ops:
  0.6 13.6 %copy-start.1 = (bf16[1,128,1024]{2,1,0:T(8,128)(2,1)S(1)}, bf16[1,128,1024]{2,1,0:T(8,128)(2,1)}, u32[]{:S(2)}) copy-start(bf16[1,128,1024]{2,1,0:T(8,128)(2,1)} %param.11) | copy-start | bytes 786436
  5.6 37.3 %copy-start.3 = (bf16[31,1024]{1,0:T(8,128)(2,1)S(1)}, bf16[31,1024]{1,0:T(8,128)(2,1)}, u32[]{:S(2)}) copy-start(bf16[31,1024]{1,0:T(8,128)(2,1)} %param.21) | copy-start | bytes 190468
  5.6 49.7 %copy-start = (bf16[1024,1024]{1,0:T(8,128)(2,1)S(1)}, bf16[1024,1024]{1,0:T(8,128)(2,1)}, u32[]{:S(2)}) copy-start(bf16[1024,1024]{1,0:T(8,128)(2,1)} %wo_ref.1) | copy-start | bytes 6291460
  5.6 49.7 %copy-start.2 = (f32[1024]{0:T(1024)S(1)}, f32[1024]{0:T(1024)}, u32[]{:S(2)}) copy-start(f32[1024]{0:T(1024)} %param.16) | copy-start | bytes 12292
  5.6 22.9 %all-to-all-start = ((bf16[16,192,128]{2,1,0:T(8,128)(2,1)}), bf16[16,192,128]{2,1,0:T(8,128)(2,1)S(1)}, u32[]{:S(2)}, u32[]{:S(2)}) async-start(bf16[16,192,128]{2,1,0:T(8,128)(2,1)} %project.1), calls=%async_computation | async-start | bytes 1572864 | tf_op jit(solution)/shard_map/all_to_all | solution.py:396
  14.2 14.3 %collective-permute-start = (bf16[32,1024]{1,0:T(8,128)(2,1)S(1)}, bf16[32,1024]{1,0:T(8,128)(2,1)S(1)}, u32[]{:S(2)}, u32[]{:S(2)}) collective-permute-start(bf16[32,1024]{1,0:T(8,128)(2,1)S(1)} %slice_bitcast_fusion), channel_id=1, source_target_pairs={{0,16},{16,32},{32,48},{48,64},{64,80},{80,96},{96,112},{112,128},... | collective-permute-start | bytes 196616 | tf_op jit(solution)/shard_map/ppermute | solution.py:429
  19.3 9.2 %collective-permute-start.1 = (bf16[16,1024]{1,0:T(8,128)(2,1)S(1)}, bf16[16,1024]{1,0:T(8,128)(2,1)S(1)}, u32[]{:S(2)}, u32[]{:S(2)}) collective-permute-start(bf16[16,1024]{1,0:T(8,128)(2,1)S(1)} %slice_bitcast_fusion.1), channel_id=1, source_target_pairs={{16,0},{32,16},{48,32},{64,48},{80,64},{96,80},{112,96},{128,112},... | collective-permute-start | bytes 98312 | tf_op jit(solution)/shard_map/ppermute | solution.py:430
  38.5 16.8 %all-to-all-start.1 = ((bf16[16,160,128]{2,1,0:T(8,128)(2,1)}), bf16[16,160,128]{2,1,0:T(8,128)(2,1)S(1)}, u32[]{:S(2)}, u32[]{:S(2)}) async-start(bf16[16,160,128]{2,1,0:T(8,128)(2,1)} %attend.1), calls=%async_computation.1 | async-start | bytes 1310720 | tf_op jit(solution)/shard_map/all_to_all | solution.py:396

commit v8 on v7

--- a/solution.py
+++ b/solution.py
@@ -208,11 +208,16 @@
                 raw = s_ref[span, pl.ds(pl.multiple_of(other * rows, rows), rows)]
                 pieces.append(jnp.where(inside, raw, FLOOR_SCORE))
             weights, totals = row_softmax(jnp.concatenate(pieces, axis=1))
-            w_ref[span, part * rows : (part + 3) * rows] = weights
+            own_part = part % 2
+            w_ref[span, own_part * rows : (own_part + 3) * rows] = weights
             sums.append(totals)
-        others = [jnp.clip(index * share + b, 0, blocks - 1) for b in range(-1, share + 1)]
-        window = jnp.concatenate([packed_ref[b, :rows] for b in others], axis=0)
-        mixed = jnp.dot(w_ref[...], window, preferred_element_type=F32)
+        mixed = []
+        for pair in range(share // 2):
+            others = [jnp.clip(index * share + 2 * pair + b, 0, blocks - 1) for b in range(-1, 3)]
+            window = jnp.concatenate([packed_ref[b, :rows] for b in others], axis=0)
+            span = slice(2 * pair * rows, 2 * (pair + 1) * rows)
+            mixed.append(jnp.dot(w_ref[span], window, preferred_element_type=F32))
+        mixed = jnp.concatenate(mixed, axis=0)
         near_ref[pl.ds(pl.multiple_of(index * QUERIES + BEFORE, BEFORE), QUERIES)] = (
             mixed / jnp.concatenate(sums, axis=0)
         ).astype(BF16)
@@ -259,7 +264,7 @@
             pltpu.VMEM((8, total), F32),
             pltpu.VMEM((QUERIES, total + LANES), F32),
             pltpu.VMEM((QUERIES, total + LANES), F32),
-            pltpu.VMEM((QUERIES, QUERIES + 2 * rows), BF16),
+            pltpu.VMEM((QUERIES, 4 * rows), BF16),
             pltpu.VMEM((total + 2 * AFTER, LANES), BF16),
             pltpu.VMEM((BEFORE + total, LANES), BF16),
         ],

time: 102 us -> 102 us (level)
  no operation moved by 1% of the time
where the time goes in v8:
time: 102 us; the launch traced here: 101 us
  blocking collectives  39.9 us (39%)
  Pallas kernels  20.3 us (20%)
  starting transfers between devices  19.9 us (20%)
  waiting for transfers between devices  17.7 us (17%)
  between operations  2.67 us (3%)
    all_to_all x3, blocking collectives, swap(): lax.all_to_all(value, axis, 0, 0, tiled=True, axis_index_groups=groups)  39.9 us
    all_to_all x2, starting transfers between devices, swap(): lax.all_to_all(value, axis, 0, 0, tiled=True, axis_index_groups=groups)  12.9 us
    all_to_all x2, waiting for transfers between devices, swap(): lax.all_to_all(value, axis, 0, 0, tiled=True, axis_index_groups=groups)  12.4 us
    pallas_call x1, Pallas kernels, attend(): pl.pallas_call(attend_kernel, in_specs=[SMEM_SPEC] * 3 + [VMEM_SPEC] + [p...  9.44 us
    pallas_call x1, Pallas kernels, finish(): pl.pallas_call(finish_kernel, in_specs=[SMEM_SPEC] * 2 + [VMEM_SPEC] * 7,...  6 us
    ppermute x1, waiting for transfers between devices, per_device(): after = lax.ppermute(source[:AFTER], 'seq', down)  5.37 us
    ppermute x1, starting transfers between devices, per_device(): before = lax.ppermute(source[rows - BEFORE:], 'seq', up)  5.04 us
    pallas_call x1, Pallas kernels, project(): pl.pallas_call(project_kernel, in_specs=[hbm, VMEM_SPEC, hbm, hbm, hbm],...  4.9 us
  transfers between devices with their start and end apart: 4, of which 2 were waited for; matrix products, arithmetic and copies ran while one was open for 0% of the time, Pallas kernels for 0%

profile of v8, /device:TPU:1, one launch (start us, length us, event | category | flops | bytes accessed | tf_op | source)
XLA Modules:
  0.0 101.3 jit_solution(9915007797708723149)
XLA Ops:
  0.6 0.0 copy-start.1
  0.6 4.9 %project.1 = bf16[16,192,128]{2,1,0:T(8,128)(2,1)} custom-call(bf16[128,1024]{1,0:T(8,128)(2,1)} %bitcast.20, f32[1,1024]{1,0:T(1,128)} %bitcast.24, bf16[1024,1024]{1,0:T(8,128)(2,1)} %wq_hbm.1, bf16[1024,1024]{1,0:T(8,128)(2,1)} %wk_hbm.1, bf16[1024,1024]{1,0:T(8,128)(2,1)} %wv_hbm.1), custom_call_target="tpu_custom_call" | custom-call | tf_op jit(solution)/shard_map/project/pallas_call | solution.py:93
  5.6 0.0 copy-start.3
  5.6 0.0 copy-start
  5.6 0.0 copy-start.2
  5.6 8.6 %all-to-all-start = ((bf16[16,192,128]{2,1,0:T(8,128)(2,1)}), bf16[16,192,128]{2,1,0:T(8,128)(2,1)S(1)}, u32[]{:S(2)}, u32[]{:S(2)}) async-start(bf16[16,192,128]{2,1,0:T(8,128)(2,1)} %project.1), calls=%async_computation | async-start | bytes 1572864 | tf_op jit(solution)/shard_map/all_to_all | solution.py:401
  14.2 0.0 copy-done.1
  14.2 5.0 %collective-permute-start = (bf16[32,1024]{1,0:T(8,128)(2,1)S(1)}, bf16[32,1024]{1,0:T(8,128)(2,1)S(1)}, u32[]{:S(2)}, u32[]{:S(2)}) collective-permute-start(bf16[32,1024]{1,0:T(8,128)(2,1)S(1)} %slice_bitcast_fusion), channel_id=1, source_target_pairs={{0,16},{16,32},{32,48},{48,64},{64,80},{80,96},{96,112},{112,128},... | collective-permute-start | bytes 196616 | tf_op jit(solution)/shard_map/ppermute | solution.py:434
  19.3 1.9 %collective-permute-start.1 = (bf16[16,1024]{1,0:T(8,128)(2,1)S(1)}, bf16[16,1024]{1,0:T(8,128)(2,1)S(1)}, u32[]{:S(2)}, u32[]{:S(2)}) collective-permute-start(bf16[16,1024]{1,0:T(8,128)(2,1)S(1)} %slice_bitcast_fusion.1), channel_id=1, source_target_pairs={{16,0},{32,16},{48,32},{64,48},{80,64},{96,80},{112,96},{128,112},... | collective-permute-start | bytes 98312 | tf_op jit(solution)/shard_map/ppermute | solution.py:435
  23.1 5.4 %collective-permute-done.1.after_ref = bf16[16,1024]{1,0:T(8,128)(2,1)S(1)} collective-permute-done((bf16[16,1024]{1,0:T(8,128)(2,1)S(1)}, bf16[16,1024]{1,0:T(8,128)(2,1)S(1)}, u32[]{:S(2)}, u32[]{:S(2)}) %collective-permute-start.1) | collective-permute-done | bytes 32800 | tf_op jit(solution)/shard_map/ppermute | solution.py:435
  28.5 0.0 collective-permute-done.before_ref
  28.5 0.0 all-to-all-done.packed_ref
  28.5 9.4 %attend.1 = bf16[16,160,128]{2,1,0:T(8,128)(2,1)} custom-call(s32[1]{0:T(128)S(6)} %copy.15.length_ref, s32[1]{0:T(128)S(6)} %copy.16.stretch_ref, s32[1]{0:T(128)S(6)} %copy.17.look_ref, bf16[16,192,128]{2,1,0:T(8,128)(2,1)S(1)} %all-to-all-done.packed_ref, bf16[32,1024]{1,0:T(8,128)(2,1)S(1)} %collective-permute-done.before_ref, ...), custom_call_target="tpu_custom_call" | custom-call | tf_op jit(solution)/shard_map/attend/pallas_call | solution.py:257
  38.0 4.3 %all-to-all-start.1 = ((bf16[16,160,128]{2,1,0:T(8,128)(2,1)}), bf16[16,160,128]{2,1,0:T(8,128)(2,1)S(1)}, u32[]{:S(2)}, u32[]{:S(2)}) async-start(bf16[16,160,128]{2,1,0:T(8,128)(2,1)} %attend.1), calls=%async_computation.1 | async-start | bytes 1310720 | tf_op jit(solution)/shard_map/all_to_all | solution.py:401
  42.3 0.0 copy-done.3
  42.3 0.1 reshape.28.taps_ref
  42.4 12.4 %all-to-all-done.1.ctx_ref = bf16[16,160,128]{2,1,0:T(8,128)(2,1)S(1)} async-done(((bf16[16,160,128]{2,1,0:T(8,128)(2,1)}), bf16[16,160,128]{2,1,0:T(8,128)(2,1)S(1)}, u32[]{:S(2)}, u32[]{:S(2)}) %all-to-all-start.1) | async-done | bytes 655392 | tf_op jit(solution)/shard_map/all_to_all | solution.py:401
  54.7 0.0 copy-done
  54.7 0.0 copy-done.2
  54.7 6.0 %finish.1 = (bf16[128,1024]{1,0:T(8,128)(2,1)}, bf16[128,1024]{1,0:T(8,128)(2,1)}, f32[32,8,128]{2,1,0:T(8,128)S(1)}) custom-call(s32[1]{0:T(128)} %bitcast.place_ref, s32[1]{0:T(128)S(6)} %copy.15.length_ref, bf16[16,160,128]{2,1,0:T(8,128)(2,1)S(1)} %all-to-all-done.1.ctx_ref, bf16[32,1024]{1,0:T(8,128)(2,1)S(1)} %collective-permute-done.before_ref, ...), custom_call_target="tpu_custom_call" | custom-call | tf_op jit(solution)/shard_map/finish/pallas_call | solution.py:376
  60.7 11.9 %all_to_all.25 = f32[32,8,128]{2,1,0:T(8,128)S(1)} all-to-all(f32[32,8,128]{2,1,0:T(8,128)S(1)} %get-tuple-element.8), channel_id=1, replica_groups={{0,1,16,17,32,33,48,49,64,65,80,81,96,97,112,113,128,129,144,145,160,16..., dimensions={0} | all-to-all | bytes 262144 | tf_op jit(solution)/shard_map/all_to_all | solution.py:401
  72.7 15.2 %all_to_all.26 = f32[8,8,128]{2,1,0:T(8,128)S(1)} all-to-all(f32[8,8,128]{2,1,0:T(8,128)S(1)} %broadcast_in_dim.33), channel_id=1, replica_groups={{0,2,4,6,8,10,12,14},{1,3,5,7,9,11,13,15},{16,18,20,22,24,26,28,30},{17..., dimensions={0} | all-to-all | bytes 65536 | tf_op jit(solution)/shard_map/all_to_all | solution.py:401
  87.9 12.7 %all_to_all.27 = f32[32,8,128]{2,1,0:T(8,128)S(1)} all-to-all(f32[32,8,128]{2,1,0:T(8,128)S(1)} %broadcast_in_dim.35), channel_id=1, replica_groups={{0,1,16,17,32,33,48,49,64,65,80,81,96,97,112,113,128,129,144,145,160,16..., dimensions={0} | all-to-all | bytes 262144 | tf_op jit(solution)/shard_map/all_to_all | solution.py:401
  100.7 0.7 copy.18
  (6 shorter events, 0.1 us)
Async XLA Ops:
  0.6 13.6 %copy-start.1 = (bf16[1,128,1024]{2,1,0:T(8,128)(2,1)S(1)}, bf16[1,128,1024]{2,1,0:T(8,128)(2,1)}, u32[]{:S(2)}) copy-start(bf16[1,128,1024]{2,1,0:T(8,128)(2,1)} %param.11) | copy-start | bytes 786436
  5.6 36.7 %copy-start.3 = (bf16[31,1024]{1,0:T(8,128)(2,1)S(1)}, bf16[31,1024]{1,0:T(8,128)(2,1)}, u32[]{:S(2)}) copy-start(bf16[31,1024]{1,0:T(8,128)(2,1)} %param.21) | copy-start | bytes 190468
  5.6 49.2 %copy-start = (bf16[1024,1024]{1,0:T(8,128)(2,1)S(1)}, bf16[1024,1024]{1,0:T(8,128)(2,1)}, u32[]{:S(2)}) copy-start(bf16[1024,1024]{1,0:T(8,128)(2,1)} %wo_ref.1) | copy-start | bytes 6291460
  5.6 49.1 %copy-start.2 = (f32[1024]{0:T(1024)S(1)}, f32[1024]{0:T(1024)}, u32[]{:S(2)}) copy-start(f32[1024]{0:T(1024)} %param.16) | copy-start | bytes 12292
  5.6 22.9 %all-to-all-start = ((bf16[16,192,128]{2,1,0:T(8,128)(2,1)}), bf16[16,192,128]{2,1,0:T(8,128)(2,1)S(1)}, u32[]{:S(2)}, u32[]{:S(2)}) async-start(bf16[16,192,128]{2,1,0:T(8,128)(2,1)} %project.1), calls=%async_computation | async-start | bytes 1572864 | tf_op jit(solution)/shard_map/all_to_all | solution.py:401
  14.2 14.3 %collective-permute-start = (bf16[32,1024]{1,0:T(8,128)(2,1)S(1)}, bf16[32,1024]{1,0:T(8,128)(2,1)S(1)}, u32[]{:S(2)}, u32[]{:S(2)}) collective-permute-start(bf16[32,1024]{1,0:T(8,128)(2,1)S(1)} %slice_bitcast_fusion), channel_id=1, source_target_pairs={{0,16},{16,32},{32,48},{48,64},{64,80},{80,96},{96,112},{112,128},... | collective-permute-start | bytes 196616 | tf_op jit(solution)/shard_map/ppermute | solution.py:434
  19.3 9.2 %collective-permute-start.1 = (bf16[16,1024]{1,0:T(8,128)(2,1)S(1)}, bf16[16,1024]{1,0:T(8,128)(2,1)S(1)}, u32[]{:S(2)}, u32[]{:S(2)}) collective-permute-start(bf16[16,1024]{1,0:T(8,128)(2,1)S(1)} %slice_bitcast_fusion.1), channel_id=1, source_target_pairs={{16,0},{32,16},{48,32},{64,48},{80,64},{96,80},{112,96},{128,112},... | collective-permute-start | bytes 98312 | tf_op jit(solution)/shard_map/ppermute | solution.py:435
  38.0 16.8 %all-to-all-start.1 = ((bf16[16,160,128]{2,1,0:T(8,128)(2,1)}), bf16[16,160,128]{2,1,0:T(8,128)(2,1)S(1)}, u32[]{:S(2)}, u32[]{:S(2)}) async-start(bf16[16,160,128]{2,1,0:T(8,128)(2,1)} %attend.1), calls=%async_computation.1 | async-start | bytes 1310720 | tf_op jit(solution)/shard_map/all_to_all | solution.py:401

commit v9 on v8

--- a/solution.py
+++ b/solution.py
@@ -112,7 +112,7 @@
 
 
 def attend_kernel(
-    length_ref, stretch_ref, look_ref, packed_ref, before_ref, after_ref, out_ref,
+    length_ref, stretch_ref, look_ref, packed_ref, before_ref, out_ref,
     q_ref, bias_ref, s0_ref, s1_ref, w_ref, full_ref, near_ref,
 ):
     blocks, packed_rows, _ = packed_ref.shape
@@ -250,13 +250,13 @@
         out_ref[block] = jnp.where(low, full_ref[span], near_ref[span])
 
 
-def attend(length, stretch, look, packed, before, after):
+def attend(length, stretch, look, packed, before):
     blocks, packed_rows, _ = packed.shape
     rows = packed_rows * 2 // 3
     total = blocks * rows
     return pl.pallas_call(
         attend_kernel,
-        in_specs=[SMEM_SPEC] * 3 + [VMEM_SPEC] + [pl.BlockSpec(memory_space=pl.ANY)] * 2,
+        in_specs=[SMEM_SPEC] * 3 + [VMEM_SPEC] + [pl.BlockSpec(memory_space=pl.ANY)],
         out_specs=VMEM_SPEC,
         out_shape=jax.ShapeDtypeStruct((blocks, BEFORE + rows, LANES), BF16),
         scratch_shapes=[
@@ -270,7 +270,7 @@
         ],
         compiler_params=pltpu.CompilerParams(vmem_limit_bytes=32 << 20),
         name="attend",
-    )(length, stretch, look, packed, before, after)
+    )(length, stretch, look, packed, before)
 
 
 def frame_tile(ref, index):
@@ -437,7 +437,7 @@
     packed = project(source, norm_one[None], w_query, w_key, w_value)
     packed = swap(packed, "seq")
     gain = norm_two[None]
-    ctx = swap(attend(lengths, stretch_sizes, look_ahead, packed, before, after), "seq")
+    ctx = swap(attend(lengths, stretch_sizes, look_ahead, packed, before), "seq")
     full, near, grad = finish(place, lengths, ctx, before, source, after, w_out, gain, taps)
     pairs = lax.axis_size("dp") // 2
     both = ("seq", "dp")

time: 102 us -> 102 us (level)
    all_to_all x2, waiting for transfers between devices: 12.4 us -> 9.56 us  [swap(): lax.all_to_all(value, axis, 0, 0, tiled=True, axis_index_groups=groups)]
    ppermute x1, waiting for transfers between devices: 5.37 us -> 6.75 us  [per_device(): after = lax.ppermute(source[:AFTER], 'seq', down)]
  transfers between devices with their start and end apart: 4 -> 4, of which waited for: 2 -> 4; matrix products, arithmetic and copies ran while one was open for 0% -> 0% of each run, Pallas kernels for 0% -> 0%
where the time goes in v9:
time: 102 us; the launch traced here: 101 us
  blocking collectives  39.9 us (39%)
  starting transfers between devices  20.4 us (20%)
  Pallas kernels  20.3 us (20%)
  waiting for transfers between devices  17.2 us (17%)
  between operations  2.68 us (3%)
    all_to_all x3, blocking collectives, swap(): lax.all_to_all(value, axis, 0, 0, tiled=True, axis_index_groups=groups)  39.9 us
    all_to_all x2, starting transfers between devices, swap(): lax.all_to_all(value, axis, 0, 0, tiled=True, axis_index_groups=groups)  13.1 us
    all_to_all x2, waiting for transfers between devices, swap(): lax.all_to_all(value, axis, 0, 0, tiled=True, axis_index_groups=groups)  9.56 us
    pallas_call x1, Pallas kernels, attend(): pl.pallas_call(attend_kernel, in_specs=[SMEM_SPEC] * 3 + [VMEM_SPEC] + [p...  9.44 us
    ppermute x1, waiting for transfers between devices, per_device(): after = lax.ppermute(source[:AFTER], 'seq', down)  6.75 us
    pallas_call x1, Pallas kernels, finish(): pl.pallas_call(finish_kernel, in_specs=[SMEM_SPEC] * 2 + [VMEM_SPEC] * 7,...  6 us
    ppermute x1, starting transfers between devices, per_device(): before = lax.ppermute(source[rows - BEFORE:], 'seq', up)  5.04 us
    pallas_call x1, Pallas kernels, project(): pl.pallas_call(project_kernel, in_specs=[hbm, VMEM_SPEC, hbm, hbm, hbm],...  4.9 us
  transfers between devices with their start and end apart: 4, of which 4 were waited for; matrix products, arithmetic and copies ran while one was open for 0% of the time, Pallas kernels for 0%

profile of v9, /device:TPU:1, one launch (start us, length us, event | category | flops | bytes accessed | tf_op | source)
XLA Modules:
  0.0 101.3 jit_solution(3466827293092770339)
XLA Ops:
  0.6 0.0 copy-start.1
  0.6 4.9 %project.1 = bf16[16,192,128]{2,1,0:T(8,128)(2,1)} custom-call(bf16[128,1024]{1,0:T(8,128)(2,1)} %bitcast.20, f32[1,1024]{1,0:T(1,128)} %bitcast.24, bf16[1024,1024]{1,0:T(8,128)(2,1)} %wq_hbm.1, bf16[1024,1024]{1,0:T(8,128)(2,1)} %wk_hbm.1, bf16[1024,1024]{1,0:T(8,128)(2,1)} %wv_hbm.1), custom_call_target="tpu_custom_call" | custom-call | tf_op jit(solution)/shard_map/project/pallas_call | solution.py:93
  5.6 0.0 copy-start.3
  5.6 0.0 copy-start
  5.6 0.0 copy-start.2
  5.6 8.6 %all-to-all-start = ((bf16[16,192,128]{2,1,0:T(8,128)(2,1)}), bf16[16,192,128]{2,1,0:T(8,128)(2,1)S(1)}, u32[]{:S(2)}, u32[]{:S(2)}) async-start(bf16[16,192,128]{2,1,0:T(8,128)(2,1)} %project.1), calls=%async_computation | async-start | bytes 1572864 | tf_op jit(solution)/shard_map/all_to_all | solution.py:401
  14.2 0.0 copy-done.1
  14.2 5.0 %collective-permute-start = (bf16[32,1024]{1,0:T(8,128)(2,1)S(1)}, bf16[32,1024]{1,0:T(8,128)(2,1)S(1)}, u32[]{:S(2)}, u32[]{:S(2)}) collective-permute-start(bf16[32,1024]{1,0:T(8,128)(2,1)S(1)} %slice_bitcast_fusion), channel_id=1, source_target_pairs={{0,16},{16,32},{32,48},{48,64},{64,80},{80,96},{96,112},{112,128},... | collective-permute-start | bytes 196616 | tf_op jit(solution)/shard_map/ppermute | solution.py:434
  21.2 0.9 collective-permute-done.before_ref
  22.0 6.3 %all-to-all-done.packed_ref = bf16[16,192,128]{2,1,0:T(8,128)(2,1)S(1)} async-done(((bf16[16,192,128]{2,1,0:T(8,128)(2,1)}), bf16[16,192,128]{2,1,0:T(8,128)(2,1)S(1)}, u32[]{:S(2)}, u32[]{:S(2)}) %all-to-all-start) | async-done | bytes 786464 | tf_op jit(solution)/shard_map/all_to_all | solution.py:401
  28.3 9.4 %attend.1 = bf16[16,160,128]{2,1,0:T(8,128)(2,1)} custom-call(s32[1]{0:T(128)S(6)} %copy.15.length_ref, s32[1]{0:T(128)S(6)} %copy.16.stretch_ref, s32[1]{0:T(128)S(6)} %copy.17.look_ref, bf16[16,192,128]{2,1,0:T(8,128)(2,1)S(1)} %all-to-all-done.packed_ref, bf16[32,1024]{1,0:T(8,128)(2,1)S(1)} %collective-permute-done.before_ref), custom_call_target="tpu_custom_call" | custom-call | tf_op jit(solution)/shard_map/attend/pallas_call | solution.py:257
  37.8 4.5 %all-to-all-start.1 = ((bf16[16,160,128]{2,1,0:T(8,128)(2,1)}), bf16[16,160,128]{2,1,0:T(8,128)(2,1)S(1)}, u32[]{:S(2)}, u32[]{:S(2)}) async-start(bf16[16,160,128]{2,1,0:T(8,128)(2,1)} %attend.1), calls=%async_computation.1 | async-start | bytes 1310720 | tf_op jit(solution)/shard_map/all_to_all | solution.py:401
  42.3 2.3 %collective-permute-start.1 = (bf16[16,1024]{1,0:T(8,128)(2,1)S(1)}, bf16[16,1024]{1,0:T(8,128)(2,1)S(1)}, u32[]{:S(2)}, u32[]{:S(2)}) collective-permute-start(bf16[16,1024]{1,0:T(8,128)(2,1)S(1)} %slice_bitcast_fusion.1), channel_id=1, source_target_pairs={{16,0},{32,16},{48,32},{64,48},{80,64},{96,80},{112,96},{128,112},... | collective-permute-start | bytes 98312 | tf_op jit(solution)/shard_map/ppermute | solution.py:435
  44.6 0.0 copy-done.3
  44.6 0.1 reshape.28.taps_ref
  44.7 6.8 %collective-permute-done.1.after_ref = bf16[16,1024]{1,0:T(8,128)(2,1)S(1)} collective-permute-done((bf16[16,1024]{1,0:T(8,128)(2,1)S(1)}, bf16[16,1024]{1,0:T(8,128)(2,1)S(1)}, u32[]{:S(2)}, u32[]{:S(2)}) %collective-permute-start.1) | collective-permute-done | bytes 32800 | tf_op jit(solution)/shard_map/ppermute | solution.py:435
  51.4 3.3 %all-to-all-done.1.ctx_ref = bf16[16,160,128]{2,1,0:T(8,128)(2,1)S(1)} async-done(((bf16[16,160,128]{2,1,0:T(8,128)(2,1)}), bf16[16,160,128]{2,1,0:T(8,128)(2,1)S(1)}, u32[]{:S(2)}, u32[]{:S(2)}) %all-to-all-start.1) | async-done | bytes 655392 | tf_op jit(solution)/shard_map/all_to_all | solution.py:401
  54.7 0.0 copy-done
  54.7 0.0 copy-done.2
  54.7 6.0 %finish.1 = (bf16[128,1024]{1,0:T(8,128)(2,1)}, bf16[128,1024]{1,0:T(8,128)(2,1)}, f32[32,8,128]{2,1,0:T(8,128)S(1)}) custom-call(s32[1]{0:T(128)} %bitcast.place_ref, s32[1]{0:T(128)S(6)} %copy.15.length_ref, bf16[16,160,128]{2,1,0:T(8,128)(2,1)S(1)} %all-to-all-done.1.ctx_ref, bf16[32,1024]{1,0:T(8,128)(2,1)S(1)} %collective-permute-done.before_ref, ...), custom_call_target="tpu_custom_call" | custom-call | tf_op jit(solution)/shard_map/finish/pallas_call | solution.py:376
  60.7 12.1 %all_to_all.25 = f32[32,8,128]{2,1,0:T(8,128)S(1)} all-to-all(f32[32,8,128]{2,1,0:T(8,128)S(1)} %get-tuple-element.8), channel_id=1, replica_groups={{0,1,16,17,32,33,48,49,64,65,80,81,96,97,112,113,128,129,144,145,160,16..., dimensions={0} | all-to-all | bytes 262144 | tf_op jit(solution)/shard_map/all_to_all | solution.py:401
  72.8 15.1 %all_to_all.26 = f32[8,8,128]{2,1,0:T(8,128)S(1)} all-to-all(f32[8,8,128]{2,1,0:T(8,128)S(1)} %broadcast_in_dim.33), channel_id=1, replica_groups={{0,2,4,6,8,10,12,14},{1,3,5,7,9,11,13,15},{16,18,20,22,24,26,28,30},{17..., dimensions={0} | all-to-all | bytes 65536 | tf_op jit(solution)/shard_map/all_to_all | solution.py:401
  87.9 12.7 %all_to_all.27 = f32[32,8,128]{2,1,0:T(8,128)S(1)} all-to-all(f32[32,8,128]{2,1,0:T(8,128)S(1)} %broadcast_in_dim.35), channel_id=1, replica_groups={{0,1,16,17,32,33,48,49,64,65,80,81,96,97,112,113,128,129,144,145,160,16..., dimensions={0} | all-to-all | bytes 262144 | tf_op jit(solution)/shard_map/all_to_all | solution.py:401
  100.7 0.7 copy.18
  (6 shorter events, 0.1 us)
Async XLA Ops:
  0.6 13.6 %copy-start.1 = (bf16[1,128,1024]{2,1,0:T(8,128)(2,1)S(1)}, bf16[1,128,1024]{2,1,0:T(8,128)(2,1)}, u32[]{:S(2)}) copy-start(bf16[1,128,1024]{2,1,0:T(8,128)(2,1)} %param.11) | copy-start | bytes 786436
  5.6 39.1 %copy-start.3 = (bf16[31,1024]{1,0:T(8,128)(2,1)S(1)}, bf16[31,1024]{1,0:T(8,128)(2,1)}, u32[]{:S(2)}) copy-start(bf16[31,1024]{1,0:T(8,128)(2,1)} %param.21) | copy-start | bytes 190468
  5.6 49.2 %copy-start = (bf16[1024,1024]{1,0:T(8,128)(2,1)S(1)}, bf16[1024,1024]{1,0:T(8,128)(2,1)}, u32[]{:S(2)}) copy-start(bf16[1024,1024]{1,0:T(8,128)(2,1)} %wo_ref.1) | copy-start | bytes 6291460
  5.6 49.1 %copy-start.2 = (f32[1024]{0:T(1024)S(1)}, f32[1024]{0:T(1024)}, u32[]{:S(2)}) copy-start(f32[1024]{0:T(1024)} %param.16) | copy-start | bytes 12292
  5.6 22.8 %all-to-all-start = ((bf16[16,192,128]{2,1,0:T(8,128)(2,1)}), bf16[16,192,128]{2,1,0:T(8,128)(2,1)S(1)}, u32[]{:S(2)}, u32[]{:S(2)}) async-start(bf16[16,192,128]{2,1,0:T(8,128)(2,1)} %project.1), calls=%async_computation | async-start | bytes 1572864 | tf_op jit(solution)/shard_map/all_to_all | solution.py:401
  14.2 7.8 %collective-permute-start = (bf16[32,1024]{1,0:T(8,128)(2,1)S(1)}, bf16[32,1024]{1,0:T(8,128)(2,1)S(1)}, u32[]{:S(2)}, u32[]{:S(2)}) collective-permute-start(bf16[32,1024]{1,0:T(8,128)(2,1)S(1)} %slice_bitcast_fusion), channel_id=1, source_target_pairs={{0,16},{16,32},{32,48},{48,64},{64,80},{80,96},{96,112},{112,128},... | collective-permute-start | bytes 196616 | tf_op jit(solution)/shard_map/ppermute | solution.py:434
  37.8 16.9 %all-to-all-start.1 = ((bf16[16,160,128]{2,1,0:T(8,128)(2,1)}), bf16[16,160,128]{2,1,0:T(8,128)(2,1)S(1)}, u32[]{:S(2)}, u32[]{:S(2)}) async-start(bf16[16,160,128]{2,1,0:T(8,128)(2,1)} %attend.1), calls=%async_computation.1 | async-start | bytes 1310720 | tf_op jit(solution)/shard_map/all_to_all | solution.py:401
  42.3 9.2 %collective-permute-start.1 = (bf16[16,1024]{1,0:T(8,128)(2,1)S(1)}, bf16[16,1024]{1,0:T(8,128)(2,1)S(1)}, u32[]{:S(2)}, u32[]{:S(2)}) collective-permute-start(bf16[16,1024]{1,0:T(8,128)(2,1)S(1)} %slice_bitcast_fusion.1), channel_id=1, source_target_pairs={{16,0},{32,16},{48,32},{64,48},{80,64},{96,80},{112,96},{128,112},... | collective-permute-start | bytes 98312 | tf_op jit(solution)/shard_map/ppermute | solution.py:435
